TPU v7x, 32 devices: a whole 2x2x4 slice. The times are simulated.
32 devices in a mesh: grp: 2 (over y), op: 4 (over z), sec: 2 (over x), sub: 2 (over core).
Axes of the slice: x: 2, y: 2, z: 4, core: 2. Of those that a mesh axis runs over, the one named last changes fastest.
Arguments:
- wavefunction: float32 [16, 256, 256], P(('grp', 'sec'), None, 'sub'), parts along dimension 0, may hold values from -100 to 100
- diagonal: float32 [16, 256, 256], P(('grp', 'sec'), None, 'sub'), parts along dimension 0, may hold values from 0.5 to 10
- left_env: bfloat16 [192, 8, 256, 256], P(('grp', 'op'), 'sec'), parts along dimension 0, may hold values from -1 to 2
- right_env: bfloat16 [192, 8, 256, 256], P(('grp', 'op'), 'sec', 'sub'), parts along dimension 0, may hold values from -1 to 1
- targets: int32 [192, 8], P(('grp', 'op'), 'sec'), parts along dimension 0, may hold values from -1 to 7, as said below
Outputs:
- refined: float32 [16, 256, 256], P(('grp', 'sec'), None, 'sub'), parts along dimension 0
- ritz_values: float32 [4], P('grp'), parts along dimension 0
There are 2 independent parts, one for each index of `grp`. A program takes and returns all parts, laid end to end along the dimension named above; each array names one. Nothing has to cross between parts.
Inputs may be any that keep to these rules, and one draw needn't show every extreme that they name: `targets`: -1 marks a term that does not act on the block; any other value is the block that receives its image.
All inputs are finite; a program needn't handle non-finite values.
Results may differ from a plain program's by a relative error of at most 0.0029.
Values sent between devices are 32-bit elements; how exact they have to be, the bound alone decides.
No kernel may reach another device: no remote copies, remote signals or barrier semaphores. Data moves between devices by JAX's collectives and lax.ppermute only.
A program may use at most 128 MiB of HBM per device.

v0:
```python
import jax
import jax.numpy as jnp
from jax import lax
from jax.sharding import PartitionSpec as P

ITERS = 2


def route_images(vector_bf, left_env, right_split, slots, total_blocks):
    terms_here, blocks_here, half_rows, sub_count, half = right_split.shape
    tile = left_env.shape[2]

    def accumulate(total, pieces):
        left_term, right_term, slot_row = pieces
        product = jnp.einsum(
            "bij,bjk->bik", left_term, vector_bf, preferred_element_type=jnp.float32
        ).astype(jnp.bfloat16)
        image = jnp.einsum(
            "bik,bkhc->bihc", product, right_term, preferred_element_type=jnp.float32
        )
        return (total.at[slot_row].add(image, mode="drop"), None)

    empty = jnp.zeros((total_blocks, tile, sub_count, half), jnp.float32)
    total, _ = lax.scan(accumulate, empty, (left_env, right_split, slots))
    return total


def per_device(wavefunction, diagonal, left_env, right_env, targets):
    sec_count = lax.axis_size("sec")
    sub_count = lax.axis_size("sub")
    blocks_here, tile, half = wavefunction.shape
    terms_here = left_env.shape[0]
    total_blocks = blocks_here * sec_count
    entries = total_blocks * tile * tile
    start = lax.psum(jnp.sum(wavefunction * wavefunction), ("sec", "sub"))
    vector = wavefunction / jnp.sqrt(start / entries)
    right_split = right_env.reshape(terms_here, blocks_here, half, sub_count, half)
    slots = jnp.where(targets < 0, total_blocks, targets)
    ritz_list = []
    for turn_index in range(ITERS):
        vector_bf = vector.astype(jnp.bfloat16)
        total = route_images(vector_bf, left_env, right_split, slots, total_blocks)
        parted = total.reshape(sec_count, blocks_here, tile, sub_count, half)
        partial_sum = parted.transpose(0, 3, 1, 2, 4).reshape(-1, tile, half)
        full_sum = lax.psum(partial_sum, ("op", "sec", "sub"))
        position = (lax.axis_index("sec") * sub_count + lax.axis_index("sub")) * blocks_here
        received = lax.dynamic_slice_in_dim(full_sum, position, blocks_here, 0)
        sigma = diagonal * vector + received
        theta = lax.psum(jnp.sum(vector * sigma), ("sec", "sub")) / entries
        correction = (sigma - theta * vector) / (1.0 + jnp.abs(diagonal - theta))
        along = lax.psum(jnp.sum(vector * correction), ("sec", "sub")) / entries
        updated = vector - (correction - along * vector)
        length_sq = lax.psum(jnp.sum(updated * updated), ("sec", "sub")) / entries
        vector = updated / jnp.sqrt(length_sq)
        ritz_list.append(theta)
    return (vector, jnp.stack(ritz_list))


def solution(mesh):
    placed = (
        P(("grp", "sec"), None, "sub"),
        P(("grp", "sec"), None, "sub"),
        P(("grp", "op"), "sec", None, None),
        P(("grp", "op"), "sec", "sub", None),
        P(("grp", "op"), "sec"),
    )
    return jax.shard_map(
        per_device,
        mesh=mesh,
        in_specs=placed,
        out_specs=(P(("grp", "sec"), None, "sub"), P("grp")),
        check_vma=False,
    )
```

profile of v0, /device:TPU:0, one launch (start us, length us, event | category | flops | bytes accessed | tf_op | source)
XLA Modules:
  0.0 431.6 jit_solution(13573034157138543646)
XLA Ops:
  7.2 1.8 multiply_reduce_fusion.6
  9.0 8.9 %psum.63 = f32[]{:T(128)} all-reduce(f32[]{:T(128)} %multiply_reduce_fusion.6), channel_id=1, replica_groups=mesh['grp'=2,'op'=4,'sec'=2,'sub'=2] {'sec','sub'}, use_global_device_ids=true, to_apply=%region_1.0 | all-reduce | flops 1 | bytes 8 | tf_op jit(solution)/shard_map/psum | solution.py:35
  19.7 8.6 %copy.20 = bf16[24,4,128,256]{2,3,1,0:T(8,128)(2,1)} copy(bf16[24,4,128,256]{3,2,1,0:T(8,128)(2,1)} %param.12) | data formatting | bytes 12582912 | tf_op args[3]
  28.4 8.7 %copy.22 = bf16[24,4,128,2,128]{4,2,3,1,0:T(8,128)(2,1)} copy(bf16[24,4,128,2,128]{2,4,3,1,0:T(8,128)(2,1)} %bitcast.81) | data formatting | bytes 12582912 | tf_op jit(solution)/shard_map/while | solution.py:24
  37.3 65.5 %while.20 = (s32[]{:T(128)}, f32[8,256,2,128]{3,1,2,0:T(8,128)S(1)}, s32[24,4]{1,0:T(8,128)S(1)}, bf16[24,4,256,256]{3,2,1,0:T(8,128)(2,1)}, bf16[4,256,128]{2,1...) while((s32[]{:T(128)}, f32[8,256,2,128]{3,1,2,0:T(8,128)S(1)}, s32[24,4]{1,0:T(8,128)S(1)}, ...), condition=%wide.region_4.5_spmd, body=%wide.region_2.4_spmd.sunk | while | flops 134610960 | bytes 5244033 | solution.py:24
  50.9 1.5 fusion.42
  59.1 1.5 fusion.42
  61.9 1.5 fusion.42
  67.3 1.5 fusion.42
  72.8 1.5 fusion.42
  75.6 1.5 fusion.42
  86.5 1.5 fusion.42
  102.8 1.5 copy.23
  104.5 98.2 %all-reduce.3.cloned.1.call-done = f32[16,256,128]{2,1,0:T(8,128)} async-done(((f32[16,256,128]{2,1,0:T(8,128)}), f32[16,256,128]{2,1,0:T(8,128)}) %all-reduce.3.cloned.1.call-update) | async-done | bytes 2097168 | tf_op jit(solution)/shard_map/psum | solution.py:45
  202.6 1.8 multiply_reduce_fusion.5
  204.4 6.3 %psum.65 = f32[]{:T(128)} all-reduce(f32[]{:T(128)} %multiply_reduce_fusion.5), channel_id=1, replica_groups=mesh['grp'=2,'op'=4,'sec'=2,'sub'=2] {'sec','sub'}, use_global_device_ids=true, to_apply=%region_7.8 | all-reduce | flops 1 | bytes 8 | tf_op jit(solution)/shard_map/psum | solution.py:49
  211.3 1.9 multiply_reduce_fusion.4
  213.2 7.1 %psum.66 = f32[]{:T(128)} all-reduce(f32[]{:T(128)} %multiply_reduce_fusion.4), channel_id=1, replica_groups=mesh['grp'=2,'op'=4,'sec'=2,'sub'=2] {'sec','sub'}, use_global_device_ids=true, to_apply=%region_9.10 | all-reduce | flops 1 | bytes 8 | tf_op jit(solution)/shard_map/psum | solution.py:51
  221.0 1.9 multiply_reduce_fusion.3
  222.9 6.6 %psum.67 = f32[]{:T(128)} all-reduce(f32[]{:T(128)} %multiply_reduce_fusion.3), channel_id=1, replica_groups=mesh['grp'=2,'op'=4,'sec'=2,'sub'=2] {'sec','sub'}, use_global_device_ids=true, to_apply=%region_11.12 | all-reduce | flops 1 | bytes 8 | tf_op jit(solution)/shard_map/psum | solution.py:53
  230.2 2.1 fusion.25
  232.5 65.5 %while.21 = (s32[]{:T(128)}, f32[8,256,2,128]{3,1,2,0:T(8,128)S(1)}, s32[24,4]{1,0:T(8,128)S(1)}, bf16[24,4,256,256]{3,2,1,0:T(8,128)(2,1)}, bf16[4,256,128]{2,1...) while((s32[]{:T(128)}, f32[8,256,2,128]{3,1,2,0:T(8,128)S(1)}, ...), condition=%wide.region_14.15_spmd, body=%wide.region_12.14_spmd.sunk | while | flops 134610960 | bytes 5244033 | solution.py:24
  237.9 1.5 fusion.47
  243.4 1.5 fusion.47
  265.2 1.5 fusion.47
  292.5 1.5 fusion.47
  299.4 97.1 %all-reduce.5.cloned.1.call-done = f32[16,256,128]{2,1,0:T(8,128)} async-done(((f32[16,256,128]{2,1,0:T(8,128)}), f32[16,256,128]{2,1,0:T(8,128)}) %all-reduce.5.cloned.1.call-update) | async-done | bytes 2097168 | tf_op jit(solution)/shard_map/psum | solution.py:45
  396.6 1.9 multiply_reduce_fusion.2
  398.5 6.3 %psum.69 = f32[]{:T(128)} all-reduce(f32[]{:T(128)} %multiply_reduce_fusion.2), channel_id=1, replica_groups=mesh['grp'=2,'op'=4,'sec'=2,'sub'=2] {'sec','sub'}, use_global_device_ids=true, to_apply=%region_17.18 | all-reduce | flops 1 | bytes 8 | tf_op jit(solution)/shard_map/psum | solution.py:49
  405.4 1.8 multiply_reduce_fusion.1
  407.2 7.1 %psum.70 = f32[]{:T(128)} all-reduce(f32[]{:T(128)} %multiply_reduce_fusion.1), channel_id=1, replica_groups=mesh['grp'=2,'op'=4,'sec'=2,'sub'=2] {'sec','sub'}, use_global_device_ids=true, to_apply=%region_19.20 | all-reduce | flops 1 | bytes 8 | tf_op jit(solution)/shard_map/psum | solution.py:51
  415.9 6.6 %psum.71 = f32[]{:T(128)} all-reduce(f32[]{:T(128)} %multiply_reduce_fusion), channel_id=1, replica_groups=mesh['grp'=2,'op'=4,'sec'=2,'sub'=2] {'sec','sub'}, use_global_device_ids=true, to_apply=%region_21.22 | all-reduce | flops 1 | bytes 8 | tf_op jit(solution)/shard_map/psum | solution.py:53
  (158 shorter events, 118.2 us)
Async XLA Ops:
  7.2 195.5 %all-reduce.3.cloned.1.call-start = ((), (), s32[]{:S(2)}) async-start(), calls=%async_computation | async-start | bytes 4194304 | tf_op jit(solution)/shard_map/psum | solution.py:45
  28.4 8.7 %copy-start.5 = (s32[24,4]{0,1:T(4,128)S(1)}, s32[24,4]{0,1:T(4,128)}, u32[]{:S(2)}) copy-start(s32[24,4]{0,1:T(4,128)} %param.13) | copy-start | bytes 1156
  104.4 98.2 %copy-start = (f32[4,256,128]{2,1,0:T(8,128)S(1)}, f32[4,256,128]{2,1,0:T(8,128)}, u32[]{:S(2)}) copy-start(f32[4,256,128]{2,1,0:T(8,128)} %param.10) | copy-start | bytes 1572868
  104.4 98.2 %copy-start.2 = (f32[4,256,128]{2,1,0:T(8,128)S(1)}, f32[4,256,128]{2,1,0:T(8,128)}, u32[]{:S(2)}) copy-start(f32[4,256,128]{2,1,0:T(8,128)} %param.9) | copy-start | bytes 1572868
  104.4 292.1 %all-reduce.5.cloned.1.call-start = ((), (), s32[]{:S(2)}) async-start(), calls=%async_computation.1 | async-start | bytes 4194304 | tf_op jit(solution)/shard_map/psum | solution.py:45
  299.4 97.1 %copy-start.1 = (f32[4,256,128]{2,1,0:T(8,128)S(1)}, f32[4,256,128]{2,1,0:T(8,128)}, u32[]{:S(2)}) copy-start(f32[4,256,128]{2,1,0:T(8,128)} %param.10) | copy-start | bytes 1572868
  299.4 97.1 %copy-start.3 = (f32[4,256,128]{2,1,0:T(8,128)S(1)}, f32[4,256,128]{2,1,0:T(8,128)}, u32[]{:S(2)}) copy-start(f32[4,256,128]{2,1,0:T(8,128)} %get-tuple-element.117) | copy-start | bytes 1572868
  396.5 18.5 %copy-start.4 = (f32[16,256,128]{2,1,0:T(8,128)S(1)}, f32[16,256,128]{2,1,0:T(8,128)}, u32[]{:S(2)}) copy-start(f32[16,256,128]{2,1,0:T(8,128)} %all-reduce.5.cloned.1.call-done) | copy-start | bytes 6291460
Sparse Core Ops, SparseCore 0:
  104.5 98.0 all-reduce.2
  299.6 96.9 all-reduce.4
where the time goes:
time: 434 us; the launch traced here: 432 us
  waiting for transfers between devices  195 us (45%)
  matrix products  73.4 us (17%)
  other arithmetic  72.8 us (17%)
  blocking collectives  48.9 us (11%)
  local copies, waits for them, and re-layouts  20.8 us (5%)
  between operations  18.8 us (4%)
    psum x2, waiting for transfers between devices, per_device(): full_sum = lax.psum(partial_sum, ('op', 'sec', 'sub'))  195 us
    dot_general x48, matrix products, accumulate(): jnp.einsum('bik,bkhc->bihc', product, right_term, preferred_element_type=...  73.4 us
    scatter-add x48, other arithmetic, accumulate(): return (total.at[slot_row].add(image, mode='drop'), None)  55.4 us
    psum x2, blocking collectives, per_device(): along = lax.psum(jnp.sum(vector * correction), ('sec', 'sub')) / entries  14.2 us
    psum x2, blocking collectives, per_device(): length_sq = lax.psum(jnp.sum(updated * updated), ('sec', 'sub')) / entries  13.2 us
    psum x2, blocking collectives, per_device(): theta = lax.psum(jnp.sum(vector * sigma), ('sec', 'sub')) / entries  12.5 us
    psum x1, blocking collectives, per_device(): start = lax.psum(jnp.sum(wavefunction * wavefunction), ('sec', 'sub'))  8.94 us
    while x2, local copies, waits for them, and re-layouts, route_images(): total, _ = lax.scan(accumulate, empty, (left_env, right_split, slots))  8.77 us
  transfers between devices with their start and end apart: 2, of which 2 were waited for; matrix products, arithmetic and copies ran while one was open for 0% of the time, Pallas kernels for 0%

commit v1 on v0

v1 whole, which is shorter than its diff:
```python
import functools

import jax
import jax.numpy as jnp
from jax import lax
from jax.experimental import pallas as pl
from jax.experimental.pallas import tpu as pltpu
from jax.sharding import PartitionSpec as P

ITERS = 2
GROUP = 2
SLOTS = 10
REMOTE, OWN = 0, 1
VMEM = pl.BlockSpec(memory_space=pltpu.VMEM)
SMEM = pl.BlockSpec(memory_space=pltpu.SMEM)
ANY = pl.BlockSpec(memory_space=pl.ANY)


def f32(*shape):
    return jax.ShapeDtypeStruct(shape, jnp.float32)


def i32(*shape):
    return jax.ShapeDtypeStruct(shape, jnp.int32)


def step_cap(pairs, slots):
    steps = (pairs + slots) // 2 + GROUP
    return -(-steps // GROUP) * GROUP


def plan_kernel(secs, cap, targets, wave, tile, block, slot, groups, square, fill):
    terms, blocks = targets.shape
    total = secs * blocks
    my_sec = lax.axis_index("sec")

    def clear(index, carry):
        tile[index] = 0
        block[index] = blocks
        return carry

    lax.fori_loop(0, 4 * cap, clear, 0)
    lax.fori_loop(0, 2 * cap, lambda index, carry: (slot.__setitem__(index, 0), carry)[1], 0)
    for index in range(total + 1):
        fill[index] = 0

    def relative(target):
        owner = lax.div(jnp.maximum(target, 0), blocks)
        turn = owner - my_sec
        turn = jnp.where(turn < 0, turn + secs, turn)
        place = turn * blocks + (target - owner * blocks)
        return jnp.where(target < 0, total, place)

    def count(term, carry):
        for b in range(blocks):
            place = relative(targets[term, b])
            fill[place] = fill[place] + 1
        return carry

    lax.fori_loop(0, terms, count, 0)

    for region, places in ((REMOTE, range(blocks, total)), (OWN, range(blocks))):
        step = jnp.int32(region * cap)
        for place in places:
            steps = lax.div(fill[place] + 1, 2)

            def mark(index, carry, place=place, places=places):
                slot[index] = place - places[0]
                return carry

            lax.fori_loop(step, step + steps, mark, 0)
            fill[place] = 2 * step
            step = step + steps
        groups[region] = lax.div(step - region * cap + GROUP - 1, GROUP)
    fill[total] = 4 * cap

    def place_pairs(term, carry):
        for b in range(blocks):
            place = relative(targets[term, b])
            at = fill[place]
            fill[place] = at + 1
            tile[at] = term * blocks + b
            block[at] = b
        return carry

    lax.fori_loop(0, terms, place_pairs, 0)
    square[0, 0] = jnp.sum(wave[...] * wave[...])


def plan(targets, wave, secs):
    terms, blocks = targets.shape
    pairs = terms * blocks
    cap = step_cap(pairs, secs * blocks)
    return pl.pallas_call(
        functools.partial(plan_kernel, secs, cap),
        out_shape=(i32(4 * cap + pairs), i32(4 * cap + pairs), i32(2 * cap), i32(2), f32(1, 1)),
        in_specs=[SMEM, VMEM],
        out_specs=(SMEM,) * 5,
        scratch_shapes=[pltpu.SMEM((secs * blocks + 1,), jnp.int32)],
        name="plan",
    )(targets, wave)


def terms_kernel(
    region, cap, tile, block, slot, groups, vector, left, right, keep, send,
    vector_bf, left_buf, right_buf, product, total, left_sem, right_sem, out_sem,
):
    blocks = vector.shape[0]
    my_sub = lax.axis_index("sub")
    many = 2 * GROUP
    count = groups[region]

    def fetch(group, carry):
        buf = lax.rem(group, SLOTS)
        for k in range(many):
            pair = tile[2 * region * cap + group * many + k]
            pltpu.make_async_copy(left.at[pair], left_buf.at[buf, k], left_sem.at[buf]).start()
            pltpu.make_async_copy(right.at[pair], right_buf.at[buf, k], right_sem.at[buf]).start()
        return carry

    def arrive(group):
        buf = lax.rem(group, SLOTS)
        pltpu.make_async_copy(left_buf.at[buf], left_buf.at[buf], left_sem.at[buf]).wait()
        pltpu.make_async_copy(right_buf.at[buf], right_buf.at[buf], right_sem.at[buf]).wait()

    def first(group):
        buf = lax.rem(group, SLOTS)
        for k in range(many):
            b = block[2 * region * cap + group * many + k]
            part = jnp.dot(left_buf[buf, k], vector_bf[b], preferred_element_type=jnp.float32)
            half = part.shape[1]
            product[k // 2, :, (k % 2) * half : (k % 2 + 1) * half] = part.astype(jnp.bfloat16)

    def second(group):
        buf = lax.rem(group, SLOTS)
        for g in range(GROUP):
            n = slot[region * cap + group * GROUP + g]
            pair = right_buf[buf, 2 * g : 2 * g + 2]
            pair = pair.reshape(2 * pair.shape[1], pair.shape[2])
            image = jnp.dot(product[g], pair, preferred_element_type=jnp.float32)
            half = image.shape[1] // 2
            total[0, n] += image[:, :half]
            total[1, n] += image[:, half:]

    lax.fori_loop(0, jnp.minimum(count, SLOTS), fetch, 0)
    vector_bf[:blocks] = vector[...].astype(jnp.bfloat16)
    vector_bf[blocks] = jnp.zeros(vector_bf.shape[1:], jnp.bfloat16)
    total[...] = jnp.zeros_like(total)

    @pl.when(count > 0)
    def _():
        arrive(0)
        first(0)

        def turn(group, carry):
            arrive(group)
            second(group - 1)
            first(group)

            @pl.when(group - 1 + SLOTS < count)
            def _():
                fetch(group - 1 + SLOTS, 0)

            return carry

        lax.fori_loop(1, count, turn, 0)
        second(count - 1)

    kept = pltpu.make_async_copy(total.at[my_sub], keep, out_sem.at[0])
    sent = pltpu.make_async_copy(total.at[1 - my_sub], send, out_sem.at[1])
    sent.start()
    kept.start()
    sent.wait()
    kept.wait()


def term_images(region, slots, planned, vector, left, right):
    tile, block, slot, groups, cap = planned
    blocks, rows, half = vector.shape
    many = 2 * GROUP
    return pl.pallas_call(
        functools.partial(terms_kernel, region, cap),
        out_shape=(f32(slots, rows, half), f32(slots, rows, half)),
        in_specs=[SMEM] * 4 + [VMEM, ANY, ANY],
        out_specs=(ANY, ANY),
        scratch_shapes=[
            pltpu.VMEM((blocks + 1, rows, half), jnp.bfloat16),
            pltpu.VMEM((SLOTS, many, rows, rows), jnp.bfloat16),
            pltpu.VMEM((SLOTS, many, half, rows), jnp.bfloat16),
            pltpu.VMEM((GROUP, rows, rows), jnp.bfloat16),
            pltpu.VMEM((2, slots, rows, half), jnp.float32),
            pltpu.SemaphoreType.DMA((SLOTS,)),
            pltpu.SemaphoreType.DMA((SLOTS,)),
            pltpu.SemaphoreType.DMA((2,)),
        ],
        compiler_params=pltpu.CompilerParams(vmem_limit_bytes=24 * 1024 * 1024),
        cost_estimate=pl.CostEstimate(flops=10**9, bytes_accessed=9 * 2**20, transcendentals=0),
        name="remote_images" if region == REMOTE else "own_images",
    )(tile, block, slot, groups, vector, left, right)


def add_kernel(a, b, out):
    out[...] = a[...] + b[...]


def add(a, b):
    return pl.pallas_call(
        add_kernel, out_shape=f32(*a.shape), in_specs=[VMEM] * 2, out_specs=VMEM, name="add"
    )(a, b)


def combine_kernel(arrived, vector, diagonal, *refs):
    parts, outs, inner = refs[:arrived], refs[arrived:-1], refs[-1]
    ops = len(outs)
    my_op = lax.axis_index("op")
    inner_sum = jnp.float32(0)
    for turn in range(ops):
        at = lax.rem(my_op + turn, ops)
        total = parts[0][at]
        for part in parts[1:]:
            total = total + part[at]
        outs[turn][...] = total
        held = vector[at]
        if turn == 0:
            inner_sum += jnp.sum(held * (diagonal[at] * held + total))
        else:
            inner_sum += jnp.sum(held * total)
    inner[0, 0] = inner_sum


def combine(vector, diagonal, parts):
    ops, rows, half = vector.shape
    outs = pl.pallas_call(
        functools.partial(combine_kernel, len(parts)),
        out_shape=(f32(rows, half),) * ops + (f32(1, 1),),
        in_specs=[VMEM] * (2 + len(parts)),
        out_specs=(VMEM,) * ops + (SMEM,),
        name="combine",
    )(vector, diagonal, *parts)
    return outs[:-1], outs[-1]


def correct_kernel(entries, theta_sum, vector, diagonal, *refs):
    parts, (correction, sums) = refs[:-2], refs[-2:]
    my_op = lax.axis_index("op")
    theta = theta_sum[0, 0] / entries
    held, diag = vector[my_op], diagonal[my_op]
    sigma = diag * held
    for part in parts:
        sigma = sigma + part[...]
    value = (sigma - theta * held) / (1.0 + jnp.abs(diag - theta))
    correction[...] = value
    sums[0, 0] = jnp.sum(held * value)
    sums[0, 1] = jnp.sum(value * value)
    sums[0, 2] = jnp.sum(held * held)


def correct(entries, theta_sum, vector, diagonal, parts):
    ops, rows, half = vector.shape
    return pl.pallas_call(
        functools.partial(correct_kernel, entries),
        out_shape=(f32(rows, half), f32(1, 3)),
        in_specs=[SMEM] + [VMEM] * (2 + len(parts)),
        out_specs=(VMEM, SMEM),
        name="correct",
    )(theta_sum, vector, diagonal, *parts)


def refine_kernel(entries, sums, vector, *refs):
    parts, out = refs[:-1], refs[-1]
    ops = len(parts)
    my_op = lax.axis_index("op")
    shape = parts[0].shape
    along = jnp.full(shape, sums[0, 0] / entries)
    square = jnp.full(shape, sums[0, 1] / entries)
    own = jnp.full(shape, sums[0, 2] / entries)
    length_sq = (1.0 + along) * (1.0 + along) * own - 2.0 * (1.0 + along) * along + square
    length = jnp.sqrt(length_sq)
    for turn in range(ops):
        at = lax.rem(my_op + ops - turn, ops)
        held = vector[at]
        out[at] = (held - (parts[turn][...] - along * held)) / length


def refine(entries, sums, vector, parts):
    return pl.pallas_call(
        functools.partial(refine_kernel, entries),
        out_shape=f32(*vector.shape),
        in_specs=[SMEM] + [VMEM] * (1 + len(parts)),
        out_specs=VMEM,
        name="refine",
    )(sums, vector, *parts)


def shift(array, axis, turn):
    count = lax.axis_size(axis)
    return lax.ppermute(array, axis, [(i, (i + turn) % count) for i in range(count)])


def per_device(wavefunction, diagonal, left_env, right_env, targets):
    ops, secs = lax.axis_size("op"), lax.axis_size("sec")
    blocks, tile, half = wavefunction.shape
    terms = left_env.shape[0]
    entries = blocks * secs * tile * tile
    left = left_env.reshape(terms * blocks, tile, tile)
    right = right_env.reshape(terms * blocks, half, tile)
    split = (ops, blocks * tile // ops, half)
    *lists, square = plan(targets, wavefunction, secs)
    planned = (*lists, step_cap(terms * blocks, secs * blocks))
    start = lax.psum(square, ("sec", "sub"))
    vector = wavefunction / jnp.sqrt(start[0, 0] / entries)
    diagonal = diagonal.reshape(split)
    ritz_list = []
    for turn_index in range(ITERS):
        keep, send = term_images(REMOTE, (secs - 1) * blocks, planned, vector, left, right)
        remote = add(keep, shift(send, "sub", 1))
        arrived = [shift(remote[(r - 1) * blocks : r * blocks], "sec", r) for r in range(1, secs)]
        keep, send = term_images(OWN, blocks, planned, vector, left, right)
        parts = [keep, shift(send, "sub", 1), *arrived]
        vector = vector.reshape(split)
        pieces, inner = combine(vector, diagonal, [part.reshape(split) for part in parts])
        landed = [shift(pieces[k], "op", k) for k in range(1, ops)]
        theta_sum = lax.psum(inner, ("op", "sec", "sub"))
        correction, sums = correct(entries, theta_sum, vector, diagonal, [pieces[0], *landed])
        spread = [correction, *[shift(correction, "op", k) for k in range(1, ops)]]
        sums = lax.psum(sums, ("op", "sec", "sub"))
        vector = refine(entries, sums, vector, spread).reshape(blocks, tile, half)
        ritz_list.append(theta_sum[0, 0] / entries)
    return (vector, jnp.stack(ritz_list))


def solution(mesh):
    placed = (
        P(("grp", "sec"), None, "sub"),
        P(("grp", "sec"), None, "sub"),
        P(("grp", "op"), "sec", None, None),
        P(("grp", "op"), "sec", "sub", None),
        P(("grp", "op"), "sec"),
    )
    return jax.shard_map(
        per_device,
        mesh=mesh,
        in_specs=placed,
        out_specs=(P(("grp", "sec"), None, "sub"), P("grp")),
        check_vma=False,
    )
```

time: 434 us -> 315 us (0.73)
  waiting for transfers between devices: 195 us -> 27.7 us
  Pallas kernels: 0 us -> 97.9 us
  blocking collectives: 48.9 us -> 137 us
  matrix products: 73.4 us -> 0 us
  other arithmetic: 72.8 us -> 1.67 us
  between operations: 18.8 us -> 2.93 us
  starting transfers between devices: 0.08 us -> 15 us
  local copies, waits for them, and re-layouts: 20.8 us -> 30.5 us
    psum x2 -> x0, waiting for transfers between devices: 195 us -> none  [per_device(): full_sum = lax.psum(partial_sum, ('op', 'sec', 'sub'))]
    pallas_call x0 -> x13, Pallas kernels: none -> 97.9 us  [the longest x4 73.2 us: term_images(): pl.pallas_call(functools.partial(terms_kernel, region, cap), out_shape=(f...]
    psum x7 -> x5, blocking collectives: 48.9 us -> 137 us  [the longest x2 65.3 us: per_device(): theta_sum = lax.psum(inner, ('op', 'sec', 'sub'))]
    dot_general x48 -> x0, matrix products: 73.4 us -> none  [accumulate(): jnp.einsum('bik,bkhc->bihc', product, right_term, preferred_element_type=...]
    scatter-add x48 -> x0, other arithmetic: 55.4 us -> none  [accumulate(): return (total.at[slot_row].add(image, mode='drop'), None)]
    ppermute x0 -> x18, waiting for transfers between devices: none -> 27.7 us  [shift(): lax.ppermute(array, axis, [(i, (i + turn) % count) for i in range(count)])]
    unnamed x13 -> x73, local copies, waits for them, and re-layouts: 8.65 us -> 30.5 us
    ppermute x0 -> x18, starting transfers between devices: none -> 15 us  [shift(): lax.ppermute(array, axis, [(i, (i + turn) % count) for i in range(count)])]
  transfers between devices with their start and end apart: 2 -> 18, of which waited for: 2 -> 2; matrix products, arithmetic and copies ran while one was open for 0% -> 0% of each run, Pallas kernels for 0% -> 19%
where the time goes in v1:
time: 315 us; the launch traced here: 313 us
  blocking collectives  137 us (43%)
  Pallas kernels  97.9 us (31%)
  local copies, waits for them, and re-layouts  30.5 us (10%)
  waiting for transfers between devices  27.7 us (9%)
  starting transfers between devices  15 us (5%)
    pallas_call x4, Pallas kernels, term_images(): pl.pallas_call(functools.partial(terms_kernel, region, cap), out_shape=(f...  73.2 us
    psum x2, blocking collectives, per_device(): theta_sum = lax.psum(inner, ('op', 'sec', 'sub'))  65.3 us
    psum x2, blocking collectives, per_device(): sums = lax.psum(sums, ('op', 'sec', 'sub'))  62.8 us
    unnamed x73, local copies, waits for them, and re-layouts  30.5 us
    ppermute x18, waiting for transfers between devices, shift(): lax.ppermute(array, axis, [(i, (i + turn) % count) for i in range(count)])  27.7 us
    ppermute x18, starting transfers between devices, shift(): lax.ppermute(array, axis, [(i, (i + turn) % count) for i in range(count)])  15 us
    psum x1, blocking collectives, per_device(): start = lax.psum(square, ('sec', 'sub'))  8.85 us
  transfers between devices with their start and end apart: 18, of which 2 were waited for; matrix products, arithmetic and copies ran while one was open for 0% of the time, Pallas kernels for 19%

profile of v1, /device:TPU:0, one launch (start us, length us, event | category | flops | bytes accessed | tf_op | source)
XLA Modules:
  0.0 312.6 jit_solution(2085880002785759414)
XLA Ops:
  0.6 1.4 copy.7.targets
  2.0 5.7 %plan.1 = (s32[312]{0:T(512)}, s32[312]{0:T(512)}, s32[108]{0:T(128)}, s32[2]{0:T(128)}, f32[1,1]{1,0:T(1,128)}) custom-call(s32[24,4]{1,0:T(8,128)} %copy.7.targets, f32[4,256,128]{2,1,0:T(8,128)} %wave.1), custom_call_target="tpu_custom_call" | custom-call | tf_op jit(solution)/shard_map/plan/pallas_call | solution.py:94
  7.7 8.8 %psum.35 = f32[1,1]{1,0:T(1,128)} all-reduce(f32[1,1]{1,0:T(1,128)} %get-tuple-element.29), channel_id=1, replica_groups=mesh['grp'=2,'op'=4,'sec'=2,'sub'=2] {'sec','sub'}, use_global_device_ids=true, to_apply=%region_0.0 | all-reduce | flops 1 | bytes 8 | tf_op jit(solution)/shard_map/psum | solution.py:310
  17.3 1.1 broadcast_divide_fusion.vector
  18.4 4.8 %copy-done = bf16[24,4,256,256]{3,2,1,0:T(8,128)(2,1)S(1)} copy-done((bf16[24,4,256,256]{3,2,1,0:T(8,128)(2,1)S(1)}, bf16[24,4,256,256]{3,2,1,0:T(8,128)(2,1)}, u32[]{:S(2)}) %copy-start) | copy-done | bytes 12582936
  23.1 2.8 copy-done.2
  28.5 8.3 %remote_images.2 = (f32[4,256,128]{2,1,0:T(8,128)S(1)}, f32[4,256,128]{2,1,0:T(8,128)S(1)}) custom-call(s32[312]{0:T(512)S(1)} %copy-done.10, s32[312]{0:T(512)S(1)} %copy-done.12, s32[108]{0:T(128)S(1)} %copy-done.14, s32[2]{0:T(128)S(1)} %copy-done.16, f32[4,256,128]{2,1,0:T(8,128)S(1)} %broadcast_divide_fusion.vector, bf16[96,256,256]{2,1,0:T(8,128)(2,1)S(1)} %bitcast.5, ...), custom_call_target="tpu_custom_call" | custom-call | flops 1000000000 | bytes 9437184 | tf_op jit(solution)/shard_map/remote_images/pallas_call | solution.py:181
  37.7 28.3 %own_images.2 = (f32[4,256,128]{2,1,0:T(8,128)S(1)}, f32[4,256,128]{2,1,0:T(8,128)S(1)}) custom-call(s32[312]{0:T(512)S(1)} %copy-done.10, s32[312]{0:T(512)S(1)} %copy-done.12, s32[108]{0:T(128)S(1)} %copy-done.14, s32[2]{0:T(128)S(1)} %copy-done.16, f32[4,256,128]{2,1,0:T(8,128)S(1)} %broadcast_divide_fusion.vector, bf16[96,256,256]{2,1,0:T(8,128)(2,1)S(1)} %bitcast.6, ...), custom_call_target="tpu_custom_call" | custom-call | flops 1000000000 | bytes 9437184 | tf_op jit(solution)/shard_map/own_images/pallas_call | solution.py:181
  68.2 2.1 add.12
  70.6 13.7 %collective-permute-done.2.refs_2_ = f32[4,256,128]{2,1,0:T(8,128)S(1)} collective-permute-done((f32[4,256,128]{2,1,0:T(8,128)}, f32[4,256,128]{2,1,0:T(8,128)S(1)}, u32[]{:S(2)}, u32[]{:S(2)}) %collective-permute-start.2) | collective-permute-done | bytes 524320 | tf_op jit(solution)/shard_map/ppermute | solution.py:297
  85.1 2.6 combine.2
  87.7 3.1 collective-permute-start.3
  90.8 1.1 collective-permute-start.4
  91.9 1.4 collective-permute-start.5
  93.2 33.1 %psum.36.theta_sum = f32[1,1]{1,0:T(1,128)} all-reduce(f32[1,1]{1,0:T(1,128)} %get-tuple-element.38), channel_id=1, replica_groups=mesh['grp'=2,'op'=4,'sec'=2,'sub'=2] {'op','sec','sub'}, use_global_device_ids=true, to_apply=%region_1.0 | all-reduce | flops 1 | bytes 8 | tf_op jit(solution)/shard_map/psum | solution.py:323
  127.1 2.7 correct.2
  130.0 1.9 collective-permute-start.6
  131.9 31.8 %psum.37.sums = f32[1,3]{1,0:T(1,128)} all-reduce(f32[1,3]{1,0:T(1,128)} %get-tuple-element.43), channel_id=1, replica_groups=mesh['grp'=2,'op'=4,'sec'=2,'sub'=2] {'op','sec','sub'}, use_global_device_ids=true, to_apply=%region_2.0 | all-reduce | flops 3 | bytes 24 | tf_op jit(solution)/shard_map/psum | solution.py:326
  165.1 2.1 refine.2.vector
  167.2 4.6 %copy-done.1 = bf16[24,4,256,256]{3,2,1,0:T(8,128)(2,1)S(1)} copy-done((bf16[24,4,256,256]{3,2,1,0:T(8,128)(2,1)S(1)}, bf16[24,4,256,256]{3,2,1,0:T(8,128)(2,1)}, u32[]{:S(2)}) %copy-start.1) | copy-done | bytes 12582936
  171.8 2.8 copy-done.3
  175.6 8.3 %remote_images.3 = (f32[4,256,128]{2,1,0:T(8,128)S(1)}, f32[4,256,128]{2,1,0:T(8,128)S(1)}) custom-call(s32[312]{0:T(512)S(1)} %copy-done.11, s32[312]{0:T(512)S(1)} %copy-done.13, s32[108]{0:T(128)S(1)} %copy-done.15, s32[2]{0:T(128)S(1)} %copy-done.17, f32[4,256,128]{2,1,0:T(8,128)S(1)} %copy-done.4, bf16[96,256,256]{2,1,0:T(8,128)(2,1)S(1)} %bitcast.7, ...), custom_call_target="tpu_custom_call" | custom-call | flops 1000000000 | bytes 9437184 | tf_op jit(solution)/shard_map/remote_images/pallas_call | solution.py:181
  184.8 28.3 %own_images.3 = (f32[4,256,128]{2,1,0:T(8,128)S(1)}, f32[4,256,128]{2,1,0:T(8,128)S(1)}) custom-call(s32[312]{0:T(512)S(1)} %copy-done.11, s32[312]{0:T(512)S(1)} %copy-done.13, s32[108]{0:T(128)S(1)} %copy-done.15, s32[2]{0:T(128)S(1)} %copy-done.17, f32[4,256,128]{2,1,0:T(8,128)S(1)} %copy-done.4, bf16[96,256,256]{2,1,0:T(8,128)(2,1)S(1)} %bitcast.8, ...), custom_call_target="tpu_custom_call" | custom-call | flops 1000000000 | bytes 9437184 | tf_op jit(solution)/shard_map/own_images/pallas_call | solution.py:181
  215.2 2.1 add.13
  217.3 14.0 %collective-permute-done.11.refs_2_ = f32[4,256,128]{2,1,0:T(8,128)S(1)} collective-permute-done((f32[4,256,128]{2,1,0:T(8,128)}, f32[4,256,128]{2,1,0:T(8,128)S(1)}, u32[]{:S(2)}, u32[]{:S(2)}) %collective-permute-start.11) | collective-permute-done | bytes 524320 | tf_op jit(solution)/shard_map/ppermute | solution.py:297
  232.1 2.6 combine.3
  234.9 3.7 %collective-permute-start.14 = (f32[256,128]{1,0:T(8,128)}, f32[256,128]{1,0:T(8,128)S(1)}, u32[]{:S(2)}, u32[]{:S(2)}) collective-permute-start(f32[256,128]{1,0:T(8,128)} %get-tuple-element.53), channel_id=1, source_target_pairs={{0,12},{4,0},{8,4},{12,8},{1,13},{5,1},{9,5},{13,9},{2,14},{6,2},{... | collective-permute-start | bytes 393224 | tf_op jit(solution)/shard_map/ppermute | solution.py:297
  238.6 32.1 %psum.38.theta_sum = f32[1,1]{1,0:T(1,128)} all-reduce(f32[1,1]{1,0:T(1,128)} %get-tuple-element.49), channel_id=1, replica_groups=mesh['grp'=2,'op'=4,'sec'=2,'sub'=2] {'op','sec','sub'}, use_global_device_ids=true, to_apply=%region_3.0 | all-reduce | flops 1 | bytes 8 | tf_op jit(solution)/shard_map/psum | solution.py:323
  271.5 2.7 correct.3
  274.4 1.9 collective-permute-start.15
  278.2 31.0 %psum.39.sums = f32[1,3]{1,0:T(1,128)} all-reduce(f32[1,3]{1,0:T(1,128)} %get-tuple-element.54), channel_id=1, replica_groups=mesh['grp'=2,'op'=4,'sec'=2,'sub'=2] {'op','sec','sub'}, use_global_device_ids=true, to_apply=%region_4.0 | all-reduce | flops 3 | bytes 24 | tf_op jit(solution)/shard_map/psum | solution.py:326
  310.5 2.1 refine.3
  (97 shorter events, 16.8 us)
Async XLA Ops:
  18.4 47.7 %copy-start.5 = (f32[4,256,128]{2,1,0:T(8,128)}, f32[4,256,128]{2,1,0:T(8,128)S(1)}, u32[]{:S(2)}) copy-start(f32[4,256,128]{2,1,0:T(8,128)S(1)} %broadcast_divide_fusion.vector) | copy-start | bytes 1572868
  18.4 4.8 %copy-start = (bf16[24,4,256,256]{3,2,1,0:T(8,128)(2,1)S(1)}, bf16[24,4,256,256]{3,2,1,0:T(8,128)(2,1)}, u32[]{:S(2)}) copy-start(bf16[24,4,256,256]{3,2,1,0:T(8,128)(2,1)} %param.7) | copy-start | bytes 37748740
  23.1 2.8 copy-start.2
  37.6 129.6 %copy-start.11 = (s32[312]{0:T(512)S(1)}, s32[312]{0:T(512)}, u32[]{:S(2)}) copy-start(s32[312]{0:T(512)} %get-tuple-element.30.tile) | copy-start | bytes 3748
  37.6 129.6 %copy-start.13 = (s32[312]{0:T(512)S(1)}, s32[312]{0:T(512)}, u32[]{:S(2)}) copy-start(s32[312]{0:T(512)} %get-tuple-element.31.block) | copy-start | bytes 3748
  37.6 129.6 %copy-start.15 = (s32[108]{0:T(128)S(1)}, s32[108]{0:T(128)}, u32[]{:S(2)}) copy-start(s32[108]{0:T(128)} %get-tuple-element.32.slot) | copy-start | bytes 1300
  37.6 129.6 %copy-start.17 = (s32[2]{0:T(128)S(1)}, s32[2]{0:T(128)}, u32[]{:S(2)}) copy-start(s32[2]{0:T(128)} %get-tuple-element.33.groups) | copy-start | bytes 28
  37.7 29.7 %collective-permute-start.1 = (f32[4,256,128]{2,1,0:T(8,128)S(1)}, f32[4,256,128]{2,1,0:T(8,128)S(1)}, u32[]{:S(2)}, u32[]{:S(2)}) collective-permute-start(f32[4,256,128]{2,1,0:T(8,128)S(1)} %get-tuple-element.37), channel_id=1, source_target_pairs={{0,1},{1,0},{2,3},{3,2},{4,5},{5,4},{6,7},{7,6},{8,9},{9,8},{10,11... | collective-permute-start | bytes 1572872 | tf_op jit(solution)/shard_map/ppermute | solution.py:297
  66.8 3.8 %collective-permute-start = (f32[4,256,128]{2,1,0:T(8,128)S(1)}, f32[4,256,128]{2,1,0:T(8,128)S(1)}, u32[]{:S(2)}, u32[]{:S(2)}) collective-permute-start(f32[4,256,128]{2,1,0:T(8,128)S(1)} %get-tuple-element.35), channel_id=1, source_target_pairs={{0,1},{1,0},{2,3},{3,2},{4,5},{5,4},{6,7},{7,6},{8,9},{9,8},{10,11... | collective-permute-start | bytes 1572872 | tf_op jit(solution)/shard_map/ppermute | solution.py:297
  70.2 14.1 %collective-permute-start.2 = (f32[4,256,128]{2,1,0:T(8,128)}, f32[4,256,128]{2,1,0:T(8,128)S(1)}, u32[]{:S(2)}, u32[]{:S(2)}) collective-permute-start(f32[4,256,128]{2,1,0:T(8,128)} %add.12), channel_id=1, source_target_pairs={{0,2},{2,0},{1,3},{3,1},{4,6},{6,4},{5,7},{7,5},{8,10},{10,8},{9,1... | collective-permute-start | bytes 1572872 | tf_op jit(solution)/shard_map/ppermute | solution.py:297
  70.6 13.7 %copy-start.18 = (f32[4,256,128]{2,1,0:T(8,128)}, f32[4,256,128]{2,1,0:T(8,128)S(1)}, u32[]{:S(2)}) copy-start(f32[4,256,128]{2,1,0:T(8,128)S(1)} %collective-permute-done.refs_1_) | copy-start | bytes 1572868
  84.3 0.8 copy-start.21
  87.7 38.7 %collective-permute-start.3 = (f32[256,128]{1,0:T(8,128)}, f32[256,128]{1,0:T(8,128)S(1)}, u32[]{:S(2)}, u32[]{:S(2)}) collective-permute-start(f32[256,128]{1,0:T(8,128)} %get-tuple-element.40), channel_id=1, source_target_pairs={{0,4},{4,8},{8,12},{12,0},{1,5},{5,9},{9,13},{13,1},{2,6},{6,10},{... | collective-permute-start | bytes 393224 | tf_op jit(solution)/shard_map/ppermute | solution.py:297
  90.8 35.6 %collective-permute-start.4 = (f32[256,128]{1,0:T(8,128)}, f32[256,128]{1,0:T(8,128)S(1)}, u32[]{:S(2)}, u32[]{:S(2)}) collective-permute-start(f32[256,128]{1,0:T(8,128)} %get-tuple-element.41), channel_id=1, source_target_pairs={{0,8},{4,12},{8,0},{12,4},{1,9},{5,13},{9,1},{13,5},{2,10},{6,14},... | collective-permute-start | bytes 393224 | tf_op jit(solution)/shard_map/ppermute | solution.py:297
  91.9 34.5 %collective-permute-start.5 = (f32[256,128]{1,0:T(8,128)}, f32[256,128]{1,0:T(8,128)S(1)}, u32[]{:S(2)}, u32[]{:S(2)}) collective-permute-start(f32[256,128]{1,0:T(8,128)} %get-tuple-element.42), channel_id=1, source_target_pairs={{0,12},{4,0},{8,4},{12,8},{1,13},{5,1},{9,5},{13,9},{2,14},{6,2},{... | collective-permute-start | bytes 393224 | tf_op jit(solution)/shard_map/ppermute | solution.py:297
  129.8 33.9 %collective-permute-start.8 = (f32[256,128]{1,0:T(8,128)}, f32[256,128]{1,0:T(8,128)S(1)}, u32[]{:S(2)}, u32[]{:S(2)}) collective-permute-start(f32[256,128]{1,0:T(8,128)} %get-tuple-element.44.refs_0_), channel_id=1, source_target_pairs={{0,12},{4,0},{8,4},{12,8},{1,13},{5,1},{9,5},{13,9},{2,14},{6,2},{... | collective-permute-start | bytes 393224 | tf_op jit(solution)/shard_map/ppermute | solution.py:297
  129.9 33.8 %collective-permute-start.7 = (f32[256,128]{1,0:T(8,128)}, f32[256,128]{1,0:T(8,128)S(1)}, u32[]{:S(2)}, u32[]{:S(2)}) collective-permute-start(f32[256,128]{1,0:T(8,128)} %get-tuple-element.44.refs_0_), channel_id=1, source_target_pairs={{0,8},{4,12},{8,0},{12,4},{1,9},{5,13},{9,1},{13,5},{2,10},{6,14},... | collective-permute-start | bytes 393224 | tf_op jit(solution)/shard_map/ppermute | solution.py:297
  130.0 33.8 %collective-permute-start.6 = (f32[256,128]{1,0:T(8,128)}, f32[256,128]{1,0:T(8,128)S(1)}, u32[]{:S(2)}, u32[]{:S(2)}) collective-permute-start(f32[256,128]{1,0:T(8,128)} %get-tuple-element.44.refs_0_), channel_id=1, source_target_pairs={{0,4},{4,8},{8,12},{12,0},{1,5},{5,9},{9,13},{13,1},{2,6},{6,10},{... | collective-permute-start | bytes 393224 | tf_op jit(solution)/shard_map/ppermute | solution.py:297
  167.2 4.6 %copy-start.1 = (bf16[24,4,256,256]{3,2,1,0:T(8,128)(2,1)S(1)}, bf16[24,4,256,256]{3,2,1,0:T(8,128)(2,1)}, u32[]{:S(2)}) copy-start(bf16[24,4,256,256]{3,2,1,0:T(8,128)(2,1)} %param.7) | copy-start | bytes 37748740
  171.8 2.8 copy-start.3
  174.6 1.0 copy-start.4
  184.8 29.6 %collective-permute-start.10 = (f32[4,256,128]{2,1,0:T(8,128)S(1)}, f32[4,256,128]{2,1,0:T(8,128)S(1)}, u32[]{:S(2)}, u32[]{:S(2)}) collective-permute-start(f32[4,256,128]{2,1,0:T(8,128)S(1)} %get-tuple-element.48), channel_id=1, source_target_pairs={{0,1},{1,0},{2,3},{3,2},{4,5},{5,4},{6,7},{7,6},{8,9},{9,8},{10,11... | collective-permute-start | bytes 1572872 | tf_op jit(solution)/shard_map/ppermute | solution.py:297
  213.9 3.4 %collective-permute-start.9 = (f32[4,256,128]{2,1,0:T(8,128)S(1)}, f32[4,256,128]{2,1,0:T(8,128)S(1)}, u32[]{:S(2)}, u32[]{:S(2)}) collective-permute-start(f32[4,256,128]{2,1,0:T(8,128)S(1)} %get-tuple-element.46), channel_id=1, source_target_pairs={{0,1},{1,0},{2,3},{3,2},{4,5},{5,4},{6,7},{7,6},{8,9},{9,8},{10,11... | collective-permute-start | bytes 1572872 | tf_op jit(solution)/shard_map/ppermute | solution.py:297
  217.3 14.0 %collective-permute-start.11 = (f32[4,256,128]{2,1,0:T(8,128)}, f32[4,256,128]{2,1,0:T(8,128)S(1)}, u32[]{:S(2)}, u32[]{:S(2)}) collective-permute-start(f32[4,256,128]{2,1,0:T(8,128)} %add.13), channel_id=1, source_target_pairs={{0,2},{2,0},{1,3},{3,1},{4,6},{6,4},{5,7},{7,5},{8,10},{10,8},{9,1... | collective-permute-start | bytes 1572872 | tf_op jit(solution)/shard_map/ppermute | solution.py:297
  217.3 14.0 %copy-start.19 = (f32[4,256,128]{2,1,0:T(8,128)}, f32[4,256,128]{2,1,0:T(8,128)S(1)}, u32[]{:S(2)}) copy-start(f32[4,256,128]{2,1,0:T(8,128)S(1)} %collective-permute-done.9.refs_1_) | copy-start | bytes 1572868
  231.3 0.8 copy-start.22
  234.7 36.0 %collective-permute-start.12 = (f32[256,128]{1,0:T(8,128)}, f32[256,128]{1,0:T(8,128)S(1)}, u32[]{:S(2)}, u32[]{:S(2)}) collective-permute-start(f32[256,128]{1,0:T(8,128)} %get-tuple-element.51), channel_id=1, source_target_pairs={{0,4},{4,8},{8,12},{12,0},{1,5},{5,9},{9,13},{13,1},{2,6},{6,10},{... | collective-permute-start | bytes 393224 | tf_op jit(solution)/shard_map/ppermute | solution.py:297
  234.8 36.0 %collective-permute-start.13 = (f32[256,128]{1,0:T(8,128)}, f32[256,128]{1,0:T(8,128)S(1)}, u32[]{:S(2)}, u32[]{:S(2)}) collective-permute-start(f32[256,128]{1,0:T(8,128)} %get-tuple-element.52), channel_id=1, source_target_pairs={{0,8},{4,12},{8,0},{12,4},{1,9},{5,13},{9,1},{13,5},{2,10},{6,14},... | collective-permute-start | bytes 393224 | tf_op jit(solution)/shard_map/ppermute | solution.py:297
  234.9 35.9 %collective-permute-start.14 = (f32[256,128]{1,0:T(8,128)}, f32[256,128]{1,0:T(8,128)S(1)}, u32[]{:S(2)}, u32[]{:S(2)}) collective-permute-start(f32[256,128]{1,0:T(8,128)} %get-tuple-element.53), channel_id=1, source_target_pairs={{0,12},{4,0},{8,4},{12,8},{1,13},{5,1},{9,5},{13,9},{2,14},{6,2},{... | collective-permute-start | bytes 393224 | tf_op jit(solution)/shard_map/ppermute | solution.py:297
  274.2 34.9 %collective-permute-start.17 = (f32[256,128]{1,0:T(8,128)}, f32[256,128]{1,0:T(8,128)S(1)}, u32[]{:S(2)}, u32[]{:S(2)}) collective-permute-start(f32[256,128]{1,0:T(8,128)} %get-tuple-element.55.refs_0_), channel_id=1, source_target_pairs={{0,12},{4,0},{8,4},{12,8},{1,13},{5,1},{9,5},{13,9},{2,14},{6,2},{... | collective-permute-start | bytes 393224 | tf_op jit(solution)/shard_map/ppermute | solution.py:297
  274.3 34.9 %collective-permute-start.16 = (f32[256,128]{1,0:T(8,128)}, f32[256,128]{1,0:T(8,128)S(1)}, u32[]{:S(2)}, u32[]{:S(2)}) collective-permute-start(f32[256,128]{1,0:T(8,128)} %get-tuple-element.55.refs_0_), channel_id=1, source_target_pairs={{0,8},{4,12},{8,0},{12,4},{1,9},{5,13},{9,1},{13,5},{2,10},{6,14},... | collective-permute-start | bytes 393224 | tf_op jit(solution)/shard_map/ppermute | solution.py:297
  274.4 34.8 %collective-permute-start.15 = (f32[256,128]{1,0:T(8,128)}, f32[256,128]{1,0:T(8,128)S(1)}, u32[]{:S(2)}, u32[]{:S(2)}) collective-permute-start(f32[256,128]{1,0:T(8,128)} %get-tuple-element.55.refs_0_), channel_id=1, source_target_pairs={{0,4},{4,8},{8,12},{12,0},{1,5},{5,9},{9,13},{13,1},{2,6},{6,10},{... | collective-permute-start | bytes 393224 | tf_op jit(solution)/shard_map/ppermute | solution.py:297
  (22 other events, 15.7 us)

commit v2 on v1

v2 whole, which is shorter than its diff:
```python
import functools

import jax
import jax.numpy as jnp
from jax import lax
from jax.experimental import pallas as pl
from jax.experimental.pallas import tpu as pltpu
from jax.sharding import PartitionSpec as P

ITERS = 2
GROUP = 4
REMOTE, OWN = 0, 1
VMEM = pl.BlockSpec(memory_space=pltpu.VMEM)
SMEM = pl.BlockSpec(memory_space=pltpu.SMEM)


def f32(*shape):
    return jax.ShapeDtypeStruct(shape, jnp.float32)


def limit(mebibytes):
    return pltpu.CompilerParams(vmem_limit_bytes=mebibytes * 2**20)


def step_cap(pairs, slots):
    steps = (pairs + slots) // 2 + GROUP
    return -(-steps // GROUP) * GROUP


def list_places(pairs, slots):
    cap = step_cap(pairs, slots)
    block = 4 * cap + pairs
    slot = 2 * block
    groups = slot + 2 * cap
    return cap, block, slot, groups, groups + 2


def plan_kernel(secs, places, targets, wave, lists, square, fill):
    terms, blocks = targets.shape
    total = secs * blocks
    cap, block, slot, groups, _ = places
    my_sec = lax.axis_index("sec")

    def clear(index, carry):
        lists[index] = 0
        lists[block + index] = blocks
        return carry

    def clear_slot(index, carry):
        lists[slot + index] = 0
        return carry

    lax.fori_loop(0, 4 * cap, clear, 0)
    lax.fori_loop(0, 2 * cap, clear_slot, 0)
    for index in range(total + 1):
        fill[index] = 0

    def relative(target):
        owner = lax.div(jnp.maximum(target, 0), blocks)
        turn = owner - my_sec
        turn = jnp.where(turn < 0, turn + secs, turn)
        place = turn * blocks + (target - owner * blocks)
        return jnp.where(target < 0, total, place)

    def count(term, carry):
        for b in range(blocks):
            place = relative(targets[term, b])
            fill[place] = fill[place] + 1
        return carry

    lax.fori_loop(0, terms, count, 0)

    for region, span in ((REMOTE, range(blocks, total)), (OWN, range(blocks))):
        step = jnp.int32(region * cap)
        for place in span:
            steps = lax.div(fill[place] + 1, 2)

            def mark(index, carry, value=place - span[0]):
                lists[slot + index] = value
                return carry

            lax.fori_loop(step, step + steps, mark, 0)
            fill[place] = 2 * step
            step = step + steps
        lists[groups + region] = lax.div(step - region * cap + GROUP - 1, GROUP)
    fill[total] = 4 * cap

    def place_pairs(term, carry):
        for b in range(blocks):
            place = relative(targets[term, b])
            at = fill[place]
            fill[place] = at + 1
            lists[at] = term * blocks + b
            lists[block + at] = b
        return carry

    lax.fori_loop(0, terms, place_pairs, 0)
    square[...] = jnp.full(square.shape, jnp.sum(wave[...] * wave[...]))


def plan(targets, wave, secs):
    terms, blocks = targets.shape
    places = list_places(terms * blocks, secs * blocks)
    return pl.pallas_call(
        functools.partial(plan_kernel, secs, places),
        out_shape=(jax.ShapeDtypeStruct((places[-1],), jnp.int32), f32(8, 128)),
        in_specs=[SMEM, VMEM],
        out_specs=(SMEM, VMEM),
        scratch_shapes=[pltpu.SMEM((secs * blocks + 1,), jnp.int32)],
        compiler_params=limit(2),
        name="plan",
    )(targets, wave)


def added(refs):
    total = refs[0][...]
    for ref in refs[1:]:
        total = total + ref[...]
    return total


def multiply_terms(region, places, lists, left, right, vector_bf, product, keep, send):
    cap, block, slot, groups, _ = places
    my_sub = lax.axis_index("sub")
    many = 2 * GROUP
    half = keep.shape[2]
    count = lists[groups + region]
    keep[...] = jnp.zeros_like(keep)
    send[...] = jnp.zeros_like(send)

    def first(group):
        for k in range(many):
            at = 2 * region * cap + group * many + k
            part = jnp.dot(
                left[lists[at]], vector_bf[lists[block + at]], preferred_element_type=jnp.float32
            )
            product[k // 2, :, (k % 2) * half : (k % 2 + 1) * half] = part.astype(jnp.bfloat16)

    def second(group):
        for g in range(GROUP):
            at = region * cap + group * GROUP + g
            pair = jnp.concatenate([right[lists[2 * at]], right[lists[2 * at + 1]]], axis=0)
            image = jnp.dot(product[g], pair, preferred_element_type=jnp.float32)
            low, high = image[:, :half], image[:, half:]
            n = lists[slot + at]
            keep[n] += jnp.where(my_sub == 0, low, high)
            send[n] += jnp.where(my_sub == 0, high, low)

    @pl.when(count > 0)
    def _():
        first(0)

        def turn(group, carry):
            second(group - 1)
            first(group)
            return carry

        lax.fori_loop(1, count, turn, 0)
        second(count - 1)


def round_vector(vector, vector_bf):
    blocks = vector.shape[0]
    vector_bf[:blocks] = vector[...].astype(jnp.bfloat16)
    vector_bf[blocks] = jnp.zeros(vector_bf.shape[1:], jnp.bfloat16)


def start_kernel(entries, norms, places, lists, wave, *refs):
    norm_refs, (left, right, vector, keep, send, vector_bf, product) = refs[:norms], refs[norms:]
    length = jnp.sqrt(added(norm_refs)[:1, :1] / entries)
    vector[...] = wave[...] / length[None]
    round_vector(vector, vector_bf)
    multiply_terms(REMOTE, places, lists, left, right, vector_bf, product, keep, send)


def refined(entries, held_ref, sum_refs, parts, out):
    ops = len(parts)
    my_op = lax.axis_index("op")
    sums = added(sum_refs) / entries
    along, square, own = sums[0:1, :1], sums[1:2, :1], sums[2:3, :1]
    length = jnp.sqrt((1.0 + along) * (1.0 + along) * own - 2.0 * (1.0 + along) * along + square)
    rows = out.shape[0] * out.shape[1] // ops
    each = max(rows, out.shape[1])
    for turn in range(ops):
        place = lax.rem(my_op + ops - turn, ops)
        if rows >= out.shape[1]:
            at = pl.ds(place * (rows // out.shape[1]), rows // out.shape[1])
            held = held_ref[at]
            value = parts[turn][...].reshape(held.shape)
            out[at] = (held - (value - along[None] * held)) / length[None]
        else:
            share = out.shape[1] // rows
            at = (lax.div(place, share), pl.ds(pl.multiple_of(lax.rem(place, share) * rows, rows), rows))
            held = held_ref[at]
            out[at] = (held - (parts[turn][...] - along * held)) / length


def resume_kernel(entries, sums, ops, places, lists, held, *refs):
    sum_refs, parts, refs = refs[:sums], refs[sums : sums + ops], refs[sums + ops :]
    left, right, vector, keep, send, vector_bf, product = refs
    refined(entries, held, sum_refs, parts, vector)
    round_vector(vector, vector_bf)
    multiply_terms(REMOTE, places, lists, left, right, vector_bf, product, keep, send)


def own_kernel(places, lists, vector, left, right, keep, send, vector_bf, product):
    round_vector(vector, vector_bf)
    multiply_terms(OWN, places, lists, left, right, vector_bf, product, keep, send)


def images(kernel, slots, with_vector, name, lists, *operands):
    right = operands[-1]
    half, rows = right.shape[1:]
    vector = operands[0]
    out = (f32(slots, rows, half),) * 2
    if with_vector:
        out = (f32(*vector.shape), *out)
    return pl.pallas_call(
        kernel,
        out_shape=out,
        in_specs=[SMEM] + [VMEM] * len(operands),
        out_specs=(VMEM,) * len(out),
        scratch_shapes=[
            pltpu.VMEM((vector.shape[0] + 1, rows, half), jnp.bfloat16),
            pltpu.VMEM((GROUP, rows, rows), jnp.bfloat16),
        ],
        compiler_params=limit(28),
        cost_estimate=pl.CostEstimate(flops=10**9, bytes_accessed=9 * 2**20, transcendentals=0),
        name=name,
    )(lists, *operands)


def add_kernel(*refs):
    refs[-1][...] = added(refs[:-1])


def add(*parts):
    return pl.pallas_call(
        add_kernel,
        out_shape=f32(*parts[0].shape),
        in_specs=[VMEM] * len(parts),
        out_specs=VMEM,
        compiler_params=limit(6),
        name="add",
    )(*parts)


def combine_kernel(arrived, vector, diagonal, *refs):
    parts, outs, inner = refs[:arrived], refs[arrived:-1], refs[-1]
    ops = len(outs)
    my_op = lax.axis_index("op")
    inner_sum = jnp.float32(0)
    for turn in range(ops):
        at = lax.rem(my_op + turn, ops)
        total = parts[0][at]
        for part in parts[1:]:
            total = total + part[at]
        outs[turn][...] = total
        held = vector[at]
        if turn == 0:
            inner_sum += jnp.sum(held * (diagonal[at] * held + total))
        else:
            inner_sum += jnp.sum(held * total)
    inner[...] = jnp.full(inner.shape, inner_sum)


def combine(vector, diagonal, parts):
    ops, rows, half = vector.shape
    outs = pl.pallas_call(
        functools.partial(combine_kernel, len(parts)),
        out_shape=(f32(rows, half),) * ops + (f32(8, 128),),
        in_specs=[VMEM] * (2 + len(parts)),
        out_specs=(VMEM,) * (ops + 1),
        compiler_params=limit(8),
        name="combine",
    )(vector, diagonal, *parts)
    return outs[:-1], outs[-1]


def correct_kernel(entries, thetas, vector, diagonal, *refs):
    theta_refs, parts, (correction, sums, ritz) = refs[:thetas], refs[thetas:-3], refs[-3:]
    my_op = lax.axis_index("op")
    ritz[...] = added(theta_refs) / entries
    theta = ritz[:1, :1]
    held, diag = vector[my_op], diagonal[my_op]
    sigma = diag * held + added(parts)
    value = (sigma - theta * held) / (1.0 + jnp.abs(diag - theta))
    correction[...] = value
    sums[...] = jnp.zeros_like(sums)
    sums[0:1] = jnp.full((1, 128), jnp.sum(held * value))
    sums[1:2] = jnp.full((1, 128), jnp.sum(value * value))
    sums[2:3] = jnp.full((1, 128), jnp.sum(held * held))


def correct(entries, thetas, vector, diagonal, parts):
    ops, rows, half = vector.shape
    return pl.pallas_call(
        functools.partial(correct_kernel, entries, len(thetas)),
        out_shape=(f32(rows, half), f32(8, 128), f32(8, 128)),
        in_specs=[VMEM] * (2 + len(thetas) + len(parts)),
        out_specs=(VMEM,) * 3,
        compiler_params=limit(4),
        name="correct",
    )(vector, diagonal, *thetas, *parts)


def finish_kernel(entries, sums, held, *refs):
    refined(entries, held, refs[:sums], refs[sums:-1], refs[-1])


def finish(entries, vector, sums, spread):
    return pl.pallas_call(
        functools.partial(finish_kernel, entries, len(sums)),
        out_shape=f32(*vector.shape),
        in_specs=[VMEM] * (1 + len(sums) + len(spread)),
        out_specs=VMEM,
        compiler_params=limit(4),
        name="finish",
    )(vector, *sums, *spread)


def shift(array, axis, turn):
    count = lax.axis_size(axis)
    return lax.ppermute(array, axis, [(i, (i + turn) % count) for i in range(count)])


def from_all(array, axis):
    return [array, *[shift(array, axis, k) for k in range(1, lax.axis_size(axis))]]


def per_device(wavefunction, diagonal, left_env, right_env, targets):
    ops, secs = lax.axis_size("op"), lax.axis_size("sec")
    blocks, tile, half = wavefunction.shape
    terms = left_env.shape[0]
    entries = blocks * secs * tile * tile
    left = left_env.reshape(terms * blocks, tile, tile)
    right = right_env.reshape(terms * blocks, half, tile)
    split = (ops, blocks * tile // ops, half)
    places = list_places(terms * blocks, secs * blocks)
    lists, square = plan(targets, wavefunction, secs)
    away = (secs - 1) * blocks
    split_diagonal = diagonal.reshape(split)
    norms = from_all(square, ("sec", "sub"))
    start = functools.partial(start_kernel, entries, len(norms), places)
    vector, keep, send = images(start, away, True, "remote_images", lists, wavefunction, *norms, left, right)
    ritz_list = []
    for turn_index in range(ITERS):
        remote = add(keep, shift(send, "sub", 1))
        arrived = [shift(remote[(r - 1) * blocks : r * blocks], "sec", r) for r in range(1, secs)]
        own = functools.partial(own_kernel, places)
        keep, send = images(own, blocks, False, "own_images", lists, vector, left, right)
        parts = [keep, shift(send, "sub", 1), *arrived]
        held = vector.reshape(split)
        pieces, inner = combine(held, split_diagonal, [part.reshape(split) for part in parts])
        inner = add(*from_all(inner, ("sec", "sub")))
        thetas = from_all(inner, "op")
        landed = [shift(pieces[k], "op", k) for k in range(1, ops)]
        correction, sums, ritz = correct(entries, thetas, held, split_diagonal, [pieces[0], *landed])
        ritz_list.append(ritz[0, 0])
        sums = add(*from_all(sums, ("sec", "sub")))
        sums = from_all(sums, "op")
        spread = from_all(correction, "op")
        if turn_index < ITERS - 1:
            resume = functools.partial(resume_kernel, entries, len(sums), ops, places)
            vector, keep, send = images(
                resume, away, True, "remote_images", lists, vector, *sums, *spread, left, right
            )
        else:
            vector = finish(entries, vector, sums, spread)
    return (vector, jnp.stack(ritz_list))


def solution(mesh):
    placed = (
        P(("grp", "sec"), None, "sub"),
        P(("grp", "sec"), None, "sub"),
        P(("grp", "op"), "sec", None, None),
        P(("grp", "op"), "sec", "sub", None),
        P(("grp", "op"), "sec"),
    )
    return jax.shard_map(
        per_device,
        mesh=mesh,
        in_specs=placed,
        out_specs=(P(("grp", "sec"), None, "sub"), P("grp")),
        check_vma=False,
    )
```

time: 315 us -> 151 us (0.48)
  blocking collectives: 137 us -> 0 us
  Pallas kernels: 97.9 us -> 28 us
  starting transfers between devices: 15 us -> 51 us
  waiting for transfers between devices: 27.7 us -> 53.2 us
  local copies, waits for them, and re-layouts: 30.5 us -> 15.6 us
    psum x5 -> x0, blocking collectives: 137 us -> none  [the longest x2 65.3 us: per_device(): theta_sum = lax.psum(inner, ('op', 'sec', 'sub'))]
    pallas_call x11 -> x14, Pallas kernels: 92.8 us -> 27.4 us  [the longest x4 20.4 us: images(): pl.pallas_call(kernel, out_shape=out, in_specs=[SMEM] + [VMEM] * len(oper...]
    ppermute x18 -> x45, starting transfers between devices: 15 us -> 51 us  [shift(): lax.ppermute(array, axis, [(i, (i + turn) % count) for i in range(count)])]
    ppermute x18 -> x45, waiting for transfers between devices: 27.7 us -> 53.2 us  [shift(): lax.ppermute(array, axis, [(i, (i + turn) % count) for i in range(count)])]
    unnamed x73 -> x15, local copies, waits for them, and re-layouts: 30.5 us -> 14.6 us
    pallas_call x2, Pallas kernels: 5.12 us -> 0.58 us  [combine(): pl.pallas_call(functools.partial(combine_kernel, len(parts)), out_shape=(...]
  transfers between devices with their start and end apart: 18 -> 45, of which waited for: 2 -> 24; matrix products, arithmetic and copies ran while one was open for 0% -> 2% of each run, Pallas kernels for 19% -> 10%
where the time goes in v2:
time: 151 us; the launch traced here: 150 us
  waiting for transfers between devices  53.2 us (35%)
  starting transfers between devices  51 us (34%)
  Pallas kernels  28 us (19%)
  local copies, waits for them, and re-layouts  15.6 us (10%)
  other arithmetic  1.78 us (1%)
    ppermute x45, waiting for transfers between devices, shift(): lax.ppermute(array, axis, [(i, (i + turn) % count) for i in range(count)])  53.2 us
    ppermute x45, starting transfers between devices, shift(): lax.ppermute(array, axis, [(i, (i + turn) % count) for i in range(count)])  51 us
    pallas_call x4, Pallas kernels, images(): pl.pallas_call(kernel, out_shape=out, in_specs=[SMEM] + [VMEM] * len(oper...  20.4 us
    unnamed x15, local copies, waits for them, and re-layouts  14.6 us
    pallas_call x1, Pallas kernels, plan(): pl.pallas_call(functools.partial(plan_kernel, secs, places), out_shape=(j...  5.39 us
  transfers between devices with their start and end apart: 45, of which 24 were waited for; matrix products, arithmetic and copies ran while one was open for 2% of the time, Pallas kernels for 10%

profile of v2, /device:TPU:0, one launch (start us, length us, event | category | flops | bytes accessed | tf_op | source)
XLA Modules:
  0.0 150.4 jit_solution(10830768049209541111)
XLA Ops:
  2.4 5.4 %plan.1 = (s32[754]{0:T(1024)S(1)}, f32[8,128]{1,0:T(8,128)S(1)}) custom-call(s32[24,4]{1,0:T(8,128)S(1)} %copy.7.targets, f32[4,256,128]{2,1,0:T(8,128)S(1)} %copy-done.5), custom_call_target="tpu_custom_call" | custom-call | tf_op jit(solution)/shard_map/plan/pallas_call | solution.py:104
  7.8 2.4 %collective-permute-start.2 = (f32[8,128]{1,0:T(8,128)S(1)}, f32[8,128]{1,0:T(8,128)S(1)}, u32[]{:S(2)}, u32[]{:S(2)}) collective-permute-start(f32[8,128]{1,0:T(8,128)S(1)} %get-tuple-element.31.refs_0_), channel_id=1, source_target_pairs={{0,3},{1,0},{2,1},{3,2},{4,7},{5,4},{6,5},{7,6},{8,11},{9,8},{10,9... | collective-permute-start | bytes 12296 | tf_op jit(solution)/shard_map/ppermute | solution.py:324
  11.6 2.3 %collective-permute-done.1.refs_2_ = f32[8,128]{1,0:T(8,128)S(1)} collective-permute-done((f32[8,128]{1,0:T(8,128)S(1)}, f32[8,128]{1,0:T(8,128)S(1)}, u32[]{:S(2)}, u32[]{:S(2)}) %collective-permute-start.1) | collective-permute-done | bytes 4128 | tf_op jit(solution)/shard_map/ppermute | solution.py:324
  13.9 4.6 %copy-done = bf16[24,4,256,256]{3,2,1,0:T(8,128)(2,1)S(1)} copy-done((bf16[24,4,256,256]{3,2,1,0:T(8,128)(2,1)S(1)}, bf16[24,4,256,256]{3,2,1,0:T(8,128)(2,1)}, u32[]{:S(2)}) %copy-start) | copy-done | bytes 12582936
  18.5 2.8 %copy-done.2 = bf16[24,4,128,256]{3,2,1,0:T(8,128)(2,1)S(1)} copy-done((bf16[24,4,128,256]{3,2,1,0:T(8,128)(2,1)S(1)}, bf16[24,4,128,256]{3,2,1,0:T(8,128)(2,1)}, u32[]{:S(2)}) %copy-start.2) | copy-done | bytes 6291480
  22.3 2.8 %remote_images.2 = (f32[4,256,128]{2,1,0:T(8,128)S(1)}, f32[4,256,128]{2,1,0:T(8,128)S(1)}, f32[4,256,128]{2,1,0:T(8,128)S(1)}) custom-call(s32[754]{0:T(1024)S(1)} %get-tuple-element.30.lists, f32[4,256,128]{2,1,0:T(8,128)S(1)} %copy-done.6, f32[8,128]{1,0:T(8,128)S(1)} %get-tuple-element.31.refs_0_, f32[8,128]{1,0:T(8,128)S(1)} %collective-permute-done.refs_1_, ...), custom_call_target="tpu_custom_call" | custom-call | flops 1000000000 | bytes 9437184 | tf_op jit(solution)/shard_map/remote_images/pallas_call | solution.py:218
  25.2 1.7 %copy-done.1 = bf16[24,4,256,256]{3,2,1,0:T(8,128)(2,1)S(1)} copy-done((bf16[24,4,256,256]{3,2,1,0:T(8,128)(2,1)S(1)}, bf16[24,4,256,256]{3,2,1,0:T(8,128)(2,1)}, u32[]{:S(2)}) %copy-start.1) | copy-done | bytes 12582936
  26.9 2.8 %copy-done.3 = bf16[24,4,128,256]{3,2,1,0:T(8,128)(2,1)S(1)} copy-done((bf16[24,4,128,256]{3,2,1,0:T(8,128)(2,1)S(1)}, bf16[24,4,128,256]{3,2,1,0:T(8,128)(2,1)}, u32[]{:S(2)}) %copy-start.3) | copy-done | bytes 6291480
  29.7 7.4 %own_images.2 = (f32[4,256,128]{2,1,0:T(8,128)S(1)}, f32[4,256,128]{2,1,0:T(8,128)S(1)}) custom-call(s32[754]{0:T(1024)S(1)} %get-tuple-element.30.lists, f32[4,256,128]{2,1,0:T(8,128)S(1)} %get-tuple-element.32.vector.held, bf16[96,256,256]{2,1,0:T(8,128)(2,1)S(1)} %bitcast.5, bf16[96,128,256]{2,1,0:T(8,128)(2,1)S(1)} %bitcast.9), custom_call_target="tpu_custom_call" | custom-call | flops 1000000000 | bytes 9437184 | tf_op jit(solution)/shard_map/own_images/pallas_call | solution.py:218
  39.0 12.6 %collective-permute-done.5.refs_2_ = f32[4,256,128]{2,1,0:T(8,128)S(1)} collective-permute-done((f32[4,256,128]{2,1,0:T(8,128)S(1)}, f32[4,256,128]{2,1,0:T(8,128)S(1)}, u32[]{:S(2)}, u32[]{:S(2)}) %collective-permute-start.5) | collective-permute-done | bytes 524320 | tf_op jit(solution)/shard_map/ppermute | solution.py:324
  52.8 2.6 %collective-permute-start.13 = (f32[256,128]{1,0:T(8,128)S(1)}, f32[256,128]{1,0:T(8,128)S(1)}, u32[]{:S(2)}, u32[]{:S(2)}) collective-permute-start(f32[256,128]{1,0:T(8,128)S(1)} %get-tuple-element.40), channel_id=1, source_target_pairs={{0,8},{4,12},{8,0},{12,4},{1,9},{5,13},{9,1},{13,5},{2,10},{6,14},... | collective-permute-start | bytes 393224 | tf_op jit(solution)/shard_map/ppermute | solution.py:324
  58.8 1.7 %collective-permute-start.6 = (f32[8,128]{1,0:T(8,128)S(1)}, f32[8,128]{1,0:T(8,128)S(1)}, u32[]{:S(2)}, u32[]{:S(2)}) collective-permute-start(f32[8,128]{1,0:T(8,128)S(1)} %get-tuple-element.37.refs_0_), channel_id=1, source_target_pairs={{0,1},{1,2},{2,3},{3,0},{4,5},{5,6},{6,7},{7,4},{8,9},{9,10},{10,1... | collective-permute-start | bytes 12296 | tf_op jit(solution)/shard_map/ppermute | solution.py:324
  63.4 2.2 %collective-permute-done.11.refs_3_ = f32[8,128]{1,0:T(8,128)S(1)} collective-permute-done((f32[8,128]{1,0:T(8,128)S(1)}, f32[8,128]{1,0:T(8,128)S(1)}, u32[]{:S(2)}, u32[]{:S(2)}) %collective-permute-start.11) | collective-permute-done | bytes 4128 | tf_op jit(solution)/shard_map/ppermute | solution.py:324
  65.5 2.2 %collective-permute-start.9 = (f32[8,128]{1,0:T(8,128)S(1)}, f32[8,128]{1,0:T(8,128)S(1)}, u32[]{:S(2)}, u32[]{:S(2)}) collective-permute-start(f32[8,128]{1,0:T(8,128)S(1)} %add.7.refs_0_), channel_id=1, source_target_pairs={{0,4},{4,8},{8,12},{12,0},{1,5},{5,9},{9,13},{13,1},{2,6},{6,10},{... | collective-permute-start | bytes 12296 | tf_op jit(solution)/shard_map/ppermute | solution.py:324
  67.7 3.2 %collective-permute-done.9.refs_1_ = f32[8,128]{1,0:T(8,128)S(1)} collective-permute-done((f32[8,128]{1,0:T(8,128)S(1)}, f32[8,128]{1,0:T(8,128)S(1)}, u32[]{:S(2)}, u32[]{:S(2)}) %collective-permute-start.9) | collective-permute-done | bytes 4128 | tf_op jit(solution)/shard_map/ppermute | solution.py:324
  74.9 1.7 %collective-permute-start.15 = (f32[8,128]{1,0:T(8,128)S(1)}, f32[8,128]{1,0:T(8,128)S(1)}, u32[]{:S(2)}, u32[]{:S(2)}) collective-permute-start(f32[8,128]{1,0:T(8,128)S(1)} %get-tuple-element.42.refs_0_), channel_id=1, source_target_pairs={{0,1},{1,2},{2,3},{3,0},{4,5},{5,6},{6,7},{7,4},{8,9},{9,10},{10,1... | collective-permute-start | bytes 12296 | tf_op jit(solution)/shard_map/ppermute | solution.py:324
  77.9 3.6 %collective-permute-start.20 = (f32[8,128]{1,0:T(8,128)S(1)}, f32[8,128]{1,0:T(8,128)S(1)}, u32[]{:S(2)}, u32[]{:S(2)}) collective-permute-start(f32[8,128]{1,0:T(8,128)S(1)} %add.8.refs_0_), channel_id=1, source_target_pairs={{0,12},{4,0},{8,4},{12,8},{1,13},{5,1},{9,5},{13,9},{2,14},{6,2},{... | collective-permute-start | bytes 12296 | tf_op jit(solution)/shard_map/ppermute | solution.py:324
  84.1 2.0 %collective-permute-done.19.refs_2_ = f32[8,128]{1,0:T(8,128)S(1)} collective-permute-done((f32[8,128]{1,0:T(8,128)S(1)}, f32[8,128]{1,0:T(8,128)S(1)}, u32[]{:S(2)}, u32[]{:S(2)}) %collective-permute-start.19) | collective-permute-done | bytes 4128 | tf_op jit(solution)/shard_map/ppermute | solution.py:324
  86.1 2.5 %collective-permute-done.18.refs_1_ = f32[8,128]{1,0:T(8,128)S(1)} collective-permute-done((f32[8,128]{1,0:T(8,128)S(1)}, f32[8,128]{1,0:T(8,128)S(1)}, u32[]{:S(2)}, u32[]{:S(2)}) %collective-permute-start.18) | collective-permute-done | bytes 4128 | tf_op jit(solution)/shard_map/ppermute | solution.py:324
  88.6 2.9 %remote_images.3 = (f32[4,256,128]{2,1,0:T(8,128)S(1)}, f32[4,256,128]{2,1,0:T(8,128)S(1)}, f32[4,256,128]{2,1,0:T(8,128)S(1)}) custom-call(s32[754]{0:T(1024)S(1)} %get-tuple-element.30.lists, f32[4,256,128]{2,1,0:T(8,128)S(1)} %get-tuple-element.32.vector.held, f32[8,128]{1,0:T(8,128)S(1)} %add.8.refs_0_, f32[8,128]{1,0:T(8,128)S(1)} %collective-permute-done.18.refs_1_, ...), custom_call_target="tpu_custom_call" | custom-call | flops 1000000000 | bytes 9437184 | tf_op jit(solution)/shard_map/remote_images/pallas_call | solution.py:218
  91.5 7.4 %own_images.3 = (f32[4,256,128]{2,1,0:T(8,128)S(1)}, f32[4,256,128]{2,1,0:T(8,128)S(1)}) custom-call(s32[754]{0:T(1024)S(1)} %get-tuple-element.30.lists, f32[4,256,128]{2,1,0:T(8,128)S(1)} %get-tuple-element.44.vector.held, bf16[96,256,256]{2,1,0:T(8,128)(2,1)S(1)} %bitcast.7, bf16[96,128,256]{2,1,0:T(8,128)(2,1)S(1)} %bitcast.11), custom_call_target="tpu_custom_call" | custom-call | flops 1000000000 | bytes 9437184 | tf_op jit(solution)/shard_map/own_images/pallas_call | solution.py:218
  101.0 12.4 %collective-permute-done.26.refs_2_ = f32[4,256,128]{2,1,0:T(8,128)S(1)} collective-permute-done((f32[4,256,128]{2,1,0:T(8,128)S(1)}, f32[4,256,128]{2,1,0:T(8,128)S(1)}, u32[]{:S(2)}, u32[]{:S(2)}) %collective-permute-start.26) | collective-permute-done | bytes 524320 | tf_op jit(solution)/shard_map/ppermute | solution.py:324
  113.8 1.9 %collective-permute-start.34 = (f32[256,128]{1,0:T(8,128)S(1)}, f32[256,128]{1,0:T(8,128)S(1)}, u32[]{:S(2)}, u32[]{:S(2)}) collective-permute-start(f32[256,128]{1,0:T(8,128)S(1)} %get-tuple-element.52), channel_id=1, source_target_pairs={{0,8},{4,12},{8,0},{12,4},{1,9},{5,13},{9,1},{13,5},{2,10},{6,14},... | collective-permute-start | bytes 393224 | tf_op jit(solution)/shard_map/ppermute | solution.py:324
  115.7 1.9 %collective-permute-start.35 = (f32[256,128]{1,0:T(8,128)S(1)}, f32[256,128]{1,0:T(8,128)S(1)}, u32[]{:S(2)}, u32[]{:S(2)}) collective-permute-start(f32[256,128]{1,0:T(8,128)S(1)} %get-tuple-element.53), channel_id=1, source_target_pairs={{0,12},{4,0},{8,4},{12,8},{1,13},{5,1},{9,5},{13,9},{2,14},{6,2},{... | collective-permute-start | bytes 393224 | tf_op jit(solution)/shard_map/ppermute | solution.py:324
  119.1 1.7 %collective-permute-start.27 = (f32[8,128]{1,0:T(8,128)S(1)}, f32[8,128]{1,0:T(8,128)S(1)}, u32[]{:S(2)}, u32[]{:S(2)}) collective-permute-start(f32[8,128]{1,0:T(8,128)S(1)} %get-tuple-element.49.refs_0_), channel_id=1, source_target_pairs={{0,1},{1,2},{2,3},{3,0},{4,5},{5,6},{6,7},{7,4},{8,9},{9,10},{10,1... | collective-permute-start | bytes 12296 | tf_op jit(solution)/shard_map/ppermute | solution.py:324
  125.9 2.6 %collective-permute-start.30 = (f32[8,128]{1,0:T(8,128)S(1)}, f32[8,128]{1,0:T(8,128)S(1)}, u32[]{:S(2)}, u32[]{:S(2)}) collective-permute-start(f32[8,128]{1,0:T(8,128)S(1)} %add.10.refs_0_), channel_id=1, source_target_pairs={{0,4},{4,8},{8,12},{12,0},{1,5},{5,9},{9,13},{13,1},{2,6},{6,10},{... | collective-permute-start | bytes 12296 | tf_op jit(solution)/shard_map/ppermute | solution.py:324
  128.5 2.8 %collective-permute-done.30.refs_1_ = f32[8,128]{1,0:T(8,128)S(1)} collective-permute-done((f32[8,128]{1,0:T(8,128)S(1)}, f32[8,128]{1,0:T(8,128)S(1)}, u32[]{:S(2)}, u32[]{:S(2)}) %collective-permute-start.30) | collective-permute-done | bytes 4128 | tf_op jit(solution)/shard_map/ppermute | solution.py:324
  132.1 1.8 %collective-permute-start.43 = (f32[256,128]{1,0:T(8,128)S(1)}, f32[256,128]{1,0:T(8,128)S(1)}, u32[]{:S(2)}, u32[]{:S(2)}) collective-permute-start(f32[256,128]{1,0:T(8,128)S(1)} %get-tuple-element.55.refs_4_), channel_id=1, source_target_pairs={{0,8},{4,12},{8,0},{12,4},{1,9},{5,13},{9,1},{13,5},{2,10},{6,14},... | collective-permute-start | bytes 393224 | tf_op jit(solution)/shard_map/ppermute | solution.py:324
  135.4 1.7 %collective-permute-start.36 = (f32[8,128]{1,0:T(8,128)S(1)}, f32[8,128]{1,0:T(8,128)S(1)}, u32[]{:S(2)}, u32[]{:S(2)}) collective-permute-start(f32[8,128]{1,0:T(8,128)S(1)} %get-tuple-element.54.refs_0_), channel_id=1, source_target_pairs={{0,1},{1,2},{2,3},{3,0},{4,5},{5,6},{6,7},{7,4},{8,9},{9,10},{10,1... | collective-permute-start | bytes 12296 | tf_op jit(solution)/shard_map/ppermute | solution.py:324
  138.6 3.8 %collective-permute-start.41 = (f32[8,128]{1,0:T(8,128)S(1)}, f32[8,128]{1,0:T(8,128)S(1)}, u32[]{:S(2)}, u32[]{:S(2)}) collective-permute-start(f32[8,128]{1,0:T(8,128)S(1)} %add.11.refs_0_), channel_id=1, source_target_pairs={{0,12},{4,0},{8,4},{12,8},{1,13},{5,1},{9,5},{13,9},{2,14},{6,2},{... | collective-permute-start | bytes 12296 | tf_op jit(solution)/shard_map/ppermute | solution.py:324
  144.3 1.8 %pad_maximum_fusion = f32[2]{0:T(128)} fusion(f32[1]{0:T(128)} %bitcast.3, f32[1]{0:T(128)} %bitcast.2), kind=kLoop, calls=%fused_computation | loop fusion | flops 2 | bytes 16 | tf_op jit(solution)/shard_map/stack | solution.py:370
  146.1 1.8 %collective-permute-done.40.refs_2_ = f32[8,128]{1,0:T(8,128)S(1)} collective-permute-done((f32[8,128]{1,0:T(8,128)S(1)}, f32[8,128]{1,0:T(8,128)S(1)}, u32[]{:S(2)}, u32[]{:S(2)}) %collective-permute-start.40) | collective-permute-done | bytes 4128 | tf_op jit(solution)/shard_map/ppermute | solution.py:324
  (92 shorter events, 38.8 us)
Async XLA Ops:
  7.8 3.8 %collective-permute-start.2 = (f32[8,128]{1,0:T(8,128)S(1)}, f32[8,128]{1,0:T(8,128)S(1)}, u32[]{:S(2)}, u32[]{:S(2)}) collective-permute-start(f32[8,128]{1,0:T(8,128)S(1)} %get-tuple-element.31.refs_0_), channel_id=1, source_target_pairs={{0,3},{1,0},{2,1},{3,2},{4,7},{5,4},{6,5},{7,6},{8,11},{9,8},{10,9... | collective-permute-start | bytes 12296 | tf_op jit(solution)/shard_map/ppermute | solution.py:324
  10.2 3.6 %collective-permute-start.1 = (f32[8,128]{1,0:T(8,128)S(1)}, f32[8,128]{1,0:T(8,128)S(1)}, u32[]{:S(2)}, u32[]{:S(2)}) collective-permute-start(f32[8,128]{1,0:T(8,128)S(1)} %get-tuple-element.31.refs_0_), channel_id=1, source_target_pairs={{0,2},{1,3},{2,0},{3,1},{4,6},{5,7},{6,4},{7,5},{8,10},{9,11},{10,... | collective-permute-start | bytes 12296 | tf_op jit(solution)/shard_map/ppermute | solution.py:324
  25.2 12.0 %collective-permute-start.4 = (f32[4,256,128]{2,1,0:T(8,128)S(1)}, f32[4,256,128]{2,1,0:T(8,128)S(1)}, u32[]{:S(2)}, u32[]{:S(2)}) collective-permute-start(f32[4,256,128]{2,1,0:T(8,128)S(1)} %get-tuple-element.36), channel_id=1, source_target_pairs={{0,1},{1,0},{2,3},{3,2},{4,5},{5,4},{6,7},{7,6},{8,9},{9,8},{10,11... | collective-permute-start | bytes 1572872 | tf_op jit(solution)/shard_map/ppermute | solution.py:324
  37.2 14.4 %collective-permute-start.5 = (f32[4,256,128]{2,1,0:T(8,128)S(1)}, f32[4,256,128]{2,1,0:T(8,128)S(1)}, u32[]{:S(2)}, u32[]{:S(2)}) collective-permute-start(f32[4,256,128]{2,1,0:T(8,128)S(1)} %add.6), channel_id=1, source_target_pairs={{0,2},{2,0},{1,3},{3,1},{4,6},{6,4},{5,7},{7,5},{8,10},{10,8},{9,1... | collective-permute-start | bytes 1572872 | tf_op jit(solution)/shard_map/ppermute | solution.py:324
  51.9 19.1 %collective-permute-start.12 = (f32[256,128]{1,0:T(8,128)S(1)}, f32[256,128]{1,0:T(8,128)S(1)}, u32[]{:S(2)}, u32[]{:S(2)}) collective-permute-start(f32[256,128]{1,0:T(8,128)S(1)} %get-tuple-element.39), channel_id=1, source_target_pairs={{0,4},{4,8},{8,12},{12,0},{1,5},{5,9},{9,13},{13,1},{2,6},{6,10},{... | collective-permute-start | bytes 393224 | tf_op jit(solution)/shard_map/ppermute | solution.py:324
  52.8 18.1 %collective-permute-start.13 = (f32[256,128]{1,0:T(8,128)S(1)}, f32[256,128]{1,0:T(8,128)S(1)}, u32[]{:S(2)}, u32[]{:S(2)}) collective-permute-start(f32[256,128]{1,0:T(8,128)S(1)} %get-tuple-element.40), channel_id=1, source_target_pairs={{0,8},{4,12},{8,0},{12,4},{1,9},{5,13},{9,1},{13,5},{2,10},{6,14},... | collective-permute-start | bytes 393224 | tf_op jit(solution)/shard_map/ppermute | solution.py:324
  55.4 15.5 %collective-permute-start.14 = (f32[256,128]{1,0:T(8,128)S(1)}, f32[256,128]{1,0:T(8,128)S(1)}, u32[]{:S(2)}, u32[]{:S(2)}) collective-permute-start(f32[256,128]{1,0:T(8,128)S(1)} %get-tuple-element.41), channel_id=1, source_target_pairs={{0,12},{4,0},{8,4},{12,8},{1,13},{5,1},{9,5},{13,9},{2,14},{6,2},{... | collective-permute-start | bytes 393224 | tf_op jit(solution)/shard_map/ppermute | solution.py:324
  57.3 3.6 %collective-permute-start.7 = (f32[8,128]{1,0:T(8,128)S(1)}, f32[8,128]{1,0:T(8,128)S(1)}, u32[]{:S(2)}, u32[]{:S(2)}) collective-permute-start(f32[8,128]{1,0:T(8,128)S(1)} %get-tuple-element.37.refs_0_), channel_id=1, source_target_pairs={{0,2},{1,3},{2,0},{3,1},{4,6},{5,7},{6,4},{7,5},{8,10},{9,11},{10,... | collective-permute-start | bytes 12296 | tf_op jit(solution)/shard_map/ppermute | solution.py:324
  61.9 3.6 %collective-permute-start.11 = (f32[8,128]{1,0:T(8,128)S(1)}, f32[8,128]{1,0:T(8,128)S(1)}, u32[]{:S(2)}, u32[]{:S(2)}) collective-permute-start(f32[8,128]{1,0:T(8,128)S(1)} %add.7.refs_0_), channel_id=1, source_target_pairs={{0,12},{4,0},{8,4},{12,8},{1,13},{5,1},{9,5},{13,9},{2,14},{6,2},{... | collective-permute-start | bytes 12296 | tf_op jit(solution)/shard_map/ppermute | solution.py:324
  62.2 5.5 %collective-permute-start.10 = (f32[8,128]{1,0:T(8,128)S(1)}, f32[8,128]{1,0:T(8,128)S(1)}, u32[]{:S(2)}, u32[]{:S(2)}) collective-permute-start(f32[8,128]{1,0:T(8,128)S(1)} %add.7.refs_0_), channel_id=1, source_target_pairs={{0,8},{4,12},{8,0},{12,4},{1,9},{5,13},{9,1},{13,5},{2,10},{6,14},... | collective-permute-start | bytes 12296 | tf_op jit(solution)/shard_map/ppermute | solution.py:324
  65.5 5.4 %collective-permute-start.9 = (f32[8,128]{1,0:T(8,128)S(1)}, f32[8,128]{1,0:T(8,128)S(1)}, u32[]{:S(2)}, u32[]{:S(2)}) collective-permute-start(f32[8,128]{1,0:T(8,128)S(1)} %add.7.refs_0_), channel_id=1, source_target_pairs={{0,4},{4,8},{8,12},{12,0},{1,5},{5,9},{9,13},{13,1},{2,6},{6,10},{... | collective-permute-start | bytes 12296 | tf_op jit(solution)/shard_map/ppermute | solution.py:324
  71.2 17.4 %collective-permute-start.23 = (f32[256,128]{1,0:T(8,128)S(1)}, f32[256,128]{1,0:T(8,128)S(1)}, u32[]{:S(2)}, u32[]{:S(2)}) collective-permute-start(f32[256,128]{1,0:T(8,128)S(1)} %get-tuple-element.43.refs_4_), channel_id=1, source_target_pairs={{0,12},{4,0},{8,4},{12,8},{1,13},{5,1},{9,5},{13,9},{2,14},{6,2},{... | collective-permute-start | bytes 393224 | tf_op jit(solution)/shard_map/ppermute | solution.py:324
  71.6 17.0 %collective-permute-start.22 = (f32[256,128]{1,0:T(8,128)S(1)}, f32[256,128]{1,0:T(8,128)S(1)}, u32[]{:S(2)}, u32[]{:S(2)}) collective-permute-start(f32[256,128]{1,0:T(8,128)S(1)} %get-tuple-element.43.refs_4_), channel_id=1, source_target_pairs={{0,8},{4,12},{8,0},{12,4},{1,9},{5,13},{9,1},{13,5},{2,10},{6,14},... | collective-permute-start | bytes 393224 | tf_op jit(solution)/shard_map/ppermute | solution.py:324
  73.1 15.5 %collective-permute-start.21 = (f32[256,128]{1,0:T(8,128)S(1)}, f32[256,128]{1,0:T(8,128)S(1)}, u32[]{:S(2)}, u32[]{:S(2)}) collective-permute-start(f32[256,128]{1,0:T(8,128)S(1)} %get-tuple-element.43.refs_4_), channel_id=1, source_target_pairs={{0,4},{4,8},{8,12},{12,0},{1,5},{5,9},{9,13},{13,1},{2,6},{6,10},{... | collective-permute-start | bytes 393224 | tf_op jit(solution)/shard_map/ppermute | solution.py:324
  73.3 3.6 %collective-permute-start.16 = (f32[8,128]{1,0:T(8,128)S(1)}, f32[8,128]{1,0:T(8,128)S(1)}, u32[]{:S(2)}, u32[]{:S(2)}) collective-permute-start(f32[8,128]{1,0:T(8,128)S(1)} %get-tuple-element.42.refs_0_), channel_id=1, source_target_pairs={{0,2},{1,3},{2,0},{3,1},{4,6},{5,7},{6,4},{7,5},{8,10},{9,11},{10,... | collective-permute-start | bytes 12296 | tf_op jit(solution)/shard_map/ppermute | solution.py:324
  77.9 5.0 %collective-permute-start.20 = (f32[8,128]{1,0:T(8,128)S(1)}, f32[8,128]{1,0:T(8,128)S(1)}, u32[]{:S(2)}, u32[]{:S(2)}) collective-permute-start(f32[8,128]{1,0:T(8,128)S(1)} %add.8.refs_0_), channel_id=1, source_target_pairs={{0,12},{4,0},{8,4},{12,8},{1,13},{5,1},{9,5},{13,9},{2,14},{6,2},{... | collective-permute-start | bytes 12296 | tf_op jit(solution)/shard_map/ppermute | solution.py:324
  81.6 4.5 %collective-permute-start.19 = (f32[8,128]{1,0:T(8,128)S(1)}, f32[8,128]{1,0:T(8,128)S(1)}, u32[]{:S(2)}, u32[]{:S(2)}) collective-permute-start(f32[8,128]{1,0:T(8,128)S(1)} %add.8.refs_0_), channel_id=1, source_target_pairs={{0,8},{4,12},{8,0},{12,4},{1,9},{5,13},{9,1},{13,5},{2,10},{6,14},... | collective-permute-start | bytes 12296 | tf_op jit(solution)/shard_map/ppermute | solution.py:324
  82.9 5.7 %collective-permute-start.18 = (f32[8,128]{1,0:T(8,128)S(1)}, f32[8,128]{1,0:T(8,128)S(1)}, u32[]{:S(2)}, u32[]{:S(2)}) collective-permute-start(f32[8,128]{1,0:T(8,128)S(1)} %add.8.refs_0_), channel_id=1, source_target_pairs={{0,4},{4,8},{8,12},{12,0},{1,5},{5,9},{9,13},{13,1},{2,6},{6,10},{... | collective-permute-start | bytes 12296 | tf_op jit(solution)/shard_map/ppermute | solution.py:324
  91.5 8.0 %collective-permute-start.25 = (f32[4,256,128]{2,1,0:T(8,128)S(1)}, f32[4,256,128]{2,1,0:T(8,128)S(1)}, u32[]{:S(2)}, u32[]{:S(2)}) collective-permute-start(f32[4,256,128]{2,1,0:T(8,128)S(1)} %get-tuple-element.48), channel_id=1, source_target_pairs={{0,1},{1,0},{2,3},{3,2},{4,5},{5,4},{6,7},{7,6},{8,9},{9,8},{10,11... | collective-permute-start | bytes 1572872 | tf_op jit(solution)/shard_map/ppermute | solution.py:324
  99.5 13.9 %collective-permute-start.26 = (f32[4,256,128]{2,1,0:T(8,128)S(1)}, f32[4,256,128]{2,1,0:T(8,128)S(1)}, u32[]{:S(2)}, u32[]{:S(2)}) collective-permute-start(f32[4,256,128]{2,1,0:T(8,128)S(1)} %add.9), channel_id=1, source_target_pairs={{0,2},{2,0},{1,3},{3,1},{4,6},{6,4},{5,7},{7,5},{8,10},{10,8},{9,1... | collective-permute-start | bytes 1572872 | tf_op jit(solution)/shard_map/ppermute | solution.py:324
  113.8 17.6 %collective-permute-start.33 = (f32[256,128]{1,0:T(8,128)S(1)}, f32[256,128]{1,0:T(8,128)S(1)}, u32[]{:S(2)}, u32[]{:S(2)}) collective-permute-start(f32[256,128]{1,0:T(8,128)S(1)} %get-tuple-element.51), channel_id=1, source_target_pairs={{0,4},{4,8},{8,12},{12,0},{1,5},{5,9},{9,13},{13,1},{2,6},{6,10},{... | collective-permute-start | bytes 393224 | tf_op jit(solution)/shard_map/ppermute | solution.py:324
  113.8 17.5 %collective-permute-start.34 = (f32[256,128]{1,0:T(8,128)S(1)}, f32[256,128]{1,0:T(8,128)S(1)}, u32[]{:S(2)}, u32[]{:S(2)}) collective-permute-start(f32[256,128]{1,0:T(8,128)S(1)} %get-tuple-element.52), channel_id=1, source_target_pairs={{0,8},{4,12},{8,0},{12,4},{1,9},{5,13},{9,1},{13,5},{2,10},{6,14},... | collective-permute-start | bytes 393224 | tf_op jit(solution)/shard_map/ppermute | solution.py:324
  115.7 15.6 %collective-permute-start.35 = (f32[256,128]{1,0:T(8,128)S(1)}, f32[256,128]{1,0:T(8,128)S(1)}, u32[]{:S(2)}, u32[]{:S(2)}) collective-permute-start(f32[256,128]{1,0:T(8,128)S(1)} %get-tuple-element.53), channel_id=1, source_target_pairs={{0,12},{4,0},{8,4},{12,8},{1,13},{5,1},{9,5},{13,9},{2,14},{6,2},{... | collective-permute-start | bytes 393224 | tf_op jit(solution)/shard_map/ppermute | solution.py:324
  122.3 3.6 %collective-permute-start.32 = (f32[8,128]{1,0:T(8,128)S(1)}, f32[8,128]{1,0:T(8,128)S(1)}, u32[]{:S(2)}, u32[]{:S(2)}) collective-permute-start(f32[8,128]{1,0:T(8,128)S(1)} %add.10.refs_0_), channel_id=1, source_target_pairs={{0,12},{4,0},{8,4},{12,8},{1,13},{5,1},{9,5},{13,9},{2,14},{6,2},{... | collective-permute-start | bytes 12296 | tf_op jit(solution)/shard_map/ppermute | solution.py:324
  122.8 5.8 %collective-permute-start.31 = (f32[8,128]{1,0:T(8,128)S(1)}, f32[8,128]{1,0:T(8,128)S(1)}, u32[]{:S(2)}, u32[]{:S(2)}) collective-permute-start(f32[8,128]{1,0:T(8,128)S(1)} %add.10.refs_0_), channel_id=1, source_target_pairs={{0,8},{4,12},{8,0},{12,4},{1,9},{5,13},{9,1},{13,5},{2,10},{6,14},... | collective-permute-start | bytes 12296 | tf_op jit(solution)/shard_map/ppermute | solution.py:324
  125.9 5.4 %collective-permute-start.30 = (f32[8,128]{1,0:T(8,128)S(1)}, f32[8,128]{1,0:T(8,128)S(1)}, u32[]{:S(2)}, u32[]{:S(2)}) collective-permute-start(f32[8,128]{1,0:T(8,128)S(1)} %add.10.refs_0_), channel_id=1, source_target_pairs={{0,4},{4,8},{8,12},{12,0},{1,5},{5,9},{9,13},{13,1},{2,6},{6,10},{... | collective-permute-start | bytes 12296 | tf_op jit(solution)/shard_map/ppermute | solution.py:324
  131.6 17.8 %collective-permute-start.44 = (f32[256,128]{1,0:T(8,128)S(1)}, f32[256,128]{1,0:T(8,128)S(1)}, u32[]{:S(2)}, u32[]{:S(2)}) collective-permute-start(f32[256,128]{1,0:T(8,128)S(1)} %get-tuple-element.55.refs_4_), channel_id=1, source_target_pairs={{0,12},{4,0},{8,4},{12,8},{1,13},{5,1},{9,5},{13,9},{2,14},{6,2},{... | collective-permute-start | bytes 393224 | tf_op jit(solution)/shard_map/ppermute | solution.py:324
  132.1 17.3 %collective-permute-start.43 = (f32[256,128]{1,0:T(8,128)S(1)}, f32[256,128]{1,0:T(8,128)S(1)}, u32[]{:S(2)}, u32[]{:S(2)}) collective-permute-start(f32[256,128]{1,0:T(8,128)S(1)} %get-tuple-element.55.refs_4_), channel_id=1, source_target_pairs={{0,8},{4,12},{8,0},{12,4},{1,9},{5,13},{9,1},{13,5},{2,10},{6,14},... | collective-permute-start | bytes 393224 | tf_op jit(solution)/shard_map/ppermute | solution.py:324
  133.9 15.5 %collective-permute-start.42 = (f32[256,128]{1,0:T(8,128)S(1)}, f32[256,128]{1,0:T(8,128)S(1)}, u32[]{:S(2)}, u32[]{:S(2)}) collective-permute-start(f32[256,128]{1,0:T(8,128)S(1)} %get-tuple-element.55.refs_4_), channel_id=1, source_target_pairs={{0,4},{4,8},{8,12},{12,0},{1,5},{5,9},{9,13},{13,1},{2,6},{6,10},{... | collective-permute-start | bytes 393224 | tf_op jit(solution)/shard_map/ppermute | solution.py:324
  138.6 5.1 %collective-permute-start.41 = (f32[8,128]{1,0:T(8,128)S(1)}, f32[8,128]{1,0:T(8,128)S(1)}, u32[]{:S(2)}, u32[]{:S(2)}) collective-permute-start(f32[8,128]{1,0:T(8,128)S(1)} %add.11.refs_0_), channel_id=1, source_target_pairs={{0,12},{4,0},{8,4},{12,8},{1,13},{5,1},{9,5},{13,9},{2,14},{6,2},{... | collective-permute-start | bytes 12296 | tf_op jit(solution)/shard_map/ppermute | solution.py:324
  143.4 4.5 %collective-permute-start.40 = (f32[8,128]{1,0:T(8,128)S(1)}, f32[8,128]{1,0:T(8,128)S(1)}, u32[]{:S(2)}, u32[]{:S(2)}) collective-permute-start(f32[8,128]{1,0:T(8,128)S(1)} %add.11.refs_0_), channel_id=1, source_target_pairs={{0,8},{4,12},{8,0},{12,4},{1,9},{5,13},{9,1},{13,5},{2,10},{6,14},... | collective-permute-start | bytes 12296 | tf_op jit(solution)/shard_map/ppermute | solution.py:324
  143.7 5.7 %collective-permute-start.39 = (f32[8,128]{1,0:T(8,128)S(1)}, f32[8,128]{1,0:T(8,128)S(1)}, u32[]{:S(2)}, u32[]{:S(2)}) collective-permute-start(f32[8,128]{1,0:T(8,128)S(1)} %add.11.refs_0_), channel_id=1, source_target_pairs={{0,4},{4,8},{8,12},{12,0},{1,5},{5,9},{9,13},{13,1},{2,6},{6,10},{... | collective-permute-start | bytes 12296 | tf_op jit(solution)/shard_map/ppermute | solution.py:324
  (20 other events, 79.1 us)

commit v3 on v0

v3 whole, which is shorter than its diff:
```python
import functools

import jax
import jax.numpy as jnp
from jax import lax
from jax.experimental import pallas as pl
from jax.experimental.pallas import tpu as pltpu
from jax.sharding import PartitionSpec as P

ITERS = 2
GROUP = 4
REMOTE, OWN = 0, 1
VMEM = pl.BlockSpec(memory_space=pltpu.VMEM)
SMEM = pl.BlockSpec(memory_space=pltpu.SMEM)
ANY = pl.BlockSpec(memory_space=pl.ANY)


def f32(*shape):
    return jax.ShapeDtypeStruct(shape, jnp.float32)


def limit(mebibytes):
    return pltpu.CompilerParams(vmem_limit_bytes=mebibytes * 2**20)


def list_places(pairs, targets):
    cap = (pairs + targets) // 2 + 2 * GROUP
    cap = -(-cap // GROUP) * GROUP
    slot = 3 * 2 * cap
    groups = slot + 3 * cap
    return cap, slot, groups, groups + 2


def code_unit(blocks):
    return 1 << blocks.bit_length()


def make_plan(secs, places, targets, lists, pending, filled):
    terms, blocks = targets.shape
    total = secs * blocks
    cap, slot, groups, _ = places
    unit = code_unit(blocks)
    my_sec = lax.axis_index("sec")
    for place in range(total + 1):
        pending[place] = -1
    for region in range(3):
        filled[region] = 0

    def put(region, step, first, second, value):
        lists[2 * (region * cap + step)] = first
        lists[2 * (region * cap + step) + 1] = second
        lists[slot + region * cap + step] = value

    def take(term, carry):
        for b in range(blocks):
            target = targets[term, b]
            owner = lax.div(jnp.maximum(target, 0), blocks)
            turn = owner - my_sec
            turn = jnp.where(turn < 0, turn + secs, turn)
            own = turn == 0
            place = turn * blocks + (target - owner * blocks)
            place = jnp.where(target < 0, total, place)
            region = jnp.where(target < 0, 2, jnp.where(own, OWN, REMOTE))
            value = jnp.where(own, place, place - blocks)
            waiting, code, step = pending[place], (term * blocks + b) * unit + b, filled[region]
            put(region, step, waiting, code, value)
            filled[region] = step + jnp.where(waiting >= 0, 1, 0)
            pending[place] = jnp.where(waiting >= 0, -1, code)
        return carry

    lax.fori_loop(0, terms, take, 0)
    for region, span in ((REMOTE, range(blocks, total)), (OWN, range(blocks))):
        step = filled[region]
        for place in span:
            waiting = pending[place]
            put(region, step, jnp.maximum(waiting, 0), blocks, place - span[0])
            step = step + jnp.where(waiting >= 0, 1, 0)
        for extra in range(GROUP):
            put(region, step + extra, blocks, blocks, 0)
        lists[groups + region] = lax.div(step + GROUP - 1, GROUP)


def load_kernel(secs, places, targets, left, right, lists, left_held, right_held, pending, filled, sems):
    shares = sems.shape[1]
    each = left.shape[0] // shares
    copies = []
    for share in range(shares):
        rows = pl.ds(share * each, each)
        copies.append(pltpu.make_async_copy(left.at[rows], left_held.at[rows], sems.at[0, share]))
        copies.append(pltpu.make_async_copy(right.at[rows], right_held.at[rows], sems.at[1, share]))
    for copy in copies:
        copy.start()
    make_plan(secs, places, targets, lists, pending, filled)
    for copy in copies:
        copy.wait()


def load(secs, places, targets, left, right):
    terms, blocks = targets.shape
    return pl.pallas_call(
        functools.partial(load_kernel, secs, places),
        out_shape=(
            jax.ShapeDtypeStruct((places[-1],), jnp.int32),
            pltpu.VMEM(left.shape, left.dtype),
            pltpu.VMEM(right.shape, right.dtype),
        ),
        in_specs=[SMEM, ANY, ANY],
        out_specs=(SMEM, VMEM, VMEM),
        scratch_shapes=[
            pltpu.SMEM((secs * blocks + 1,), jnp.int32),
            pltpu.SMEM((3,), jnp.int32),
            pltpu.SemaphoreType.DMA((2, 6)),
        ],
        compiler_params=limit(2),
        cost_estimate=pl.CostEstimate(flops=0, bytes_accessed=40 * 2**20, transcendentals=0),
        name="load",
    )(
        targets,
        pltpu.with_memory_space_constraint(left, pltpu.HBM),
        pltpu.with_memory_space_constraint(right, pltpu.HBM),
    )


def square_kernel(wave, square):
    square[...] = jnp.full(square.shape, jnp.sum(wave[...] * wave[...]))


def square_sum(wave):
    return pl.pallas_call(
        square_kernel,
        out_shape=f32(8, 128),
        in_specs=[VMEM],
        out_specs=VMEM,
        compiler_params=limit(2),
        name="square_sum",
    )(wave)


def added(refs):
    total = refs[0][...]
    for ref in refs[1:]:
        total = total + ref[...]
    return total


def multiply_terms(region, places, lists, left, right, vector_bf, product, keep, send):
    cap, slot, groups, _ = places
    unit = code_unit(vector_bf.shape[0] - 1)
    my_sub = lax.axis_index("sub")
    half = keep.shape[2]
    count = lists[groups + region]
    keep[...] = jnp.zeros_like(keep)
    send[...] = jnp.zeros_like(send)

    def tile(at):
        return lax.shift_right_logical(lists[at], unit.bit_length() - 1)

    def first(group):
        for k in range(2 * GROUP):
            at = 2 * (region * cap + group * GROUP) + k
            part = jnp.dot(
                left[tile(at)], vector_bf[lists[at] & (unit - 1)], preferred_element_type=jnp.float32
            )
            product[k // 2, :, (k % 2) * half : (k % 2 + 1) * half] = part.astype(jnp.bfloat16)

    def second(group):
        for g in range(GROUP):
            at = region * cap + group * GROUP + g
            pair = jnp.concatenate([right[tile(2 * at)], right[tile(2 * at + 1)]], axis=0)
            image = jnp.dot(product[g], pair, preferred_element_type=jnp.float32)
            low, high = image[:, :half], image[:, half:]
            n = lists[slot + at]
            keep[n] += jnp.where(my_sub == 0, low, high)
            send[n] += jnp.where(my_sub == 0, high, low)

    @pl.when(count > 0)
    def _():
        first(0)

        def turn(group, carry):
            second(group - 1)
            first(group)
            return carry

        lax.fori_loop(1, count, turn, 0)
        second(count - 1)


def round_vector(vector, vector_bf):
    blocks = vector.shape[0]
    vector_bf[:blocks] = vector[...].astype(jnp.bfloat16)
    vector_bf[blocks] = jnp.zeros(vector_bf.shape[1:], jnp.bfloat16)


def start_kernel(entries, norms, places, lists, wave, *refs):
    norm_refs, (left, right, vector, keep, send, vector_bf, product) = refs[:norms], refs[norms:]
    length = jnp.sqrt(added(norm_refs)[:1, :1] / entries)
    vector[...] = wave[...] / length[None]
    round_vector(vector, vector_bf)
    multiply_terms(REMOTE, places, lists, left, right, vector_bf, product, keep, send)


def refined(entries, held, correction, sum_refs):
    sums = added(sum_refs) / entries
    along, square, own = sums[0:1, :1], sums[1:2, :1], sums[2:3, :1]
    length = jnp.sqrt((1.0 + along) * (1.0 + along) * own - 2.0 * (1.0 + along) * along + square)
    return (held[...] - (correction[...] - along[None] * held[...])) / length[None]


def resume_kernel(entries, places, lists, held, correction, *refs):
    sum_refs, (left, right, vector, keep, send, vector_bf, product) = refs[:-7], refs[-7:]
    vector[...] = refined(entries, held, correction, sum_refs)
    round_vector(vector, vector_bf)
    multiply_terms(REMOTE, places, lists, left, right, vector_bf, product, keep, send)


def own_kernel(places, lists, vector, after, left, right, keep, send, vector_bf, product):
    round_vector(vector, vector_bf)
    multiply_terms(OWN, places, lists, left, right, vector_bf, product, keep, send)


def images(kernel, slots, with_vector, name, lists, operands, left, right, after=()):
    half, rows = right.shape[1:]
    vector = operands[0]
    out = (f32(slots, rows, half),) * 2
    if with_vector:
        out = (f32(*vector.shape), *out)
    return pl.pallas_call(
        kernel,
        out_shape=out,
        in_specs=[SMEM] + [VMEM] * len(operands) + [ANY] * len(after) + [VMEM] * 2,
        out_specs=(VMEM,) * len(out),
        scratch_shapes=[
            pltpu.VMEM((vector.shape[0] + 1, rows, half), jnp.bfloat16),
            pltpu.VMEM((GROUP, rows, rows), jnp.bfloat16),
        ],
        compiler_params=limit(12),
        cost_estimate=pl.CostEstimate(flops=6 * 10**9, bytes_accessed=20 * 2**20, transcendentals=0),
        name=name,
    )(
        lists,
        *operands,
        *after,
        pltpu.with_memory_space_constraint(left, pltpu.VMEM),
        pltpu.with_memory_space_constraint(right, pltpu.VMEM),
    )


def call(kernel, out_shape, operands, name, mebibytes=4):
    return pl.pallas_call(
        kernel,
        out_shape=out_shape,
        in_specs=[VMEM] * len(operands),
        out_specs=jax.tree.map(lambda _: VMEM, out_shape),
        compiler_params=limit(mebibytes),
        name=name,
    )(*operands)


def add_kernel(*refs):
    refs[-1][...] = added(refs[:-1])


def add(parts):
    return call(add_kernel, f32(*parts[0].shape), parts, "add")


def part_kernel(aways, keep, landed, *outs):
    wholes, pieces = outs[:aways], outs[aways:]
    ops = len(pieces)
    my_op = lax.axis_index("op")
    for away in range(aways):
        wholes[away][...] = keep[away, 0] + landed[away, 0]
        for turn in range(ops):
            at = lax.rem(my_op + turn, ops)
            pieces[turn][away] = keep[away, 1, at] + landed[away, 1, at]


def part(keep, landed, aways, split):
    _, ops, rows, half = split
    shape = (aways, *split)
    outs = call(
        functools.partial(part_kernel, aways),
        (f32(ops, rows, half),) * aways + (f32(aways, rows, half),) * ops,
        (keep.reshape(shape), landed.reshape(shape)),
        "part",
    )
    return outs[:aways], outs[aways:]


def sum_kernel(parts, *refs):
    for away, out in enumerate(refs[parts:]):
        total = refs[0][away]
        for ref in refs[1:parts]:
            total = total + ref[away]
        out[...] = total


def sum_parts(parts):
    aways, rows, half = parts[0].shape
    return call(functools.partial(sum_kernel, len(parts)), (f32(rows, half),) * aways, parts, "sum_parts")


def combine_kernel(arrived, keep, landed, *refs):
    wholes, outs = refs[:arrived], refs[arrived:]
    ops = len(outs)
    my_op = lax.axis_index("op")
    for turn in range(ops):
        at = lax.rem(my_op + turn, ops)
        total = keep[0, at] + landed[0, at]
        for whole in wholes:
            total = total + whole[at]
        outs[turn][0] = total
        outs[turn][1] = keep[1, at] + landed[1, at]


def combine(keep, landed, wholes, split):
    _, ops, rows, half = split
    return call(
        functools.partial(combine_kernel, len(wholes)),
        (f32(2, rows, half),) * ops,
        (keep.reshape(split), landed.reshape(split), *wholes),
        "combine",
    )


def sigma_kernel(parts, vector, diagonal, *refs):
    pieces, arrived, (sigma, inner) = refs[:parts], refs[parts:-2], refs[-2:]
    my_op = lax.axis_index("op")
    inner_sum = jnp.float32(0)
    for side in range(2):
        total = pieces[0][side]
        for piece in pieces[1:]:
            total = total + piece[side]
        if side == 1:
            total = total + added(arrived)
        held = vector[side, my_op]
        total = diagonal[side, my_op] * held + total
        sigma[side] = total
        inner_sum += jnp.sum(held * total)
    inner[...] = jnp.full(inner.shape, inner_sum)


def sigma_share(vector, diagonal, pieces, arrived):
    _, ops, rows, half = vector.shape
    return call(
        functools.partial(sigma_kernel, len(pieces)),
        (f32(2, rows, half), f32(8, 128)),
        (vector, diagonal, *pieces, *arrived),
        "sigma",
    )


def correct_kernel(entries, ops, vector, diagonal, *refs):
    spread, theta_refs, (correction, sums, ritz) = refs[:ops], refs[ops:-3], refs[-3:]
    my_op = lax.axis_index("op")
    ritz[...] = added(theta_refs) / entries
    theta = ritz[:1, :1]
    totals = [jnp.float32(0)] * 3
    for turn in range(ops):
        at = lax.rem(my_op + ops - turn, ops)
        for side in range(2):
            held, diag = vector[side, at], diagonal[side, at]
            value = (spread[turn][side] - theta * held) / (1.0 + jnp.abs(diag - theta))
            correction[side, at] = value
            for index, term in enumerate((held * value, value * value, held * held)):
                totals[index] += jnp.sum(term)
    sums[...] = jnp.zeros_like(sums)
    for index, value in enumerate(totals):
        sums[index : index + 1] = jnp.full((1, sums.shape[1]), value)


def correct(entries, vector, diagonal, spread, thetas):
    return call(
        functools.partial(correct_kernel, entries, len(spread)),
        (f32(*vector.shape), f32(8, 128), f32(8, 128)),
        (vector, diagonal, *spread, *thetas),
        "correct",
    )


def finish_kernel(entries, sums, held, correction, *refs):
    sum_refs, ritz_refs, (out, ritz) = refs[:sums], refs[sums:-2], refs[-2:]
    out[...] = refined(entries, held, correction, sum_refs)
    for index, ref in enumerate(ritz_refs):
        ritz[index] = ref[0, 0]


def finish(entries, vector, correction, sums, ritz):
    return pl.pallas_call(
        functools.partial(finish_kernel, entries, len(sums)),
        out_shape=(f32(*vector.shape), f32(len(ritz))),
        in_specs=[VMEM] * (2 + len(sums) + len(ritz)),
        out_specs=(VMEM, SMEM),
        compiler_params=limit(4),
        name="finish",
    )(vector, correction, *sums, *ritz)


def shift(array, axis, turn):
    count = lax.axis_size(axis)
    return lax.ppermute(array, axis, [(i, (i + turn) % count) for i in range(count)])


def from_all(array, axis):
    return [array, *[shift(array, axis, k) for k in range(1, lax.axis_size(axis))]]


def per_device(wavefunction, diagonal, left_env, right_env, targets):
    ops, secs = lax.axis_size("op"), lax.axis_size("sec")
    blocks, tile, half = wavefunction.shape
    terms = left_env.shape[0]
    entries = blocks * secs * tile * tile
    left = left_env.reshape(terms * blocks, tile, tile)
    right = right_env.reshape(terms * blocks, half, tile)
    split = (2, ops, blocks * tile // ops // 2, half)
    places = list_places(terms * blocks, secs * blocks)
    aways = secs - 1
    diagonal = diagonal.reshape(split)
    norms = from_all(square_sum(wavefunction), ("sec", "sub"))
    lists, left, right = load(secs, places, targets, left, right)
    start = functools.partial(start_kernel, entries, len(norms), places)
    vector, keep, send = images(
        start, aways * blocks, True, "remote_images", lists, (wavefunction, *norms), left, right
    )
    ritz = []
    for turn_index in range(ITERS):
        wholes, shares = part(keep, shift(send, "sub", 1), aways, split)
        crossed = [shift(wholes[r - 1], "sec", r) for r in range(1, secs)]
        landed = [shift(shares[k], "op", k) for k in range(1, ops)]
        own = functools.partial(own_kernel, places)
        keep, send = images(
            own, blocks, False, "own_images", lists, (vector,), left, right, after=(wholes[0],)
        )
        reduced = sum_parts((shares[0], *landed))
        arrived = [shift(reduced[r - 1], "sec", r) for r in range(1, secs)]
        pieces = combine(keep, shift(send, "sub", 1), crossed, split)
        pieces = [pieces[0], *[shift(pieces[k], "op", k) for k in range(1, ops)]]
        held = vector.reshape(split)
        sigma, inner = sigma_share(held, diagonal, pieces, arrived)
        spread = from_all(sigma, "op")
        thetas = from_all(add(from_all(inner, ("sec", "sub"))), "op")
        correction, sums, theta = correct(entries, held, diagonal, spread, thetas)
        ritz.append(theta)
        sums = from_all(sums, ("sec", "sub"))
        correction = correction.reshape(vector.shape)
        if turn_index < ITERS - 1:
            resume = functools.partial(resume_kernel, entries, places)
            operands = (vector, correction, *sums)
            vector, keep, send = images(
                resume, aways * blocks, True, "remote_images", lists, operands, left, right
            )
    return finish(entries, vector, correction, sums, ritz)


def solution(mesh):
    placed = (
        P(("grp", "sec"), None, "sub"),
        P(("grp", "sec"), None, "sub"),
        P(("grp", "op"), "sec", None, None),
        P(("grp", "op"), "sec", "sub", None),
        P(("grp", "op"), "sec"),
    )
    return jax.shard_map(
        per_device,
        mesh=mesh,
        in_specs=placed,
        out_specs=(P(("grp", "sec"), None, "sub"), P("grp")),
        check_vma=False,
    )
```

time: 434 us -> 132 us (0.30)
  waiting for transfers between devices: 195 us -> 42.5 us
  matrix products: 73.4 us -> 0 us
  other arithmetic: 72.8 us -> 0 us
  starting transfers between devices: 0.08 us -> 55.9 us
  blocking collectives: 48.9 us -> 0 us
  Pallas kernels: 0 us -> 30.8 us
  local copies, waits for them, and re-layouts: 20.8 us -> 1.8 us
  between operations: 18.8 us -> 0.86 us
    psum x2 -> x0, waiting for transfers between devices: 195 us -> none  [per_device(): full_sum = lax.psum(partial_sum, ('op', 'sec', 'sub'))]
    dot_general x48 -> x0, matrix products: 73.4 us -> none  [accumulate(): jnp.einsum('bik,bkhc->bihc', product, right_term, preferred_element_type=...]
    ppermute x0 -> x47, starting transfers between devices: none -> 55.9 us  [shift(): lax.ppermute(array, axis, [(i, (i + turn) % count) for i in range(count)])]
    scatter-add x48 -> x0, other arithmetic: 55.4 us -> none  [accumulate(): return (total.at[slot_row].add(image, mode='drop'), None)]
    psum x7 -> x0, blocking collectives: 48.9 us -> none  [the longest x2 14.2 us: per_device(): along = lax.psum(jnp.sum(vector * correction), ('sec', 'sub')) / entries]
    ppermute x0 -> x47, waiting for transfers between devices: none -> 42.5 us  [shift(): lax.ppermute(array, axis, [(i, (i + turn) % count) for i in range(count)])]
    pallas_call x0 -> x19, Pallas kernels: none -> 30.8 us  [the longest x4 20.2 us: images(): pl.pallas_call(kernel, out_shape=out, in_specs=[SMEM] + [VMEM] * len(oper...]
    reduce_sum x7 -> x0, other arithmetic: 12 us -> none  [the longest x2 3.72 us: per_device(): theta = lax.psum(jnp.sum(vector * sigma), ('sec', 'sub')) / entries]
  transfers between devices with their start and end apart: 2 -> 47, of which waited for: 2 -> 27; matrix products, arithmetic and copies ran while one was open for 0% -> 1% of each run, Pallas kernels for 0% -> 6%
where the time goes in v3:
time: 132 us
  starting transfers between devices  55.9 us (42%)
  waiting for transfers between devices  42.5 us (32%)
  Pallas kernels  30.8 us (23%)
  local copies, waits for them, and re-layouts  1.8 us (1%)
    ppermute x47, starting transfers between devices, shift(): lax.ppermute(array, axis, [(i, (i + turn) % count) for i in range(count)])  55.9 us
    ppermute x47, waiting for transfers between devices, shift(): lax.ppermute(array, axis, [(i, (i + turn) % count) for i in range(count)])  42.5 us
    pallas_call x4, Pallas kernels, images(): pl.pallas_call(kernel, out_shape=out, in_specs=[SMEM] + [VMEM] * len(oper...  20.2 us
    pallas_call x1, Pallas kernels, load(): pl.pallas_call(functools.partial(load_kernel, secs, places), out_shape=(j...  7.84 us
  transfers between devices with their start and end apart: 47, of which 27 were waited for; matrix products, arithmetic and copies ran while one was open for 1% of the time, Pallas kernels for 6%

profile of v3, /device:TPU:0, one launch (start us, length us, event | category | flops | bytes accessed | tf_op | source)
XLA Modules:
  0.0 131.9 jit_solution(1311677537459821)
XLA Ops:
  1.9 2.4 %collective-permute-start.2 = (f32[8,128]{1,0:T(8,128)S(1)}, f32[8,128]{1,0:T(8,128)S(1)}, u32[]{:S(2)}, u32[]{:S(2)}) collective-permute-start(f32[8,128]{1,0:T(8,128)S(1)} %square_sum.1.refs_0_), channel_id=1, source_target_pairs={{0,3},{1,0},{2,1},{3,2},{4,7},{5,4},{6,5},{7,6},{8,11},{9,8},{10,9... | collective-permute-start | bytes 12296 | tf_op jit(solution)/shard_map/ppermute | solution.py:402
  5.9 7.8 %load.1 = (s32[542]{0:T(1024)S(1)}, bf16[96,256,256]{2,1,0:T(8,128)(2,1)S(1)}, bf16[96,128,256]{2,1,0:T(8,128)(2,1)S(1)}) custom-call(s32[24,4]{1,0:T(8,128)S(1)} %copy.7.targets, bf16[96,256,256]{2,1,0:T(8,128)(2,1)} %bitcast.33, bf16[96,128,256]{2,1,0:T(8,128)(2,1)} %bitcast.34), custom_call_target="tpu_custom_call" | custom-call | bytes 41943040 | tf_op jit(solution)/shard_map/load/pallas_call | solution.py:100
  13.8 2.8 %remote_images.2 = (f32[4,256,128]{2,1,0:T(8,128)S(1)}, f32[4,256,128]{2,1,0:T(8,128)S(1)}, f32[4,256,128]{2,1,0:T(8,128)S(1)}) custom-call(s32[542]{0:T(1024)S(1)} %get-tuple-element.43.lists, f32[4,256,128]{2,1,0:T(8,128)S(1)} %copy-done.2, f32[8,128]{1,0:T(8,128)S(1)} %square_sum.1.refs_0_, f32[8,128]{1,0:T(8,128)S(1)} %collective-permute-done.refs_1_, ...), custom_call_target="tpu_custom_call" | custom-call | flops 6000000000 | bytes 20971520 | tf_op jit(solution)/shard_map/remote_images/pallas_call | solution.py:228
  18.0 1.5 %collective-permute-done.3 = f32[4,256,128]{2,1,0:T(8,128)S(1)} collective-permute-done((f32[4,256,128]{2,1,0:T(8,128)S(1)}, f32[4,256,128]{2,1,0:T(8,128)S(1)}, u32[]{:S(2)}, u32[]{:S(2)}) %collective-permute-start.3) | collective-permute-done | bytes 524320 | tf_op jit(solution)/shard_map/ppermute | solution.py:402
  19.6 7.2 %own_images.2 = (f32[4,256,128]{2,1,0:T(8,128)S(1)}, f32[4,256,128]{2,1,0:T(8,128)S(1)}) custom-call(s32[542]{0:T(1024)S(1)} %get-tuple-element.43.lists, f32[4,256,128]{2,1,0:T(8,128)S(1)} %get-tuple-element.46.vector.held, f32[4,128,128]{2,1,0:T(8,128)S(1)} %get-tuple-element.49.after, bf16[96,256,256]{2,1,0:T(8,128)(2,1)S(1)} %get-tuple-element.44.refs_4_.left, ...), custom_call_target="tpu_custom_call" | custom-call | flops 6000000000 | bytes 20971520 | tf_op jit(solution)/shard_map/own_images/pallas_call | solution.py:228
  28.9 2.6 %collective-permute-start.10 = (f32[1,128,128]{2,1,0:T(8,128)S(1)}, f32[1,128,128]{2,1,0:T(8,128)S(1)}, u32[]{:S(2)}, u32[]{:S(2)}) collective-permute-start(f32[1,128,128]{2,1,0:T(8,128)S(1)} %get-tuple-element.58), channel_id=1, source_target_pairs={{0,8},{4,12},{8,0},{12,4},{1,9},{5,13},{9,1},{13,5},{2,10},{6,14},... | collective-permute-start | bytes 196616 | tf_op jit(solution)/shard_map/ppermute | solution.py:402
  32.8 2.8 %collective-permute-done.5.refs_0_ = f32[4,128,128]{2,1,0:T(8,128)S(1)} collective-permute-done((f32[4,128,128]{2,1,0:T(8,128)S(1)}, f32[4,128,128]{2,1,0:T(8,128)S(1)}, u32[]{:S(2)}, u32[]{:S(2)}) %collective-permute-start.5) | collective-permute-done | bytes 262176 | tf_op jit(solution)/shard_map/ppermute | solution.py:402
  35.7 1.6 %collective-permute-start.6 = (f32[2,128,128]{2,1,0:T(8,128)S(1)}, f32[2,128,128]{2,1,0:T(8,128)S(1)}, u32[]{:S(2)}, u32[]{:S(2)}) collective-permute-start(f32[2,128,128]{2,1,0:T(8,128)S(1)} %get-tuple-element.53), channel_id=1, source_target_pairs={{0,4},{4,8},{8,12},{12,0},{1,5},{5,9},{9,13},{13,1},{2,6},{6,10},{... | collective-permute-start | bytes 393224 | tf_op jit(solution)/shard_map/ppermute | solution.py:402
  37.3 2.0 %collective-permute-start.7 = (f32[2,128,128]{2,1,0:T(8,128)S(1)}, f32[2,128,128]{2,1,0:T(8,128)S(1)}, u32[]{:S(2)}, u32[]{:S(2)}) collective-permute-start(f32[2,128,128]{2,1,0:T(8,128)S(1)} %get-tuple-element.54), channel_id=1, source_target_pairs={{0,8},{4,12},{8,0},{12,4},{1,9},{5,13},{9,1},{13,5},{2,10},{6,14},... | collective-permute-start | bytes 393224 | tf_op jit(solution)/shard_map/ppermute | solution.py:402
  39.3 2.0 %collective-permute-start.8 = (f32[2,128,128]{2,1,0:T(8,128)S(1)}, f32[2,128,128]{2,1,0:T(8,128)S(1)}, u32[]{:S(2)}, u32[]{:S(2)}) collective-permute-start(f32[2,128,128]{2,1,0:T(8,128)S(1)} %get-tuple-element.55), channel_id=1, source_target_pairs={{0,12},{4,0},{8,4},{12,8},{1,13},{5,1},{9,5},{13,9},{2,14},{6,2},{... | collective-permute-start | bytes 393224 | tf_op jit(solution)/shard_map/ppermute | solution.py:402
  41.7 4.0 %collective-permute-done.12.refs_4_ = f32[128,128]{1,0:T(8,128)S(1)} collective-permute-done((f32[128,128]{1,0:T(8,128)S(1)}, f32[128,128]{1,0:T(8,128)S(1)}, u32[]{:S(2)}, u32[]{:S(2)}) %collective-permute-start.12) | collective-permute-done | bytes 65568 | tf_op jit(solution)/shard_map/ppermute | solution.py:402
  45.6 2.3 %collective-permute-done.7.refs_2_ = f32[2,128,128]{2,1,0:T(8,128)S(1)} collective-permute-done((f32[2,128,128]{2,1,0:T(8,128)S(1)}, f32[2,128,128]{2,1,0:T(8,128)S(1)}, u32[]{:S(2)}, u32[]{:S(2)}) %collective-permute-start.7) | collective-permute-done | bytes 131104 | tf_op jit(solution)/shard_map/ppermute | solution.py:402
  48.2 4.5 %collective-permute-start.15 = (f32[2,128,128]{2,1,0:T(8,128)S(1)}, f32[2,128,128]{2,1,0:T(8,128)S(1)}, u32[]{:S(2)}, u32[]{:S(2)}) collective-permute-start(f32[2,128,128]{2,1,0:T(8,128)S(1)} %get-tuple-element.60.refs_0_), channel_id=1, source_target_pairs={{0,12},{4,0},{8,4},{12,8},{1,13},{5,1},{9,5},{13,9},{2,14},{6,2},{... | collective-permute-start | bytes 393224 | tf_op jit(solution)/shard_map/ppermute | solution.py:402
  57.6 3.8 %collective-permute-start.21 = (f32[8,128]{1,0:T(8,128)S(1)}, f32[8,128]{1,0:T(8,128)S(1)}, u32[]{:S(2)}, u32[]{:S(2)}) collective-permute-start(f32[8,128]{1,0:T(8,128)S(1)} %add.2.refs_4_), channel_id=1, source_target_pairs={{0,12},{4,0},{8,4},{12,8},{1,13},{5,1},{9,5},{13,9},{2,14},{6,2},{... | collective-permute-start | bytes 12296 | tf_op jit(solution)/shard_map/ppermute | solution.py:402
  62.7 2.8 %collective-permute-start.19 = (f32[8,128]{1,0:T(8,128)S(1)}, f32[8,128]{1,0:T(8,128)S(1)}, u32[]{:S(2)}, u32[]{:S(2)}) collective-permute-start(f32[8,128]{1,0:T(8,128)S(1)} %add.2.refs_4_), channel_id=1, source_target_pairs={{0,4},{4,8},{8,12},{12,0},{1,5},{5,9},{9,13},{13,1},{2,6},{6,10},{... | collective-permute-start | bytes 12296 | tf_op jit(solution)/shard_map/ppermute | solution.py:402
  65.9 2.5 %collective-permute-done.19.refs_5_ = f32[8,128]{1,0:T(8,128)S(1)} collective-permute-done((f32[8,128]{1,0:T(8,128)S(1)}, f32[8,128]{1,0:T(8,128)S(1)}, u32[]{:S(2)}, u32[]{:S(2)}) %collective-permute-start.19) | collective-permute-done | bytes 4128 | tf_op jit(solution)/shard_map/ppermute | solution.py:402
  70.3 2.4 %collective-permute-done.23.refs_2_ = f32[8,128]{1,0:T(8,128)S(1)} collective-permute-done((f32[8,128]{1,0:T(8,128)S(1)}, f32[8,128]{1,0:T(8,128)S(1)}, u32[]{:S(2)}, u32[]{:S(2)}) %collective-permute-start.23) | collective-permute-done | bytes 4128 | tf_op jit(solution)/shard_map/ppermute | solution.py:402
  72.8 3.0 %remote_images.3 = (f32[4,256,128]{2,1,0:T(8,128)S(1)}, f32[4,256,128]{2,1,0:T(8,128)S(1)}, f32[4,256,128]{2,1,0:T(8,128)S(1)}) custom-call(s32[542]{0:T(1024)S(1)} %get-tuple-element.43.lists, f32[4,256,128]{2,1,0:T(8,128)S(1)} %get-tuple-element.46.vector.held, f32[4,256,128]{2,1,0:T(8,128)S(1)} %bitcast.32, f32[8,128]{1,0:T(8,128)S(1)} %get-tuple-element.63.refs_0_, ...), custom_call_target="tpu_custom_call" | custom-call | flops 6000000000 | bytes 20971520 | tf_op jit(solution)/shard_map/remote_images/pallas_call | solution.py:228
  75.9 1.9 %collective-permute-done.25 = f32[4,256,128]{2,1,0:T(8,128)S(1)} collective-permute-done((f32[4,256,128]{2,1,0:T(8,128)S(1)}, f32[4,256,128]{2,1,0:T(8,128)S(1)}, u32[]{:S(2)}, u32[]{:S(2)}) %collective-permute-start.25) | collective-permute-done | bytes 524320 | tf_op jit(solution)/shard_map/ppermute | solution.py:402
  77.9 7.2 %own_images.3 = (f32[4,256,128]{2,1,0:T(8,128)S(1)}, f32[4,256,128]{2,1,0:T(8,128)S(1)}) custom-call(s32[542]{0:T(1024)S(1)} %get-tuple-element.43.lists, f32[4,256,128]{2,1,0:T(8,128)S(1)} %get-tuple-element.64.vector.held, f32[4,128,128]{2,1,0:T(8,128)S(1)} %get-tuple-element.67.after, bf16[96,256,256]{2,1,0:T(8,128)(2,1)S(1)} %get-tuple-element.44.refs_4_.left, ...), custom_call_target="tpu_custom_call" | custom-call | flops 6000000000 | bytes 20971520 | tf_op jit(solution)/shard_map/own_images/pallas_call | solution.py:228
  86.6 1.8 %collective-permute-start.32 = (f32[1,128,128]{2,1,0:T(8,128)S(1)}, f32[1,128,128]{2,1,0:T(8,128)S(1)}, u32[]{:S(2)}, u32[]{:S(2)}) collective-permute-start(f32[1,128,128]{2,1,0:T(8,128)S(1)} %get-tuple-element.76), channel_id=1, source_target_pairs={{0,8},{4,12},{8,0},{12,4},{1,9},{5,13},{9,1},{13,5},{2,10},{6,14},... | collective-permute-start | bytes 196616 | tf_op jit(solution)/shard_map/ppermute | solution.py:402
  88.5 1.9 %collective-permute-start.33 = (f32[1,128,128]{2,1,0:T(8,128)S(1)}, f32[1,128,128]{2,1,0:T(8,128)S(1)}, u32[]{:S(2)}, u32[]{:S(2)}) collective-permute-start(f32[1,128,128]{2,1,0:T(8,128)S(1)} %get-tuple-element.77), channel_id=1, source_target_pairs={{0,12},{4,0},{8,4},{12,8},{1,13},{5,1},{9,5},{13,9},{2,14},{6,2},{... | collective-permute-start | bytes 196616 | tf_op jit(solution)/shard_map/ppermute | solution.py:402
  90.3 3.5 %collective-permute-done.27.refs_0_ = f32[4,128,128]{2,1,0:T(8,128)S(1)} collective-permute-done((f32[4,128,128]{2,1,0:T(8,128)S(1)}, f32[4,128,128]{2,1,0:T(8,128)S(1)}, u32[]{:S(2)}, u32[]{:S(2)}) %collective-permute-start.27) | collective-permute-done | bytes 262176 | tf_op jit(solution)/shard_map/ppermute | solution.py:402
  95.9 1.9 %collective-permute-start.30 = (f32[2,128,128]{2,1,0:T(8,128)S(1)}, f32[2,128,128]{2,1,0:T(8,128)S(1)}, u32[]{:S(2)}, u32[]{:S(2)}) collective-permute-start(f32[2,128,128]{2,1,0:T(8,128)S(1)} %get-tuple-element.73), channel_id=1, source_target_pairs={{0,12},{4,0},{8,4},{12,8},{1,13},{5,1},{9,5},{13,9},{2,14},{6,2},{... | collective-permute-start | bytes 393224 | tf_op jit(solution)/shard_map/ppermute | solution.py:402
  99.1 3.0 %collective-permute-done.34.refs_4_ = f32[128,128]{1,0:T(8,128)S(1)} collective-permute-done((f32[128,128]{1,0:T(8,128)S(1)}, f32[128,128]{1,0:T(8,128)S(1)}, u32[]{:S(2)}, u32[]{:S(2)}) %collective-permute-start.34) | collective-permute-done | bytes 65568 | tf_op jit(solution)/shard_map/ppermute | solution.py:402
  102.2 4.3 %collective-permute-done.29.refs_2_ = f32[2,128,128]{2,1,0:T(8,128)S(1)} collective-permute-done((f32[2,128,128]{2,1,0:T(8,128)S(1)}, f32[2,128,128]{2,1,0:T(8,128)S(1)}, u32[]{:S(2)}, u32[]{:S(2)}) %collective-permute-start.29) | collective-permute-done | bytes 131104 | tf_op jit(solution)/shard_map/ppermute | solution.py:402
  106.7 2.2 %collective-permute-start.37 = (f32[2,128,128]{2,1,0:T(8,128)S(1)}, f32[2,128,128]{2,1,0:T(8,128)S(1)}, u32[]{:S(2)}, u32[]{:S(2)}) collective-permute-start(f32[2,128,128]{2,1,0:T(8,128)S(1)} %get-tuple-element.78.refs_0_), channel_id=1, source_target_pairs={{0,12},{4,0},{8,4},{12,8},{1,13},{5,1},{9,5},{13,9},{2,14},{6,2},{... | collective-permute-start | bytes 393224 | tf_op jit(solution)/shard_map/ppermute | solution.py:402
  108.9 2.0 %collective-permute-start.36 = (f32[2,128,128]{2,1,0:T(8,128)S(1)}, f32[2,128,128]{2,1,0:T(8,128)S(1)}, u32[]{:S(2)}, u32[]{:S(2)}) collective-permute-start(f32[2,128,128]{2,1,0:T(8,128)S(1)} %get-tuple-element.78.refs_0_), channel_id=1, source_target_pairs={{0,8},{4,12},{8,0},{12,4},{1,9},{5,13},{9,1},{13,5},{2,10},{6,14},... | collective-permute-start | bytes 393224 | tf_op jit(solution)/shard_map/ppermute | solution.py:402
  115.2 4.1 %collective-permute-start.43 = (f32[8,128]{1,0:T(8,128)S(1)}, f32[8,128]{1,0:T(8,128)S(1)}, u32[]{:S(2)}, u32[]{:S(2)}) collective-permute-start(f32[8,128]{1,0:T(8,128)S(1)} %add.3.refs_4_), channel_id=1, source_target_pairs={{0,12},{4,0},{8,4},{12,8},{1,13},{5,1},{9,5},{13,9},{2,14},{6,2},{... | collective-permute-start | bytes 12296 | tf_op jit(solution)/shard_map/ppermute | solution.py:402
  120.6 2.2 %collective-permute-start.41 = (f32[8,128]{1,0:T(8,128)S(1)}, f32[8,128]{1,0:T(8,128)S(1)}, u32[]{:S(2)}, u32[]{:S(2)}) collective-permute-start(f32[8,128]{1,0:T(8,128)S(1)} %add.3.refs_4_), channel_id=1, source_target_pairs={{0,4},{4,8},{8,12},{12,0},{1,5},{5,9},{9,13},{13,1},{2,6},{6,10},{... | collective-permute-start | bytes 12296 | tf_op jit(solution)/shard_map/ppermute | solution.py:402
  123.8 2.5 %collective-permute-done.41.refs_5_ = f32[8,128]{1,0:T(8,128)S(1)} collective-permute-done((f32[8,128]{1,0:T(8,128)S(1)}, f32[8,128]{1,0:T(8,128)S(1)}, u32[]{:S(2)}, u32[]{:S(2)}) %collective-permute-start.41) | collective-permute-done | bytes 4128 | tf_op jit(solution)/shard_map/ppermute | solution.py:402
  128.2 2.4 %collective-permute-done.45.refs_2_ = f32[8,128]{1,0:T(8,128)S(1)} collective-permute-done((f32[8,128]{1,0:T(8,128)S(1)}, f32[8,128]{1,0:T(8,128)S(1)}, u32[]{:S(2)}, u32[]{:S(2)}) %collective-permute-start.45) | collective-permute-done | bytes 4128 | tf_op jit(solution)/shard_map/ppermute | solution.py:402
  (88 shorter events, 32.4 us)
Async XLA Ops:
  1.9 11.8 %collective-permute-start.2 = (f32[8,128]{1,0:T(8,128)S(1)}, f32[8,128]{1,0:T(8,128)S(1)}, u32[]{:S(2)}, u32[]{:S(2)}) collective-permute-start(f32[8,128]{1,0:T(8,128)S(1)} %square_sum.1.refs_0_), channel_id=1, source_target_pairs={{0,3},{1,0},{2,1},{3,2},{4,7},{5,4},{6,5},{7,6},{8,11},{9,8},{10,9... | collective-permute-start | bytes 12296 | tf_op jit(solution)/shard_map/ppermute | solution.py:402
  4.4 9.4 %collective-permute-start.1 = (f32[8,128]{1,0:T(8,128)S(1)}, f32[8,128]{1,0:T(8,128)S(1)}, u32[]{:S(2)}, u32[]{:S(2)}) collective-permute-start(f32[8,128]{1,0:T(8,128)S(1)} %square_sum.1.refs_0_), channel_id=1, source_target_pairs={{0,2},{1,3},{2,0},{3,1},{4,6},{5,7},{6,4},{7,5},{8,10},{9,11},{10,... | collective-permute-start | bytes 12296 | tf_op jit(solution)/shard_map/ppermute | solution.py:402
  5.0 8.8 %collective-permute-start = (f32[8,128]{1,0:T(8,128)S(1)}, f32[8,128]{1,0:T(8,128)S(1)}, u32[]{:S(2)}, u32[]{:S(2)}) collective-permute-start(f32[8,128]{1,0:T(8,128)S(1)} %square_sum.1.refs_0_), channel_id=1, source_target_pairs={{0,1},{1,2},{2,3},{3,0},{4,5},{5,6},{6,7},{7,4},{8,9},{9,10},{10,1... | collective-permute-start | bytes 12296 | tf_op jit(solution)/shard_map/ppermute | solution.py:402
  26.8 8.8 %collective-permute-start.4 = (f32[4,256,128]{2,1,0:T(8,128)S(1)}, f32[4,256,128]{2,1,0:T(8,128)S(1)}, u32[]{:S(2)}, u32[]{:S(2)}) collective-permute-start(f32[4,256,128]{2,1,0:T(8,128)S(1)} %get-tuple-element.51), channel_id=1, source_target_pairs={{0,1},{1,0},{2,3},{3,2},{4,5},{5,4},{6,7},{7,6},{8,9},{9,8},{10,11... | collective-permute-start | bytes 1572872 | tf_op jit(solution)/shard_map/ppermute | solution.py:402
  27.3 8.3 %collective-permute-start.5 = (f32[4,128,128]{2,1,0:T(8,128)S(1)}, f32[4,128,128]{2,1,0:T(8,128)S(1)}, u32[]{:S(2)}, u32[]{:S(2)}) collective-permute-start(f32[4,128,128]{2,1,0:T(8,128)S(1)} %get-tuple-element.49.after), channel_id=1, source_target_pairs={{0,2},{2,0},{1,3},{3,1},{4,6},{6,4},{5,7},{7,5},{8,10},{10,8},{9,1... | collective-permute-start | bytes 786440 | tf_op jit(solution)/shard_map/ppermute | solution.py:402
  27.9 11.4 %collective-permute-start.9 = (f32[1,128,128]{2,1,0:T(8,128)S(1)}, f32[1,128,128]{2,1,0:T(8,128)S(1)}, u32[]{:S(2)}, u32[]{:S(2)}) collective-permute-start(f32[1,128,128]{2,1,0:T(8,128)S(1)} %get-tuple-element.57), channel_id=1, source_target_pairs={{0,4},{4,8},{8,12},{12,0},{1,5},{5,9},{9,13},{13,1},{2,6},{6,10},{... | collective-permute-start | bytes 196616 | tf_op jit(solution)/shard_map/ppermute | solution.py:402
  28.9 12.4 %collective-permute-start.10 = (f32[1,128,128]{2,1,0:T(8,128)S(1)}, f32[1,128,128]{2,1,0:T(8,128)S(1)}, u32[]{:S(2)}, u32[]{:S(2)}) collective-permute-start(f32[1,128,128]{2,1,0:T(8,128)S(1)} %get-tuple-element.58), channel_id=1, source_target_pairs={{0,8},{4,12},{8,0},{12,4},{1,9},{5,13},{9,1},{13,5},{2,10},{6,14},... | collective-permute-start | bytes 196616 | tf_op jit(solution)/shard_map/ppermute | solution.py:402
  31.5 9.8 %collective-permute-start.11 = (f32[1,128,128]{2,1,0:T(8,128)S(1)}, f32[1,128,128]{2,1,0:T(8,128)S(1)}, u32[]{:S(2)}, u32[]{:S(2)}) collective-permute-start(f32[1,128,128]{2,1,0:T(8,128)S(1)} %get-tuple-element.59), channel_id=1, source_target_pairs={{0,12},{4,0},{8,4},{12,8},{1,13},{5,1},{9,5},{13,9},{2,14},{6,2},{... | collective-permute-start | bytes 196616 | tf_op jit(solution)/shard_map/ppermute | solution.py:402
  35.7 9.9 %collective-permute-start.6 = (f32[2,128,128]{2,1,0:T(8,128)S(1)}, f32[2,128,128]{2,1,0:T(8,128)S(1)}, u32[]{:S(2)}, u32[]{:S(2)}) collective-permute-start(f32[2,128,128]{2,1,0:T(8,128)S(1)} %get-tuple-element.53), channel_id=1, source_target_pairs={{0,4},{4,8},{8,12},{12,0},{1,5},{5,9},{9,13},{13,1},{2,6},{6,10},{... | collective-permute-start | bytes 393224 | tf_op jit(solution)/shard_map/ppermute | solution.py:402
  37.3 10.6 %collective-permute-start.7 = (f32[2,128,128]{2,1,0:T(8,128)S(1)}, f32[2,128,128]{2,1,0:T(8,128)S(1)}, u32[]{:S(2)}, u32[]{:S(2)}) collective-permute-start(f32[2,128,128]{2,1,0:T(8,128)S(1)} %get-tuple-element.54), channel_id=1, source_target_pairs={{0,8},{4,12},{8,0},{12,4},{1,9},{5,13},{9,1},{13,5},{2,10},{6,14},... | collective-permute-start | bytes 393224 | tf_op jit(solution)/shard_map/ppermute | solution.py:402
  39.3 8.7 %collective-permute-start.8 = (f32[2,128,128]{2,1,0:T(8,128)S(1)}, f32[2,128,128]{2,1,0:T(8,128)S(1)}, u32[]{:S(2)}, u32[]{:S(2)}) collective-permute-start(f32[2,128,128]{2,1,0:T(8,128)S(1)} %get-tuple-element.55), channel_id=1, source_target_pairs={{0,12},{4,0},{8,4},{12,8},{1,13},{5,1},{9,5},{13,9},{2,14},{6,2},{... | collective-permute-start | bytes 393224 | tf_op jit(solution)/shard_map/ppermute | solution.py:402
  41.3 4.3 %collective-permute-start.12 = (f32[128,128]{1,0:T(8,128)S(1)}, f32[128,128]{1,0:T(8,128)S(1)}, u32[]{:S(2)}, u32[]{:S(2)}) collective-permute-start(f32[128,128]{1,0:T(8,128)S(1)} %sum_parts.2), channel_id=1, source_target_pairs={{0,2},{2,0},{1,3},{3,1},{4,6},{6,4},{5,7},{7,5},{8,10},{10,8},{9,1... | collective-permute-start | bytes 196616 | tf_op jit(solution)/shard_map/ppermute | solution.py:402
  48.2 20.2 %collective-permute-start.15 = (f32[2,128,128]{2,1,0:T(8,128)S(1)}, f32[2,128,128]{2,1,0:T(8,128)S(1)}, u32[]{:S(2)}, u32[]{:S(2)}) collective-permute-start(f32[2,128,128]{2,1,0:T(8,128)S(1)} %get-tuple-element.60.refs_0_), channel_id=1, source_target_pairs={{0,12},{4,0},{8,4},{12,8},{1,13},{5,1},{9,5},{13,9},{2,14},{6,2},{... | collective-permute-start | bytes 393224 | tf_op jit(solution)/shard_map/ppermute | solution.py:402
  52.6 15.8 %collective-permute-start.14 = (f32[2,128,128]{2,1,0:T(8,128)S(1)}, f32[2,128,128]{2,1,0:T(8,128)S(1)}, u32[]{:S(2)}, u32[]{:S(2)}) collective-permute-start(f32[2,128,128]{2,1,0:T(8,128)S(1)} %get-tuple-element.60.refs_0_), channel_id=1, source_target_pairs={{0,8},{4,12},{8,0},{12,4},{1,9},{5,13},{9,1},{13,5},{2,10},{6,14},... | collective-permute-start | bytes 393224 | tf_op jit(solution)/shard_map/ppermute | solution.py:402
  53.0 15.5 %collective-permute-start.13 = (f32[2,128,128]{2,1,0:T(8,128)S(1)}, f32[2,128,128]{2,1,0:T(8,128)S(1)}, u32[]{:S(2)}, u32[]{:S(2)}) collective-permute-start(f32[2,128,128]{2,1,0:T(8,128)S(1)} %get-tuple-element.60.refs_0_), channel_id=1, source_target_pairs={{0,4},{4,8},{8,12},{12,0},{1,5},{5,9},{9,13},{13,1},{2,6},{6,10},{... | collective-permute-start | bytes 393224 | tf_op jit(solution)/shard_map/ppermute | solution.py:402
  57.6 5.1 %collective-permute-start.21 = (f32[8,128]{1,0:T(8,128)S(1)}, f32[8,128]{1,0:T(8,128)S(1)}, u32[]{:S(2)}, u32[]{:S(2)}) collective-permute-start(f32[8,128]{1,0:T(8,128)S(1)} %add.2.refs_4_), channel_id=1, source_target_pairs={{0,12},{4,0},{8,4},{12,8},{1,13},{5,1},{9,5},{13,9},{2,14},{6,2},{... | collective-permute-start | bytes 12296 | tf_op jit(solution)/shard_map/ppermute | solution.py:402
  61.4 4.5 %collective-permute-start.20 = (f32[8,128]{1,0:T(8,128)S(1)}, f32[8,128]{1,0:T(8,128)S(1)}, u32[]{:S(2)}, u32[]{:S(2)}) collective-permute-start(f32[8,128]{1,0:T(8,128)S(1)} %add.2.refs_4_), channel_id=1, source_target_pairs={{0,8},{4,12},{8,0},{12,4},{1,9},{5,13},{9,1},{13,5},{2,10},{6,14},... | collective-permute-start | bytes 12296 | tf_op jit(solution)/shard_map/ppermute | solution.py:402
  62.7 5.7 %collective-permute-start.19 = (f32[8,128]{1,0:T(8,128)S(1)}, f32[8,128]{1,0:T(8,128)S(1)}, u32[]{:S(2)}, u32[]{:S(2)}) collective-permute-start(f32[8,128]{1,0:T(8,128)S(1)} %add.2.refs_4_), channel_id=1, source_target_pairs={{0,4},{4,8},{8,12},{12,0},{1,5},{5,9},{9,13},{13,1},{2,6},{6,10},{... | collective-permute-start | bytes 12296 | tf_op jit(solution)/shard_map/ppermute | solution.py:402
  85.1 8.8 %collective-permute-start.26 = (f32[4,256,128]{2,1,0:T(8,128)S(1)}, f32[4,256,128]{2,1,0:T(8,128)S(1)}, u32[]{:S(2)}, u32[]{:S(2)}) collective-permute-start(f32[4,256,128]{2,1,0:T(8,128)S(1)} %get-tuple-element.69), channel_id=1, source_target_pairs={{0,1},{1,0},{2,3},{3,2},{4,5},{5,4},{6,7},{7,6},{8,9},{9,8},{10,11... | collective-permute-start | bytes 1572872 | tf_op jit(solution)/shard_map/ppermute | solution.py:402
  85.3 8.6 %collective-permute-start.27 = (f32[4,128,128]{2,1,0:T(8,128)S(1)}, f32[4,128,128]{2,1,0:T(8,128)S(1)}, u32[]{:S(2)}, u32[]{:S(2)}) collective-permute-start(f32[4,128,128]{2,1,0:T(8,128)S(1)} %get-tuple-element.67.after), channel_id=1, source_target_pairs={{0,2},{2,0},{1,3},{3,1},{4,6},{6,4},{5,7},{7,5},{8,10},{10,8},{9,1... | collective-permute-start | bytes 786440 | tf_op jit(solution)/shard_map/ppermute | solution.py:402
  86.5 9.4 %collective-permute-start.31 = (f32[1,128,128]{2,1,0:T(8,128)S(1)}, f32[1,128,128]{2,1,0:T(8,128)S(1)}, u32[]{:S(2)}, u32[]{:S(2)}) collective-permute-start(f32[1,128,128]{2,1,0:T(8,128)S(1)} %get-tuple-element.75), channel_id=1, source_target_pairs={{0,4},{4,8},{8,12},{12,0},{1,5},{5,9},{9,13},{13,1},{2,6},{6,10},{... | collective-permute-start | bytes 196616 | tf_op jit(solution)/shard_map/ppermute | solution.py:402
  86.6 11.2 %collective-permute-start.32 = (f32[1,128,128]{2,1,0:T(8,128)S(1)}, f32[1,128,128]{2,1,0:T(8,128)S(1)}, u32[]{:S(2)}, u32[]{:S(2)}) collective-permute-start(f32[1,128,128]{2,1,0:T(8,128)S(1)} %get-tuple-element.76), channel_id=1, source_target_pairs={{0,8},{4,12},{8,0},{12,4},{1,9},{5,13},{9,1},{13,5},{2,10},{6,14},... | collective-permute-start | bytes 196616 | tf_op jit(solution)/shard_map/ppermute | solution.py:402
  88.5 9.4 %collective-permute-start.33 = (f32[1,128,128]{2,1,0:T(8,128)S(1)}, f32[1,128,128]{2,1,0:T(8,128)S(1)}, u32[]{:S(2)}, u32[]{:S(2)}) collective-permute-start(f32[1,128,128]{2,1,0:T(8,128)S(1)} %get-tuple-element.77), channel_id=1, source_target_pairs={{0,12},{4,0},{8,4},{12,8},{1,13},{5,1},{9,5},{13,9},{2,14},{6,2},{... | collective-permute-start | bytes 196616 | tf_op jit(solution)/shard_map/ppermute | solution.py:402
  93.9 8.3 %collective-permute-start.28 = (f32[2,128,128]{2,1,0:T(8,128)S(1)}, f32[2,128,128]{2,1,0:T(8,128)S(1)}, u32[]{:S(2)}, u32[]{:S(2)}) collective-permute-start(f32[2,128,128]{2,1,0:T(8,128)S(1)} %get-tuple-element.71), channel_id=1, source_target_pairs={{0,4},{4,8},{8,12},{12,0},{1,5},{5,9},{9,13},{13,1},{2,6},{6,10},{... | collective-permute-start | bytes 393224 | tf_op jit(solution)/shard_map/ppermute | solution.py:402
  94.6 11.9 %collective-permute-start.29 = (f32[2,128,128]{2,1,0:T(8,128)S(1)}, f32[2,128,128]{2,1,0:T(8,128)S(1)}, u32[]{:S(2)}, u32[]{:S(2)}) collective-permute-start(f32[2,128,128]{2,1,0:T(8,128)S(1)} %get-tuple-element.72), channel_id=1, source_target_pairs={{0,8},{4,12},{8,0},{12,4},{1,9},{5,13},{9,1},{13,5},{2,10},{6,14},... | collective-permute-start | bytes 393224 | tf_op jit(solution)/shard_map/ppermute | solution.py:402
  95.9 10.6 %collective-permute-start.30 = (f32[2,128,128]{2,1,0:T(8,128)S(1)}, f32[2,128,128]{2,1,0:T(8,128)S(1)}, u32[]{:S(2)}, u32[]{:S(2)}) collective-permute-start(f32[2,128,128]{2,1,0:T(8,128)S(1)} %get-tuple-element.73), channel_id=1, source_target_pairs={{0,12},{4,0},{8,4},{12,8},{1,13},{5,1},{9,5},{13,9},{2,14},{6,2},{... | collective-permute-start | bytes 393224 | tf_op jit(solution)/shard_map/ppermute | solution.py:402
  106.7 19.6 %collective-permute-start.37 = (f32[2,128,128]{2,1,0:T(8,128)S(1)}, f32[2,128,128]{2,1,0:T(8,128)S(1)}, u32[]{:S(2)}, u32[]{:S(2)}) collective-permute-start(f32[2,128,128]{2,1,0:T(8,128)S(1)} %get-tuple-element.78.refs_0_), channel_id=1, source_target_pairs={{0,12},{4,0},{8,4},{12,8},{1,13},{5,1},{9,5},{13,9},{2,14},{6,2},{... | collective-permute-start | bytes 393224 | tf_op jit(solution)/shard_map/ppermute | solution.py:402
  108.9 17.4 %collective-permute-start.36 = (f32[2,128,128]{2,1,0:T(8,128)S(1)}, f32[2,128,128]{2,1,0:T(8,128)S(1)}, u32[]{:S(2)}, u32[]{:S(2)}) collective-permute-start(f32[2,128,128]{2,1,0:T(8,128)S(1)} %get-tuple-element.78.refs_0_), channel_id=1, source_target_pairs={{0,8},{4,12},{8,0},{12,4},{1,9},{5,13},{9,1},{13,5},{2,10},{6,14},... | collective-permute-start | bytes 393224 | tf_op jit(solution)/shard_map/ppermute | solution.py:402
  110.8 15.5 %collective-permute-start.35 = (f32[2,128,128]{2,1,0:T(8,128)S(1)}, f32[2,128,128]{2,1,0:T(8,128)S(1)}, u32[]{:S(2)}, u32[]{:S(2)}) collective-permute-start(f32[2,128,128]{2,1,0:T(8,128)S(1)} %get-tuple-element.78.refs_0_), channel_id=1, source_target_pairs={{0,4},{4,8},{8,12},{12,0},{1,5},{5,9},{9,13},{13,1},{2,6},{6,10},{... | collective-permute-start | bytes 393224 | tf_op jit(solution)/shard_map/ppermute | solution.py:402
  115.2 5.4 %collective-permute-start.43 = (f32[8,128]{1,0:T(8,128)S(1)}, f32[8,128]{1,0:T(8,128)S(1)}, u32[]{:S(2)}, u32[]{:S(2)}) collective-permute-start(f32[8,128]{1,0:T(8,128)S(1)} %add.3.refs_4_), channel_id=1, source_target_pairs={{0,12},{4,0},{8,4},{12,8},{1,13},{5,1},{9,5},{13,9},{2,14},{6,2},{... | collective-permute-start | bytes 12296 | tf_op jit(solution)/shard_map/ppermute | solution.py:402
  119.3 4.5 %collective-permute-start.42 = (f32[8,128]{1,0:T(8,128)S(1)}, f32[8,128]{1,0:T(8,128)S(1)}, u32[]{:S(2)}, u32[]{:S(2)}) collective-permute-start(f32[8,128]{1,0:T(8,128)S(1)} %add.3.refs_4_), channel_id=1, source_target_pairs={{0,8},{4,12},{8,0},{12,4},{1,9},{5,13},{9,1},{13,5},{2,10},{6,14},... | collective-permute-start | bytes 12296 | tf_op jit(solution)/shard_map/ppermute | solution.py:402
  120.6 5.7 %collective-permute-start.41 = (f32[8,128]{1,0:T(8,128)S(1)}, f32[8,128]{1,0:T(8,128)S(1)}, u32[]{:S(2)}, u32[]{:S(2)}) collective-permute-start(f32[8,128]{1,0:T(8,128)S(1)} %add.3.refs_4_), channel_id=1, source_target_pairs={{0,4},{4,8},{8,12},{12,0},{1,5},{5,9},{9,13},{13,1},{2,6},{6,10},{... | collective-permute-start | bytes 12296 | tf_op jit(solution)/shard_map/ppermute | solution.py:402
  (18 other events, 85.9 us)

commit v4 on v3

v4 whole, which is shorter than its diff:
```python
import functools

import jax
import jax.numpy as jnp
from jax import lax
from jax.experimental import pallas as pl
from jax.experimental.pallas import tpu as pltpu
from jax.sharding import PartitionSpec as P

ITERS = 2
GROUP = 4
EARLY = 3
REMOTE, OWN = 0, 1
VMEM = pl.BlockSpec(memory_space=pltpu.VMEM)
SMEM = pl.BlockSpec(memory_space=pltpu.SMEM)
ANY = pl.BlockSpec(memory_space=pl.ANY)


def f32(*shape):
    return jax.ShapeDtypeStruct(shape, jnp.float32)


def limit(mebibytes):
    return pltpu.CompilerParams(vmem_limit_bytes=mebibytes * 2**20)


def list_places(pairs, targets):
    cap = (pairs + targets) // 2 + 2 * GROUP
    cap = -(-cap // GROUP) * GROUP
    slot = 3 * 2 * cap
    groups = slot + 3 * cap
    return cap, slot, groups, groups + 2


def code_unit(blocks):
    return 1 << blocks.bit_length()


def make_plan(secs, places, targets, lists, pending, filled):
    terms, blocks = targets.shape
    total = secs * blocks
    cap, slot, groups, _ = places
    unit = code_unit(blocks)
    my_sec = lax.axis_index("sec")
    for place in range(total + 1):
        pending[place] = -1
    for region in range(3):
        filled[region] = 0

    def put(region, step, first, second, value):
        lists[2 * (region * cap + step)] = first
        lists[2 * (region * cap + step) + 1] = second
        lists[slot + region * cap + step] = value

    def take(term, carry):
        for b in range(blocks):
            target = targets[term, b]
            owner = lax.div(jnp.maximum(target, 0), blocks)
            turn = owner - my_sec
            turn = jnp.where(turn < 0, turn + secs, turn)
            own = turn == 0
            place = turn * blocks + (target - owner * blocks)
            place = jnp.where(target < 0, total, place)
            region = jnp.where(target < 0, 2, jnp.where(own, OWN, REMOTE))
            value = jnp.where(own, place, place - blocks)
            waiting, code, step = pending[place], (term * blocks + b) * unit + b, filled[region]
            put(region, step, waiting, code, value)
            filled[region] = step + jnp.where(waiting >= 0, 1, 0)
            pending[place] = jnp.where(waiting >= 0, -1, code)
        return carry

    lax.fori_loop(0, terms, take, 0)
    for region, span in ((REMOTE, range(blocks, total)), (OWN, range(blocks))):
        step = filled[region]
        for place in span:
            waiting = pending[place]
            put(region, step, jnp.maximum(waiting, 0), blocks, place - span[0])
            step = step + jnp.where(waiting >= 0, 1, 0)
        for extra in range(GROUP):
            put(region, step + extra, blocks, blocks, 0)
        lists[groups + region] = lax.div(step + GROUP - 1, GROUP)


def load_kernel(secs, places, targets, left, right, lists, left_held, right_held, pending, filled, sems):
    shares = sems.shape[1]
    each = left.shape[0] // shares
    copies = []
    for share in range(shares):
        rows = pl.ds(share * each, each)
        copies.append(pltpu.make_async_copy(left.at[rows], left_held.at[rows], sems.at[0, share]))
        copies.append(pltpu.make_async_copy(right.at[rows], right_held.at[rows], sems.at[1, share]))
    for copy in copies:
        copy.start()
    make_plan(secs, places, targets, lists, pending, filled)
    for copy in copies:
        copy.wait()


def load(secs, places, targets, left, right):
    terms, blocks = targets.shape
    return pl.pallas_call(
        functools.partial(load_kernel, secs, places),
        out_shape=(
            jax.ShapeDtypeStruct((places[-1],), jnp.int32),
            pltpu.VMEM(left.shape, left.dtype),
            pltpu.VMEM(right.shape, right.dtype),
        ),
        in_specs=[SMEM, ANY, ANY],
        out_specs=(SMEM, VMEM, VMEM),
        scratch_shapes=[
            pltpu.SMEM((secs * blocks + 1,), jnp.int32),
            pltpu.SMEM((3,), jnp.int32),
            pltpu.SemaphoreType.DMA((2, 6)),
        ],
        compiler_params=limit(2),
        cost_estimate=pl.CostEstimate(flops=0, bytes_accessed=40 * 2**20, transcendentals=0),
        name="load",
    )(
        targets,
        pltpu.with_memory_space_constraint(left, pltpu.HBM),
        pltpu.with_memory_space_constraint(right, pltpu.HBM),
    )


def square_kernel(wave, square):
    square[...] = jnp.full(square.shape, jnp.sum(wave[...] * wave[...]))


def square_sum(wave, devices):
    return pl.pallas_call(
        square_kernel,
        out_shape=f32(devices, 8, 128),
        in_specs=[VMEM],
        out_specs=VMEM,
        compiler_params=limit(2),
        name="square_sum",
    )(wave)


def added(refs):
    total = refs[0][...]
    for ref in refs[1:]:
        total = total + ref[...]
    return total


def multiply_terms(region, turns, places, lists, left, right, vector_bf, product, keep, send):
    cap, slot, groups, _ = places
    unit = code_unit(vector_bf.shape[0] - 1)
    my_sub = lax.axis_index("sub")
    half = keep.shape[2]
    count = lists[groups + region]
    begin = jnp.minimum(turns[0], count)
    end = count if turns[1] is None else jnp.minimum(turns[1], count)

    def tile(at):
        return lax.shift_right_logical(lists[at], unit.bit_length() - 1)

    def first(group):
        for k in range(2 * GROUP):
            at = 2 * (region * cap + group * GROUP) + k
            part = jnp.dot(
                left[tile(at)], vector_bf[lists[at] & (unit - 1)], preferred_element_type=jnp.float32
            )
            product[k // 2, :, (k % 2) * half : (k % 2 + 1) * half] = part.astype(jnp.bfloat16)

    def second(group):
        for g in range(GROUP):
            at = region * cap + group * GROUP + g
            pair = jnp.concatenate([right[tile(2 * at)], right[tile(2 * at + 1)]], axis=0)
            image = jnp.dot(product[g], pair, preferred_element_type=jnp.float32)
            low, high = image[:, :half], image[:, half:]
            n = lists[slot + at]
            keep[n] += jnp.where(my_sub == 0, low, high)
            send[n] += jnp.where(my_sub == 0, high, low)

    @pl.when(end > begin)
    def _():
        first(begin)

        def turn(group, carry):
            second(group - 1)
            first(group)
            return carry

        lax.fori_loop(begin + 1, end, turn, 0)
        second(end - 1)


def round_vector(vector, vector_bf):
    blocks = vector.shape[0]
    vector_bf[:blocks] = vector[...].astype(jnp.bfloat16)
    vector_bf[blocks] = jnp.zeros(vector_bf.shape[1:], jnp.bfloat16)


def remote_turns(places, lists, left, right, vector, vector_bf, keep, send, product):
    round_vector(vector, vector_bf)
    keep[...] = jnp.zeros_like(keep)
    send[...] = jnp.zeros_like(send)
    multiply_terms(REMOTE, (0, None), places, lists, left, right, vector_bf, product, keep, send)


def start_kernel(entries, places, lists, wave, norms, left, right, vector, *refs):
    length = jnp.sqrt(jnp.sum(norms[...], axis=0)[:1, :1] / entries)
    vector[...] = wave[...] / length[None]
    remote_turns(places, lists, left, right, vector, *refs)


def refined(entries, held, correction, sums):
    total = jnp.sum(sums[...], axis=0) / entries
    along, square, own = total[0:1, :1], total[1:2, :1], total[2:3, :1]
    length = jnp.sqrt((1.0 + along) * (1.0 + along) * own - 2.0 * (1.0 + along) * along + square)
    return (held[...] - (correction[...] - along[None] * held[...])) / length[None]


def resume_kernel(entries, places, lists, held, correction, sums, left, right, vector, *refs):
    vector[...] = refined(entries, held, correction, sums)
    remote_turns(places, lists, left, right, vector, *refs)


def own_first_kernel(places, lists, vector_bf, left, right, keep, send, product):
    keep[...] = jnp.zeros_like(keep)
    send[...] = jnp.zeros_like(send)
    multiply_terms(OWN, (0, EARLY), places, lists, left, right, vector_bf, product, keep, send)


def own_rest_kernel(places, lists, vector_bf, keep_in, send_in, after, left, right, keep, send, product):
    keep[...] = keep_in[...]
    send[...] = send_in[...]
    multiply_terms(OWN, (EARLY, None), places, lists, left, right, vector_bf, product, keep, send)


def images(kernel, out_shape, name, lists, operands, left, right, after=(), turns=4):
    rows = left.shape[1]
    work = turns * GROUP * 2 * 8 * rows * rows * rows // 4
    return pl.pallas_call(
        kernel,
        out_shape=out_shape,
        in_specs=[SMEM] + [VMEM] * len(operands) + [ANY] * len(after) + [VMEM] * 2,
        out_specs=(VMEM,) * len(out_shape),
        scratch_shapes=[pltpu.VMEM((GROUP, rows, rows), jnp.bfloat16)],
        compiler_params=limit(12),
        cost_estimate=pl.CostEstimate(flops=2 * work, bytes_accessed=turns * 2**20, transcendentals=0),
        name=name,
    )(
        lists,
        *operands,
        *after,
        pltpu.with_memory_space_constraint(left, pltpu.VMEM),
        pltpu.with_memory_space_constraint(right, pltpu.VMEM),
    )


def call(kernel, out_shape, operands, name, mebibytes=4):
    return pl.pallas_call(
        kernel,
        out_shape=out_shape,
        in_specs=[VMEM] * len(operands),
        out_specs=jax.tree.map(lambda _: VMEM, out_shape),
        compiler_params=limit(mebibytes),
        name=name,
    )(*operands)


def part_kernel(aways, keep, landed, *outs):
    wholes, pieces = outs[:aways], outs[aways]
    for away in range(aways):
        wholes[away][...] = keep[away, 0] + landed[away, 0]
        pieces[:, away] = keep[away, 1] + landed[away, 1]


def part(keep, landed, aways, split):
    _, ops, rows, half = split
    shape = (aways, *split)
    outs = call(
        functools.partial(part_kernel, aways),
        (f32(ops, rows, half),) * aways + (f32(ops, aways, rows, half),),
        (keep.reshape(shape), landed.reshape(shape)),
        "part",
    )
    return outs[:-1], outs[-1]


def sum_kernel(parts, *outs):
    for away, out in enumerate(outs):
        out[...] = jnp.sum(parts[:, away], axis=0)


def sum_parts(parts):
    _, aways, rows, half = parts.shape
    return call(sum_kernel, (f32(rows, half),) * aways, (parts,), "sum_parts")


def pass_kernel(value, after, out):
    out[...] = value[...]


def pass_after(value, after):
    return pl.pallas_call(
        pass_kernel,
        out_shape=f32(*value.shape),
        in_specs=[VMEM, ANY],
        out_specs=VMEM,
        compiler_params=limit(4),
        name="pass_after",
    )(value, after)


def combine_kernel(keep, landed, *refs):
    wholes, pieces = refs[:-1], refs[-1]
    total = keep[0] + landed[0]
    for whole in wholes:
        total = total + whole[...]
    pieces[:, 0] = total
    pieces[:, 1] = keep[1] + landed[1]


def combine(keep, landed, wholes, split):
    _, ops, rows, half = split
    operands = (keep.reshape(split), landed.reshape(split), *wholes)
    return call(combine_kernel, f32(ops, 2, rows, half), operands, "combine")


def sigma_kernel(vector, diagonal, pieces, *refs):
    arrived, (sigma, inner) = refs[:-2], refs[-2:]
    my_op = lax.axis_index("op")
    inner_sum = jnp.float32(0)
    for side in range(2):
        total = jnp.sum(pieces[:, side], axis=0)
        if side == 1:
            total = total + added(arrived)
        held = vector[side, my_op]
        total = diagonal[side, my_op] * held + total
        for place in range(sigma.shape[0]):
            sigma[place, side] = total
        inner_sum += jnp.sum(held * total)
    inner[...] = jnp.full(inner.shape, inner_sum)


def sigma_share(vector, diagonal, pieces, arrived, devices):
    _, ops, rows, half = vector.shape
    return call(
        sigma_kernel,
        (f32(ops, 2, rows, half), f32(devices, 8, 128)),
        (vector, diagonal, pieces, *arrived),
        "sigma",
    )


def correct_kernel(entries, vector, diagonal, sigma, thetas, correction, sums, ritz):
    ritz[...] = jnp.sum(thetas[...], axis=0) / entries
    theta = ritz[:1, :1][None]
    totals = [jnp.float32(0)] * 3
    for side in range(2):
        held, diag = vector[side], diagonal[side]
        value = (sigma[:, side] - theta * held) / (1.0 + jnp.abs(diag - theta))
        correction[side] = value
        for index, term in enumerate((held * value, value * value, held * held)):
            totals[index] += jnp.sum(term)
    sums[...] = jnp.zeros_like(sums)
    for index, value in enumerate(totals):
        sums[:, index : index + 1] = jnp.full((sums.shape[0], 1, sums.shape[2]), value)


def correct(entries, vector, diagonal, sigma, thetas, devices):
    return call(
        functools.partial(correct_kernel, entries),
        (f32(*vector.shape), f32(devices, 8, 128), f32(8, 128)),
        (vector, diagonal, sigma, thetas),
        "correct",
    )


def finish_kernel(entries, held, correction, sums, *refs):
    ritz_refs, (out, ritz) = refs[:-2], refs[-2:]
    out[...] = refined(entries, held, correction, sums)
    for index, ref in enumerate(ritz_refs):
        ritz[index] = ref[0, 0]


def finish(entries, vector, correction, sums, ritz):
    return pl.pallas_call(
        functools.partial(finish_kernel, entries),
        out_shape=(f32(*vector.shape), f32(len(ritz))),
        in_specs=[VMEM] * (3 + len(ritz)),
        out_specs=(VMEM, SMEM),
        compiler_params=limit(4),
        name="finish",
    )(vector, correction, sums, *ritz)


def shift(array, axis, turn):
    count = lax.axis_size(axis)
    return lax.ppermute(array, axis, [(i, (i + turn) % count) for i in range(count)])


def swap(array, axis):
    return lax.all_to_all(array, axis, 0, 0, tiled=True)


def per_device(wavefunction, diagonal, left_env, right_env, targets):
    ops, secs, subs = (lax.axis_size(axis) for axis in ("op", "sec", "sub"))
    blocks, tile, half = wavefunction.shape
    terms = left_env.shape[0]
    entries = blocks * secs * tile * tile
    left = left_env.reshape(terms * blocks, tile, tile)
    right = right_env.reshape(terms * blocks, half, tile)
    split = (2, ops, blocks * tile // ops // 2, half)
    places = list_places(terms * blocks, secs * blocks)
    aways = secs - 1
    rounded = jax.ShapeDtypeStruct((blocks + 1, tile, half), jnp.bfloat16)
    whole, own_out = f32(blocks, tile, half), (f32(blocks, tile, half),) * 2
    remote_out = (whole, rounded) + (f32(aways * blocks, tile, half),) * 2
    own_first = functools.partial(own_first_kernel, places)
    own_rest = functools.partial(own_rest_kernel, places)
    diagonal = diagonal.reshape(split)
    norms = swap(square_sum(wavefunction, secs * subs), ("sec", "sub"))
    lists, left, right = load(secs, places, targets, left, right)
    start = functools.partial(start_kernel, entries, places)
    vector, vector_bf, keep, send = images(
        start, remote_out, "remote_images", lists, (wavefunction, norms), left, right
    )
    ritz = []
    for turn_index in range(ITERS):
        landed = shift(send, "sub", 1)
        own_parts = images(own_first, own_out, "own_first", lists, (vector_bf,), left, right)
        wholes, shares = part(keep, landed, aways, split)
        crossed = [shift(wholes[r - 1], "sec", r) for r in range(1, secs)]
        shares = swap(shares, "op")
        keep, send = images(
            own_rest, own_out, "own_rest", lists, (vector_bf, *own_parts), left, right, after=(wholes[0],), turns=8
        )
        send = pass_after(send, crossed[-1])
        arrived = [shift(share, "sec", r) for r, share in enumerate(sum_parts(shares), 1)]
        pieces = swap(combine(keep, shift(send, "sub", 1), crossed, split), "op")
        held = vector.reshape(split)
        sigma, inner = sigma_share(held, diagonal, pieces, arrived, ops * secs * subs)
        thetas = swap(inner, ("op", "sec", "sub"))
        sigma = swap(sigma, "op")
        correction, sums, theta = correct(entries, held, diagonal, sigma, thetas, secs * subs)
        ritz.append(theta)
        sums = swap(sums, ("sec", "sub"))
        correction = correction.reshape(vector.shape)
        if turn_index < ITERS - 1:
            resume = functools.partial(resume_kernel, entries, places)
            operands = (vector, correction, sums)
            vector, vector_bf, keep, send = images(
                resume, remote_out, "remote_images", lists, operands, left, right
            )
    return finish(entries, vector, correction, sums, ritz)


def solution(mesh):
    placed = (
        P(("grp", "sec"), None, "sub"),
        P(("grp", "sec"), None, "sub"),
        P(("grp", "op"), "sec", None, None),
        P(("grp", "op"), "sec", "sub", None),
        P(("grp", "op"), "sec"),
    )
    return jax.shard_map(
        per_device,
        mesh=mesh,
        in_specs=placed,
        out_specs=(P(("grp", "sec"), None, "sub"), P("grp")),
        check_vma=False,
    )
```

time: 132 us -> 200 us (1.52)
  blocking collectives: 0 us -> 66.1 us
  starting transfers between devices: 55.9 us -> 24 us
  local copies, waits for them, and re-layouts: 1.8 us -> 23.6 us
  waiting for transfers between devices: 42.5 us -> 48.9 us
  Pallas kernels: 30.8 us -> 35.4 us
    all_to_all x0 -> x6, blocking collectives: none -> 66.1 us  [swap(): return lax.all_to_all(array, axis, 0, 0, tiled=True)]
    ppermute x47 -> x8, starting transfers between devices: 55.9 us -> 4.29 us  [shift(): lax.ppermute(array, axis, [(i, (i + turn) % count) for i in range(count)])]
    all_to_all x0 -> x5, waiting for transfers between devices: none -> 35.5 us  [swap(): return lax.all_to_all(array, axis, 0, 0, tiled=True)]
    ppermute x47 -> x8, waiting for transfers between devices: 42.5 us -> 13.4 us  [shift(): lax.ppermute(array, axis, [(i, (i + turn) % count) for i in range(count)])]
    unnamed x7 -> x19, local copies, waits for them, and re-layouts: 1.8 us -> 23.6 us
    all_to_all x0 -> x5, starting transfers between devices: none -> 19.7 us  [swap(): return lax.all_to_all(array, axis, 0, 0, tiled=True)]
    pallas_call x12 -> x10, Pallas kernels: 1.54 us -> 4.56 us  [call(): pl.pallas_call(kernel, out_shape=out_shape, in_specs=[VMEM] * len(operand...]
    pallas_call x6 -> x10, Pallas kernels: 21.5 us -> 23 us  [the longest x6 21.1 us: images(): pl.pallas_call(kernel, out_shape=out_shape, in_specs=[SMEM] + [VMEM] * le...]
  transfers between devices with their start and end apart: 47 -> 13, of which waited for: 27 -> 8; matrix products, arithmetic and copies ran while one was open for 1% -> 0% of each run, Pallas kernels for 6% -> 12%
where the time goes in v4:
time: 200 us; the launch traced here: 199 us
  blocking collectives  66.1 us (33%)
  waiting for transfers between devices  48.9 us (24%)
  Pallas kernels  35.4 us (18%)
  starting transfers between devices  24 us (12%)
  local copies, waits for them, and re-layouts  23.6 us (12%)
    all_to_all x6, blocking collectives, swap(): return lax.all_to_all(array, axis, 0, 0, tiled=True)  66.1 us
    all_to_all x5, waiting for transfers between devices, swap(): return lax.all_to_all(array, axis, 0, 0, tiled=True)  35.5 us
    unnamed x19, local copies, waits for them, and re-layouts  23.6 us
    pallas_call x6, Pallas kernels, images(): pl.pallas_call(kernel, out_shape=out_shape, in_specs=[SMEM] + [VMEM] * le...  21.1 us
    all_to_all x5, starting transfers between devices, swap(): return lax.all_to_all(array, axis, 0, 0, tiled=True)  19.7 us
    ppermute x8, waiting for transfers between devices, shift(): lax.ppermute(array, axis, [(i, (i + turn) % count) for i in range(count)])  13.4 us
    pallas_call x1, Pallas kernels, load(): pl.pallas_call(functools.partial(load_kernel, secs, places), out_shape=(j...  7.84 us
    pallas_call x10, Pallas kernels, call(): pl.pallas_call(kernel, out_shape=out_shape, in_specs=[VMEM] * len(operand...  4.56 us
  transfers between devices with their start and end apart: 13, of which 8 were waited for; matrix products, arithmetic and copies ran while one was open for 0% of the time, Pallas kernels for 12%

profile of v4, /device:TPU:0, one launch (start us, length us, event | category | flops | bytes accessed | tf_op | source)
XLA Modules:
  0.0 198.8 jit_solution(17279235187635619016)
XLA Ops:
  2.5 4.2 %all-to-all-start = ((f32[4,8,128]{2,1,0:T(8,128)}), f32[4,8,128]{2,1,0:T(8,128)S(1)}, u32[]{:S(2)}, u32[]{:S(2)}) async-start(f32[4,8,128]{2,1,0:T(8,128)} %square_sum.1), calls=%async_computation | async-start | bytes 32768 | tf_op jit(solution)/shard_map/all_to_all | solution.py:398
  7.5 7.8 %load.1 = (s32[542]{0:T(1024)S(1)}, bf16[96,256,256]{2,1,0:T(8,128)(2,1)S(1)}, bf16[96,128,256]{2,1,0:T(8,128)(2,1)S(1)}) custom-call(s32[24,4]{1,0:T(8,128)S(1)} %copy.7.targets, bf16[96,256,256]{2,1,0:T(8,128)(2,1)} %bitcast.33, bf16[96,128,256]{2,1,0:T(8,128)(2,1)} %bitcast.34), custom_call_target="tpu_custom_call" | custom-call | bytes 41943040 | tf_op jit(solution)/shard_map/load/pallas_call | solution.py:101
  15.4 4.5 %copy-done = bf16[96,256,256]{2,1,0:T(8,128)(2,1)} copy-done((bf16[96,256,256]{2,1,0:T(8,128)(2,1)}, bf16[96,256,256]{2,1,0:T(8,128)(2,1)S(1)}, u32[]{:S(2)}) %copy-start) | copy-done | bytes 12582936
  19.9 2.6 %copy-done.3 = bf16[96,128,256]{2,1,0:T(8,128)(2,1)} copy-done((bf16[96,128,256]{2,1,0:T(8,128)(2,1)}, bf16[96,128,256]{2,1,0:T(8,128)(2,1)S(1)}, u32[]{:S(2)}) %copy-start.3) | copy-done | bytes 6291480
  22.5 4.6 %copy-done.1 = bf16[96,256,256]{2,1,0:T(8,128)(2,1)S(1)} copy-done((bf16[96,256,256]{2,1,0:T(8,128)(2,1)S(1)}, bf16[96,256,256]{2,1,0:T(8,128)(2,1)}, u32[]{:S(2)}) %copy-start.1) | copy-done | bytes 12582936
  27.1 2.8 %copy-done.4 = bf16[96,128,256]{2,1,0:T(8,128)(2,1)S(1)} copy-done((bf16[96,128,256]{2,1,0:T(8,128)(2,1)S(1)}, bf16[96,128,256]{2,1,0:T(8,128)(2,1)}, u32[]{:S(2)}) %copy-start.4) | copy-done | bytes 6291480
  29.8 3.4 %remote_images.2 = (f32[4,256,128]{2,1,0:T(8,128)S(1)}, bf16[5,256,128]{2,1,0:T(8,128)(2,1)S(1)}, f32[4,256,128]{2,1,0:T(8,128)S(1)}, f32[4,256,128]{2,1,0:T(8,128)S(1)}) custom-call(s32[542]{0:T(1024)S(1)} %get-tuple-element.35.lists, f32[4,256,128]{2,1,0:T(8,128)S(1)} %copy-done.8, f32[4,8,128]{2,1,0:T(8,128)S(1)} %all-to-all-done.norms, ...), custom_call_target="tpu_custom_call" | custom-call | flops 2147483648 | bytes 4194304 | tf_op jit(solution)/shard_map/remote_images/pallas_call | solution.py:236
  33.8 2.6 %own_first.2 = (f32[4,256,128]{2,1,0:T(8,128)S(1)}, f32[4,256,128]{2,1,0:T(8,128)S(1)}) custom-call(s32[542]{0:T(1024)S(1)} %get-tuple-element.35.lists, bf16[5,256,128]{2,1,0:T(8,128)(2,1)S(1)} %get-tuple-element.39.vector_bf, bf16[96,256,256]{2,1,0:T(8,128)(2,1)S(1)} %copy-done.1, bf16[96,128,256]{2,1,0:T(8,128)(2,1)S(1)} %copy-done.4), custom_call_target="tpu_custom_call" | custom-call | flops 2147483648 | bytes 4194304 | tf_op jit(solution)/shard_map/own_first/pallas_call | solution.py:236
  38.9 4.5 %own_rest.2 = (f32[4,256,128]{2,1,0:T(8,128)S(1)}, f32[4,256,128]{2,1,0:T(8,128)S(1)}) custom-call(s32[542]{0:T(1024)S(1)} %get-tuple-element.35.lists, bf16[5,256,128]{2,1,0:T(8,128)(2,1)S(1)} %get-tuple-element.39.vector_bf, f32[4,256,128]{2,1,0:T(8,128)S(1)} %get-tuple-element.40.keep_in, f32[4,256,128]{2,1,0:T(8,128)S(1)} %get-tuple-element.41.send_in, ...), custom_call_target="tpu_custom_call" | custom-call | flops 4294967296 | bytes 8388608 | tf_op jit(solution)/shard_map/own_rest/pallas_call | solution.py:236
  43.4 2.3 %collective-permute-done.1.after.refs_0_ = f32[4,128,128]{2,1,0:T(8,128)S(1)} collective-permute-done((f32[4,128,128]{2,1,0:T(8,128)S(1)}, f32[4,128,128]{2,1,0:T(8,128)S(1)}, u32[]{:S(2)}, u32[]{:S(2)}) %collective-permute-start.1) | collective-permute-done | bytes 262176 | tf_op jit(solution)/shard_map/ppermute | solution.py:394
  45.8 5.1 %all-to-all-start.2 = ((f32[4,1,128,128]{3,2,1,0:T(8,128)}), f32[4,1,128,128]{3,2,1,0:T(8,128)S(1)}, u32[]{:S(2)}, u32[]{:S(2)}) async-start(f32[4,1,128,128]{3,2,1,0:T(8,128)} %get-tuple-element.47), calls=%async_computation.2 | async-start | bytes 524288 | tf_op jit(solution)/shard_map/all_to_all | solution.py:398
  51.8 8.7 %all-to-all-done.2.parts = f32[4,1,128,128]{3,2,1,0:T(8,128)S(1)} async-done(((f32[4,1,128,128]{3,2,1,0:T(8,128)}), f32[4,1,128,128]{3,2,1,0:T(8,128)S(1)}, u32[]{:S(2)}, u32[]{:S(2)}) %all-to-all-start.2) | async-done | bytes 262176 | tf_op jit(solution)/shard_map/all_to_all | solution.py:398
  60.4 3.5 %all-to-all-start.1 = ((f32[4,2,128,128]{3,2,1,0:T(8,128)}), f32[4,2,128,128]{3,2,1,0:T(8,128)S(1)}, u32[]{:S(2)}, u32[]{:S(2)}) async-start(f32[4,2,128,128]{3,2,1,0:T(8,128)} %combine.2), calls=%async_computation.1 | async-start | bytes 1048576 | tf_op jit(solution)/shard_map/all_to_all | solution.py:398
  65.4 2.9 %collective-permute-done.3.refs_0_ = f32[128,128]{1,0:T(8,128)S(1)} collective-permute-done((f32[128,128]{1,0:T(8,128)S(1)}, f32[128,128]{1,0:T(8,128)S(1)}, u32[]{:S(2)}, u32[]{:S(2)}) %collective-permute-start.3) | collective-permute-done | bytes 65568 | tf_op jit(solution)/shard_map/ppermute | solution.py:394
  68.3 8.7 %all-to-all-done.1.pieces = f32[4,2,128,128]{3,2,1,0:T(8,128)S(1)} async-done(((f32[4,2,128,128]{3,2,1,0:T(8,128)}), f32[4,2,128,128]{3,2,1,0:T(8,128)S(1)}, u32[]{:S(2)}, u32[]{:S(2)}) %all-to-all-start.1) | async-done | bytes 524320 | tf_op jit(solution)/shard_map/all_to_all | solution.py:398
  77.2 10.4 %all_to_all.55.thetas = f32[16,8,128]{2,1,0:T(8,128)S(1)} all-to-all(f32[16,8,128]{2,1,0:T(8,128)S(1)} %get-tuple-element.49), channel_id=1, replica_groups=mesh['grp'=2,'op'=4,'sec'=2,'sub'=2] {'op','sec','sub'}, dimensions={0} | all-to-all | bytes 131072 | tf_op jit(solution)/shard_map/all_to_all | solution.py:398
  87.5 16.9 %all_to_all.56.sigma = f32[4,2,128,128]{3,2,1,0:T(8,128)S(1)} all-to-all(f32[4,2,128,128]{3,2,1,0:T(8,128)S(1)} %get-tuple-element.48), channel_id=1, replica_groups=mesh['grp'=2,'op'=4,'sec'=2,'sub'=2] {'op'}, dimensions={0} | all-to-all | bytes 1048576 | tf_op jit(solution)/shard_map/all_to_all | solution.py:398
  104.9 6.2 %all_to_all.57.sums = f32[4,8,128]{2,1,0:T(8,128)S(1)} all-to-all(f32[4,8,128]{2,1,0:T(8,128)S(1)} %get-tuple-element.51), channel_id=1, replica_groups=mesh['grp'=2,'op'=4,'sec'=2,'sub'=2] {'sec','sub'}, dimensions={0} | all-to-all | bytes 32768 | tf_op jit(solution)/shard_map/all_to_all | solution.py:398
  111.1 4.6 %copy-done.2 = bf16[96,256,256]{2,1,0:T(8,128)(2,1)S(1)} copy-done((bf16[96,256,256]{2,1,0:T(8,128)(2,1)S(1)}, bf16[96,256,256]{2,1,0:T(8,128)(2,1)}, u32[]{:S(2)}) %copy-start.2) | copy-done | bytes 12582936
  115.7 2.8 %copy-done.5 = bf16[96,128,256]{2,1,0:T(8,128)(2,1)S(1)} copy-done((bf16[96,128,256]{2,1,0:T(8,128)(2,1)S(1)}, bf16[96,128,256]{2,1,0:T(8,128)(2,1)}, u32[]{:S(2)}) %copy-start.5) | copy-done | bytes 6291480
  118.5 3.5 %remote_images.3 = (f32[4,256,128]{2,1,0:T(8,128)S(1)}, bf16[5,256,128]{2,1,0:T(8,128)(2,1)S(1)}, f32[4,256,128]{2,1,0:T(8,128)S(1)}, f32[4,256,128]{2,1,0:T(8,128)S(1)}) custom-call(s32[542]{0:T(1024)S(1)} %get-tuple-element.35.lists, f32[4,256,128]{2,1,0:T(8,128)S(1)} %get-tuple-element.38.held, f32[4,256,128]{2,1,0:T(8,128)S(1)} %bitcast.27, ...), custom_call_target="tpu_custom_call" | custom-call | flops 2147483648 | bytes 4194304 | tf_op jit(solution)/shard_map/remote_images/pallas_call | solution.py:236
  122.0 2.6 %own_first.3 = (f32[4,256,128]{2,1,0:T(8,128)S(1)}, f32[4,256,128]{2,1,0:T(8,128)S(1)}) custom-call(s32[542]{0:T(1024)S(1)} %get-tuple-element.35.lists, bf16[5,256,128]{2,1,0:T(8,128)(2,1)S(1)} %get-tuple-element.53.vector_bf, bf16[96,256,256]{2,1,0:T(8,128)(2,1)S(1)} %copy-done.2, bf16[96,128,256]{2,1,0:T(8,128)(2,1)S(1)} %copy-done.5), custom_call_target="tpu_custom_call" | custom-call | flops 2147483648 | bytes 4194304 | tf_op jit(solution)/shard_map/own_first/pallas_call | solution.py:236
  125.5 4.5 %own_rest.3 = (f32[4,256,128]{2,1,0:T(8,128)S(1)}, f32[4,256,128]{2,1,0:T(8,128)S(1)}) custom-call(s32[542]{0:T(1024)S(1)} %get-tuple-element.35.lists, bf16[5,256,128]{2,1,0:T(8,128)(2,1)S(1)} %get-tuple-element.53.vector_bf, f32[4,256,128]{2,1,0:T(8,128)S(1)} %get-tuple-element.54.keep_in, f32[4,256,128]{2,1,0:T(8,128)S(1)} %get-tuple-element.55.send_in, ...), custom_call_target="tpu_custom_call" | custom-call | flops 4294967296 | bytes 8388608 | tf_op jit(solution)/shard_map/own_rest/pallas_call | solution.py:236
  130.0 4.2 %collective-permute-done.5.after.refs_0_ = f32[4,128,128]{2,1,0:T(8,128)S(1)} collective-permute-done((f32[4,128,128]{2,1,0:T(8,128)S(1)}, f32[4,128,128]{2,1,0:T(8,128)S(1)}, u32[]{:S(2)}, u32[]{:S(2)}) %collective-permute-start.5) | collective-permute-done | bytes 262176 | tf_op jit(solution)/shard_map/ppermute | solution.py:394
  134.2 3.4 %all-to-all-start.7 = ((f32[4,1,128,128]{3,2,1,0:T(8,128)}), f32[4,1,128,128]{3,2,1,0:T(8,128)S(1)}, u32[]{:S(2)}, u32[]{:S(2)}) async-start(f32[4,1,128,128]{3,2,1,0:T(8,128)} %get-tuple-element.61), calls=%async_computation.7 | async-start | bytes 524288 | tf_op jit(solution)/shard_map/all_to_all | solution.py:398
  138.5 8.9 %all-to-all-done.7.parts = f32[4,1,128,128]{3,2,1,0:T(8,128)S(1)} async-done(((f32[4,1,128,128]{3,2,1,0:T(8,128)}), f32[4,1,128,128]{3,2,1,0:T(8,128)S(1)}, u32[]{:S(2)}, u32[]{:S(2)}) %all-to-all-start.7) | async-done | bytes 262176 | tf_op jit(solution)/shard_map/all_to_all | solution.py:398
  147.4 3.5 %all-to-all-start.6 = ((f32[4,2,128,128]{3,2,1,0:T(8,128)}), f32[4,2,128,128]{3,2,1,0:T(8,128)S(1)}, u32[]{:S(2)}, u32[]{:S(2)}) async-start(f32[4,2,128,128]{3,2,1,0:T(8,128)} %combine.3), calls=%async_computation.6 | async-start | bytes 1048576 | tf_op jit(solution)/shard_map/all_to_all | solution.py:398
  151.3 4.0 %collective-permute-done.7.refs_0_ = f32[128,128]{1,0:T(8,128)S(1)} collective-permute-done((f32[128,128]{1,0:T(8,128)S(1)}, f32[128,128]{1,0:T(8,128)S(1)}, u32[]{:S(2)}, u32[]{:S(2)}) %collective-permute-start.7) | collective-permute-done | bytes 65568 | tf_op jit(solution)/shard_map/ppermute | solution.py:394
  155.3 9.3 %all-to-all-done.6.pieces = f32[4,2,128,128]{3,2,1,0:T(8,128)S(1)} async-done(((f32[4,2,128,128]{3,2,1,0:T(8,128)}), f32[4,2,128,128]{3,2,1,0:T(8,128)S(1)}, u32[]{:S(2)}, u32[]{:S(2)}) %all-to-all-start.6) | async-done | bytes 524320 | tf_op jit(solution)/shard_map/all_to_all | solution.py:398
  164.7 9.5 %all_to_all.58.thetas = f32[16,8,128]{2,1,0:T(8,128)S(1)} all-to-all(f32[16,8,128]{2,1,0:T(8,128)S(1)} %get-tuple-element.63), channel_id=1, replica_groups=mesh['grp'=2,'op'=4,'sec'=2,'sub'=2] {'op','sec','sub'}, dimensions={0} | all-to-all | bytes 131072 | tf_op jit(solution)/shard_map/all_to_all | solution.py:398
  174.2 16.9 %all_to_all.59.sigma = f32[4,2,128,128]{3,2,1,0:T(8,128)S(1)} all-to-all(f32[4,2,128,128]{3,2,1,0:T(8,128)S(1)} %get-tuple-element.62), channel_id=1, replica_groups=mesh['grp'=2,'op'=4,'sec'=2,'sub'=2] {'op'}, dimensions={0} | all-to-all | bytes 1048576 | tf_op jit(solution)/shard_map/all_to_all | solution.py:398
  191.6 6.2 %all_to_all.60.sums = f32[4,8,128]{2,1,0:T(8,128)S(1)} all-to-all(f32[4,8,128]{2,1,0:T(8,128)S(1)} %get-tuple-element.65), channel_id=1, replica_groups=mesh['grp'=2,'op'=4,'sec'=2,'sub'=2] {'sec','sub'}, dimensions={0} | all-to-all | bytes 32768 | tf_op jit(solution)/shard_map/all_to_all | solution.py:398
  (40 shorter events, 12.6 us)
Async XLA Ops:
  0.6 1.0 copy-start.7
  1.7 20.8 %copy-start.8 = (f32[4,256,128]{2,1,0:T(8,128)S(1)}, f32[4,256,128]{2,1,0:T(8,128)}, u32[]{:S(2)}) copy-start(f32[4,256,128]{2,1,0:T(8,128)} %wave.3) | copy-start | bytes 1572868
  2.5 19.9 %all-to-all-start = ((f32[4,8,128]{2,1,0:T(8,128)}), f32[4,8,128]{2,1,0:T(8,128)S(1)}, u32[]{:S(2)}, u32[]{:S(2)}) async-start(f32[4,8,128]{2,1,0:T(8,128)} %square_sum.1), calls=%async_computation | async-start | bytes 32768 | tf_op jit(solution)/shard_map/all_to_all | solution.py:398
  15.3 4.5 %copy-start = (bf16[96,256,256]{2,1,0:T(8,128)(2,1)}, bf16[96,256,256]{2,1,0:T(8,128)(2,1)S(1)}, u32[]{:S(2)}) copy-start(bf16[96,256,256]{2,1,0:T(8,128)(2,1)S(1)} %get-tuple-element.36.left) | copy-start | bytes 37748740
  19.9 2.6 %copy-start.3 = (bf16[96,128,256]{2,1,0:T(8,128)(2,1)}, bf16[96,128,256]{2,1,0:T(8,128)(2,1)S(1)}, u32[]{:S(2)}) copy-start(bf16[96,128,256]{2,1,0:T(8,128)(2,1)S(1)} %get-tuple-element.37.right) | copy-start | bytes 18874372
  22.5 4.6 %copy-start.1 = (bf16[96,256,256]{2,1,0:T(8,128)(2,1)S(1)}, bf16[96,256,256]{2,1,0:T(8,128)(2,1)}, u32[]{:S(2)}) copy-start(bf16[96,256,256]{2,1,0:T(8,128)(2,1)} %copy-done) | copy-start | bytes 37748740
  27.1 2.8 %copy-start.4 = (bf16[96,128,256]{2,1,0:T(8,128)(2,1)S(1)}, bf16[96,128,256]{2,1,0:T(8,128)(2,1)}, u32[]{:S(2)}) copy-start(bf16[96,128,256]{2,1,0:T(8,128)(2,1)} %copy-done.3) | copy-start | bytes 18874372
  33.2 3.2 %collective-permute-start = (f32[4,256,128]{2,1,0:T(8,128)S(1)}, f32[4,256,128]{2,1,0:T(8,128)S(1)}, u32[]{:S(2)}, u32[]{:S(2)}) collective-permute-start(f32[4,256,128]{2,1,0:T(8,128)S(1)} %get-tuple-element.43), channel_id=1, source_target_pairs={{0,1},{1,0},{2,3},{3,2},{4,5},{5,4},{6,7},{7,6},{8,9},{9,8},{10,11... | collective-permute-start | bytes 1572872 | tf_op jit(solution)/shard_map/ppermute | solution.py:394
  37.2 8.5 %collective-permute-start.1 = (f32[4,128,128]{2,1,0:T(8,128)S(1)}, f32[4,128,128]{2,1,0:T(8,128)S(1)}, u32[]{:S(2)}, u32[]{:S(2)}) collective-permute-start(f32[4,128,128]{2,1,0:T(8,128)S(1)} %get-tuple-element.44.after), channel_id=1, source_target_pairs={{0,2},{2,0},{1,3},{3,1},{4,6},{6,4},{5,7},{7,5},{8,10},{10,8},{9,1... | collective-permute-start | bytes 786440 | tf_op jit(solution)/shard_map/ppermute | solution.py:394
  38.9 38.1 %copy-start.6 = (f32[4,256,128]{2,1,0:T(8,128)S(1)}, f32[4,256,128]{2,1,0:T(8,128)}, u32[]{:S(2)}) copy-start(f32[4,256,128]{2,1,0:T(8,128)} %param.6) | copy-start | bytes 1572868
  45.7 5.2 %collective-permute-start.2 = (f32[4,256,128]{2,1,0:T(8,128)S(1)}, f32[4,256,128]{2,1,0:T(8,128)S(1)}, u32[]{:S(2)}, u32[]{:S(2)}) collective-permute-start(f32[4,256,128]{2,1,0:T(8,128)S(1)} %pass_after.2), channel_id=1, source_target_pairs={{0,1},{1,0},{2,3},{3,2},{4,5},{5,4},{6,7},{7,6},{8,9},{9,8},{10,11... | collective-permute-start | bytes 1572872 | tf_op jit(solution)/shard_map/ppermute | solution.py:394
  45.8 14.6 %all-to-all-start.2 = ((f32[4,1,128,128]{3,2,1,0:T(8,128)}), f32[4,1,128,128]{3,2,1,0:T(8,128)S(1)}, u32[]{:S(2)}, u32[]{:S(2)}) async-start(f32[4,1,128,128]{3,2,1,0:T(8,128)} %get-tuple-element.47), calls=%async_computation.2 | async-start | bytes 524288 | tf_op jit(solution)/shard_map/all_to_all | solution.py:398
  60.4 16.6 %all-to-all-start.1 = ((f32[4,2,128,128]{3,2,1,0:T(8,128)}), f32[4,2,128,128]{3,2,1,0:T(8,128)S(1)}, u32[]{:S(2)}, u32[]{:S(2)}) async-start(f32[4,2,128,128]{3,2,1,0:T(8,128)} %combine.2), calls=%async_computation.1 | async-start | bytes 1048576 | tf_op jit(solution)/shard_map/all_to_all | solution.py:398
  63.9 4.3 %collective-permute-start.3 = (f32[128,128]{1,0:T(8,128)S(1)}, f32[128,128]{1,0:T(8,128)S(1)}, u32[]{:S(2)}, u32[]{:S(2)}) collective-permute-start(f32[128,128]{1,0:T(8,128)S(1)} %sum_parts.2), channel_id=1, source_target_pairs={{0,2},{2,0},{1,3},{3,1},{4,6},{6,4},{5,7},{7,5},{8,10},{10,8},{9,1... | collective-permute-start | bytes 196616 | tf_op jit(solution)/shard_map/ppermute | solution.py:394
  111.1 4.6 %copy-start.2 = (bf16[96,256,256]{2,1,0:T(8,128)(2,1)S(1)}, bf16[96,256,256]{2,1,0:T(8,128)(2,1)}, u32[]{:S(2)}) copy-start(bf16[96,256,256]{2,1,0:T(8,128)(2,1)} %copy-done) | copy-start | bytes 37748740
  115.7 2.8 %copy-start.5 = (bf16[96,128,256]{2,1,0:T(8,128)(2,1)S(1)}, bf16[96,128,256]{2,1,0:T(8,128)(2,1)}, u32[]{:S(2)}) copy-start(bf16[96,128,256]{2,1,0:T(8,128)(2,1)} %copy-done.3) | copy-start | bytes 18874372
  121.9 2.7 %collective-permute-start.4 = (f32[4,256,128]{2,1,0:T(8,128)S(1)}, f32[4,256,128]{2,1,0:T(8,128)S(1)}, u32[]{:S(2)}, u32[]{:S(2)}) collective-permute-start(f32[4,256,128]{2,1,0:T(8,128)S(1)} %get-tuple-element.57), channel_id=1, source_target_pairs={{0,1},{1,0},{2,3},{3,2},{4,5},{5,4},{6,7},{7,6},{8,9},{9,8},{10,11... | collective-permute-start | bytes 1572872 | tf_op jit(solution)/shard_map/ppermute | solution.py:394
  125.4 8.7 %collective-permute-start.5 = (f32[4,128,128]{2,1,0:T(8,128)S(1)}, f32[4,128,128]{2,1,0:T(8,128)S(1)}, u32[]{:S(2)}, u32[]{:S(2)}) collective-permute-start(f32[4,128,128]{2,1,0:T(8,128)S(1)} %get-tuple-element.58.after), channel_id=1, source_target_pairs={{0,2},{2,0},{1,3},{3,1},{4,6},{6,4},{5,7},{7,5},{8,10},{10,8},{9,1... | collective-permute-start | bytes 786440 | tf_op jit(solution)/shard_map/ppermute | solution.py:394
  134.2 3.5 %collective-permute-start.6 = (f32[4,256,128]{2,1,0:T(8,128)S(1)}, f32[4,256,128]{2,1,0:T(8,128)S(1)}, u32[]{:S(2)}, u32[]{:S(2)}) collective-permute-start(f32[4,256,128]{2,1,0:T(8,128)S(1)} %pass_after.3), channel_id=1, source_target_pairs={{0,1},{1,0},{2,3},{3,2},{4,5},{5,4},{6,7},{7,6},{8,9},{9,8},{10,11... | collective-permute-start | bytes 1572872 | tf_op jit(solution)/shard_map/ppermute | solution.py:394
  134.2 13.2 %all-to-all-start.7 = ((f32[4,1,128,128]{3,2,1,0:T(8,128)}), f32[4,1,128,128]{3,2,1,0:T(8,128)S(1)}, u32[]{:S(2)}, u32[]{:S(2)}) async-start(f32[4,1,128,128]{3,2,1,0:T(8,128)} %get-tuple-element.61), calls=%async_computation.7 | async-start | bytes 524288 | tf_op jit(solution)/shard_map/all_to_all | solution.py:398
  147.4 17.1 %all-to-all-start.6 = ((f32[4,2,128,128]{3,2,1,0:T(8,128)}), f32[4,2,128,128]{3,2,1,0:T(8,128)S(1)}, u32[]{:S(2)}, u32[]{:S(2)}) async-start(f32[4,2,128,128]{3,2,1,0:T(8,128)} %combine.3), calls=%async_computation.6 | async-start | bytes 1048576 | tf_op jit(solution)/shard_map/all_to_all | solution.py:398
  150.9 4.3 %collective-permute-start.7 = (f32[128,128]{1,0:T(8,128)S(1)}, f32[128,128]{1,0:T(8,128)S(1)}, u32[]{:S(2)}, u32[]{:S(2)}) collective-permute-start(f32[128,128]{1,0:T(8,128)S(1)} %sum_parts.3), channel_id=1, source_target_pairs={{0,2},{2,0},{1,3},{3,1},{4,6},{6,4},{5,7},{7,5},{8,10},{10,8},{9,1... | collective-permute-start | bytes 196616 | tf_op jit(solution)/shard_map/ppermute | solution.py:394

commit v5 on v3

--- a/solution.py
+++ b/solution.py
@@ -9,6 +9,7 @@
 
 ITERS = 2
 GROUP = 4
+EARLY = 3
 REMOTE, OWN = 0, 1
 VMEM = pl.BlockSpec(memory_space=pltpu.VMEM)
 SMEM = pl.BlockSpec(memory_space=pltpu.SMEM)
@@ -143,14 +144,14 @@
     return total
 
 
-def multiply_terms(region, places, lists, left, right, vector_bf, product, keep, send):
+def multiply_terms(region, turns, places, lists, left, right, vector_bf, product, keep, send):
     cap, slot, groups, _ = places
     unit = code_unit(vector_bf.shape[0] - 1)
     my_sub = lax.axis_index("sub")
     half = keep.shape[2]
     count = lists[groups + region]
-    keep[...] = jnp.zeros_like(keep)
-    send[...] = jnp.zeros_like(send)
+    begin = jnp.minimum(turns[0], count)
+    end = count if turns[1] is None else jnp.minimum(turns[1], count)
 
     def tile(at):
         return lax.shift_right_logical(lists[at], unit.bit_length() - 1)
@@ -173,17 +174,17 @@
             keep[n] += jnp.where(my_sub == 0, low, high)
             send[n] += jnp.where(my_sub == 0, high, low)
 
-    @pl.when(count > 0)
+    @pl.when(end > begin)
     def _():
-        first(0)
+        first(begin)
 
         def turn(group, carry):
             second(group - 1)
             first(group)
             return carry
 
-        lax.fori_loop(1, count, turn, 0)
-        second(count - 1)
+        lax.fori_loop(begin + 1, end, turn, 0)
+        second(end - 1)
 
 
 def round_vector(vector, vector_bf):
@@ -192,50 +193,56 @@
     vector_bf[blocks] = jnp.zeros(vector_bf.shape[1:], jnp.bfloat16)
 
 
+def remote_turns(places, lists, left, right, vector, vector_bf, keep, send, product):
+    round_vector(vector, vector_bf)
+    keep[...] = jnp.zeros_like(keep)
+    send[...] = jnp.zeros_like(send)
+    multiply_terms(REMOTE, (0, None), places, lists, left, right, vector_bf, product, keep, send)
+
+
 def start_kernel(entries, norms, places, lists, wave, *refs):
-    norm_refs, (left, right, vector, keep, send, vector_bf, product) = refs[:norms], refs[norms:]
+    norm_refs, (left, right, vector, *refs) = refs[:norms], refs[norms:]
     length = jnp.sqrt(added(norm_refs)[:1, :1] / entries)
     vector[...] = wave[...] / length[None]
-    round_vector(vector, vector_bf)
-    multiply_terms(REMOTE, places, lists, left, right, vector_bf, product, keep, send)
+    remote_turns(places, lists, left, right, vector, *refs)
 
 
 def refined(entries, held, correction, sum_refs):
-    sums = added(sum_refs) / entries
-    along, square, own = sums[0:1, :1], sums[1:2, :1], sums[2:3, :1]
+    total = added(sum_refs) / entries
+    along, square, own = total[0:1, :1], total[1:2, :1], total[2:3, :1]
     length = jnp.sqrt((1.0 + along) * (1.0 + along) * own - 2.0 * (1.0 + along) * along + square)
     return (held[...] - (correction[...] - along[None] * held[...])) / length[None]
 
 
-def resume_kernel(entries, places, lists, held, correction, *refs):
-    sum_refs, (left, right, vector, keep, send, vector_bf, product) = refs[:-7], refs[-7:]
+def resume_kernel(entries, sums, places, lists, held, correction, *refs):
+    sum_refs, (left, right, vector, *refs) = refs[:sums], refs[sums:]
     vector[...] = refined(entries, held, correction, sum_refs)
-    round_vector(vector, vector_bf)
-    multiply_terms(REMOTE, places, lists, left, right, vector_bf, product, keep, send)
-
-
-def own_kernel(places, lists, vector, after, left, right, keep, send, vector_bf, product):
-    round_vector(vector, vector_bf)
-    multiply_terms(OWN, places, lists, left, right, vector_bf, product, keep, send)
-
-
-def images(kernel, slots, with_vector, name, lists, operands, left, right, after=()):
-    half, rows = right.shape[1:]
-    vector = operands[0]
-    out = (f32(slots, rows, half),) * 2
-    if with_vector:
-        out = (f32(*vector.shape), *out)
+    remote_turns(places, lists, left, right, vector, *refs)
+
+
+def own_first_kernel(places, lists, vector_bf, left, right, keep, send, product):
+    keep[...] = jnp.zeros_like(keep)
+    send[...] = jnp.zeros_like(send)
+    multiply_terms(OWN, (0, EARLY), places, lists, left, right, vector_bf, product, keep, send)
+
+
+def own_rest_kernel(places, lists, vector_bf, keep_in, send_in, after, left, right, keep, send, product):
+    keep[...] = keep_in[...]
+    send[...] = send_in[...]
+    multiply_terms(OWN, (EARLY, None), places, lists, left, right, vector_bf, product, keep, send)
+
+
+def images(kernel, out_shape, name, lists, operands, left, right, after=(), turns=4):
+    rows = left.shape[1]
+    work = turns * GROUP * 2 * 8 * rows * rows * rows // 4
     return pl.pallas_call(
         kernel,
-        out_shape=out,
+        out_shape=out_shape,
         in_specs=[SMEM] + [VMEM] * len(operands) + [ANY] * len(after) + [VMEM] * 2,
-        out_specs=(VMEM,) * len(out),
-        scratch_shapes=[
-            pltpu.VMEM((vector.shape[0] + 1, rows, half), jnp.bfloat16),
-            pltpu.VMEM((GROUP, rows, rows), jnp.bfloat16),
-        ],
+        out_specs=(VMEM,) * len(out_shape),
+        scratch_shapes=[pltpu.VMEM((GROUP, rows, rows), jnp.bfloat16)],
         compiler_params=limit(12),
-        cost_estimate=pl.CostEstimate(flops=6 * 10**9, bytes_accessed=20 * 2**20, transcendentals=0),
+        cost_estimate=pl.CostEstimate(flops=2 * work, bytes_accessed=turns * 2**20, transcendentals=0),
         name=name,
     )(
         lists,
@@ -266,88 +273,88 @@
 
 
 def part_kernel(aways, keep, landed, *outs):
-    wholes, pieces = outs[:aways], outs[aways:]
-    ops = len(pieces)
-    my_op = lax.axis_index("op")
     for away in range(aways):
-        wholes[away][...] = keep[away, 0] + landed[away, 0]
-        for turn in range(ops):
-            at = lax.rem(my_op + turn, ops)
-            pieces[turn][away] = keep[away, 1, at] + landed[away, 1, at]
-
-
-def part(keep, landed, aways, split):
-    _, ops, rows, half = split
-    shape = (aways, *split)
-    outs = call(
+        for side in range(2):
+            outs[2 * away + side][...] = keep[away, side] + landed[away, side]
+
+
+def part(keep, landed, aways):
+    blocks, rows, half = keep.shape
+    shape = (aways, 2, blocks // aways // 2, rows, half)
+    return call(
         functools.partial(part_kernel, aways),
-        (f32(ops, rows, half),) * aways + (f32(aways, rows, half),) * ops,
+        (f32(*shape[2:]),) * (2 * aways),
         (keep.reshape(shape), landed.reshape(shape)),
         "part",
     )
-    return outs[:aways], outs[aways:]
-
-
-def sum_kernel(parts, *refs):
-    for away, out in enumerate(refs[parts:]):
-        total = refs[0][away]
-        for ref in refs[1:parts]:
-            total = total + ref[away]
-        out[...] = total
-
-
-def sum_parts(parts):
-    aways, rows, half = parts[0].shape
-    return call(functools.partial(sum_kernel, len(parts)), (f32(rows, half),) * aways, parts, "sum_parts")
-
-
-def combine_kernel(arrived, keep, landed, *refs):
-    wholes, outs = refs[:arrived], refs[arrived:]
+
+
+def pass_kernel(count, *refs):
+    for value, out in zip(refs[:count], refs[count + 1 :]):
+        out[...] = value[...]
+
+
+def pass_after(values, after):
+    return pl.pallas_call(
+        functools.partial(pass_kernel, len(values)),
+        out_shape=tuple(f32(*value.shape) for value in values),
+        in_specs=[VMEM] * len(values) + [ANY],
+        out_specs=(VMEM,) * len(values),
+        compiler_params=limit(4),
+        name="pass_after",
+    )(*values, after)
+
+
+def combine_kernel(arrived, earlier, side, vector, diagonal, keep, landed, *refs):
+    wholes, outs = refs[:arrived], refs[arrived + earlier :]
     ops = len(outs)
+    rows, half = keep.shape[2:]
     my_op = lax.axis_index("op")
+    held = vector[side, my_op]
+    inner = diagonal[side, my_op] * held * held
     for turn in range(ops):
         at = lax.rem(my_op + turn, ops)
-        total = keep[0, at] + landed[0, at]
+        total = keep[side, at] + landed[side, at]
         for whole in wholes:
             total = total + whole[at]
-        outs[turn][0] = total
-        outs[turn][1] = keep[1, at] + landed[1, at]
-
-
-def combine(keep, landed, wholes, split):
-    _, ops, rows, half = split
-    return call(
-        functools.partial(combine_kernel, len(wholes)),
-        (f32(2, rows, half),) * ops,
-        (keep.reshape(split), landed.reshape(split), *wholes),
-        "combine",
-    )
-
-
-def sigma_kernel(parts, vector, diagonal, *refs):
-    pieces, arrived, (sigma, inner) = refs[:parts], refs[parts:-2], refs[-2:]
+        outs[turn][:rows] = total
+        inner = inner + vector[side, at] * total
+    share = jnp.sum(inner.reshape(rows // 8, 8, half), axis=0)
+    for turn in range(ops):
+        outs[turn][rows:] = share
+
+
+def combine(side, vector, diagonal, keep, landed, wholes, earlier):
+    _, ops, rows, half = vector.shape
+    operands = [vector, diagonal, keep.reshape(vector.shape), landed.reshape(vector.shape)]
+    operands += [whole.reshape(ops, rows, half) for whole in wholes]
+    return pl.pallas_call(
+        functools.partial(combine_kernel, len(wholes), len(earlier), side),
+        out_shape=(f32(rows + 8, half),) * ops,
+        in_specs=[VMEM] * len(operands) + [ANY] * len(earlier),
+        out_specs=(VMEM,) * ops,
+        compiler_params=limit(4),
+        name="combine",
+    )(*operands, *earlier)
+
+
+def sigma_kernel(vector, diagonal, *refs):
+    pieces, (sigma, inner) = refs[:-2], refs[-2:]
+    ops = len(pieces) // 2
+    rows = sigma.shape[1]
     my_op = lax.axis_index("op")
-    inner_sum = jnp.float32(0)
+    shares = jnp.zeros((8, sigma.shape[2]), jnp.float32)
     for side in range(2):
-        total = pieces[0][side]
-        for piece in pieces[1:]:
-            total = total + piece[side]
-        if side == 1:
-            total = total + added(arrived)
-        held = vector[side, my_op]
-        total = diagonal[side, my_op] * held + total
-        sigma[side] = total
-        inner_sum += jnp.sum(held * total)
-    inner[...] = jnp.full(inner.shape, inner_sum)
-
-
-def sigma_share(vector, diagonal, pieces, arrived):
+        total = added(pieces[side * ops : (side + 1) * ops])
+        sigma[side] = diagonal[side, my_op] * vector[side, my_op] + total[:rows]
+        shares = shares + total[rows:]
+    inner[...] = jnp.full(inner.shape, jnp.sum(shares))
+
+
+def sigma_share(vector, diagonal, pieces):
     _, ops, rows, half = vector.shape
     return call(
-        functools.partial(sigma_kernel, len(pieces)),
-        (f32(2, rows, half), f32(8, 128)),
-        (vector, diagonal, *pieces, *arrived),
-        "sigma",
+        sigma_kernel, (f32(2, rows, half), f32(8, 128)), (vector, diagonal, *pieces), "sigma"
     )
 
 
@@ -356,7 +363,7 @@
     my_op = lax.axis_index("op")
     ritz[...] = added(theta_refs) / entries
     theta = ritz[:1, :1]
-    totals = [jnp.float32(0)] * 3
+    totals = [0.0] * 3
     for turn in range(ops):
         at = lax.rem(my_op + ops - turn, ops)
         for side in range(2):
@@ -364,10 +371,10 @@
             value = (spread[turn][side] - theta * held) / (1.0 + jnp.abs(diag - theta))
             correction[side, at] = value
             for index, term in enumerate((held * value, value * value, held * held)):
-                totals[index] += jnp.sum(term)
+                totals[index] = totals[index] + term
     sums[...] = jnp.zeros_like(sums)
     for index, value in enumerate(totals):
-        sums[index : index + 1] = jnp.full((1, sums.shape[1]), value)
+        sums[index : index + 1] = jnp.full((1, sums.shape[1]), jnp.sum(value))
 
 
 def correct(entries, vector, diagonal, spread, thetas):
@@ -404,6 +411,10 @@
 
 def from_all(array, axis):
     return [array, *[shift(array, axis, k) for k in range(1, lax.axis_size(axis))]]
+
+
+def sector_sums(array):
+    return from_all(add(from_all(array, "sub")), "sec")
 
 
 def per_device(wavefunction, diagonal, left_env, right_env, targets):
@@ -416,39 +427,47 @@
     split = (2, ops, blocks * tile // ops // 2, half)
     places = list_places(terms * blocks, secs * blocks)
     aways = secs - 1
+    rounded = jax.ShapeDtypeStruct((blocks + 1, tile, half), jnp.bfloat16)
+    whole, own_out = f32(blocks, tile, half), (f32(blocks, tile, half),) * 2
+    remote_out = (whole, rounded) + (f32(aways * blocks, tile, half),) * 2
+    own_first = functools.partial(own_first_kernel, places)
+    own_rest = functools.partial(own_rest_kernel, places)
     diagonal = diagonal.reshape(split)
-    norms = from_all(square_sum(wavefunction), ("sec", "sub"))
+    norms = sector_sums(square_sum(wavefunction))
     lists, left, right = load(secs, places, targets, left, right)
     start = functools.partial(start_kernel, entries, len(norms), places)
-    vector, keep, send = images(
-        start, aways * blocks, True, "remote_images", lists, (wavefunction, *norms), left, right
+    vector, vector_bf, keep, send = images(
+        start, remote_out, "remote_images", lists, (wavefunction, *norms), left, right
     )
     ritz = []
     for turn_index in range(ITERS):
-        wholes, shares = part(keep, shift(send, "sub", 1), aways, split)
-        crossed = [shift(wholes[r - 1], "sec", r) for r in range(1, secs)]
-        landed = [shift(shares[k], "op", k) for k in range(1, ops)]
-        own = functools.partial(own_kernel, places)
+        landed = shift(send, "sub", 1)
+        own_parts = images(own_first, own_out, "own_first", lists, (vector_bf,), left, right)
+        halves = part(keep, landed, aways)
+        crossed = [shift(halves[2 * r - 2], "sec", r) for r in range(1, secs)]
         keep, send = images(
-            own, blocks, False, "own_images", lists, (vector,), left, right, after=(wholes[0],)
+            own_rest, own_out, "own_rest", lists, (vector_bf, *own_parts), left, right, after=(halves[0],), turns=8
         )
-        reduced = sum_parts((shares[0], *landed))
-        arrived = [shift(reduced[r - 1], "sec", r) for r in range(1, secs)]
-        pieces = combine(keep, shift(send, "sub", 1), crossed, split)
-        pieces = [pieces[0], *[shift(pieces[k], "op", k) for k in range(1, ops)]]
+        send, *others = pass_after((send, *halves[1::2]), crossed[-1])
+        crossed_later = [shift(other, "sec", r) for r, other in enumerate(others, 1)]
+        landed = shift(send, "sub", 1)
         held = vector.reshape(split)
-        sigma, inner = sigma_share(held, diagonal, pieces, arrived)
+        pieces = []
+        for side, wholes in enumerate((crossed, crossed_later)):
+            outs = combine(side, held, diagonal, keep, landed, wholes, pieces[1:])
+            pieces += [outs[0], *[shift(outs[k], "op", k) for k in range(1, ops)]]
+        sigma, inner = sigma_share(held, diagonal, pieces)
         spread = from_all(sigma, "op")
-        thetas = from_all(add(from_all(inner, ("sec", "sub"))), "op")
+        thetas = sector_sums(inner)
         correction, sums, theta = correct(entries, held, diagonal, spread, thetas)
         ritz.append(theta)
-        sums = from_all(sums, ("sec", "sub"))
+        sums = sector_sums(sums)
         correction = correction.reshape(vector.shape)
         if turn_index < ITERS - 1:
-            resume = functools.partial(resume_kernel, entries, places)
+            resume = functools.partial(resume_kernel, entries, len(sums), places)
             operands = (vector, correction, *sums)
-            vector, keep, send = images(
-                resume, aways * blocks, True, "remote_images", lists, operands, left, right
+            vector, vector_bf, keep, send = images(
+                resume, remote_out, "remote_images", lists, operands, left, right
             )
     return finish(entries, vector, correction, sums, ritz)
 

time: 132 us -> 124 us (0.939)
  starting transfers between devices: 55.9 us -> 36.9 us
  waiting for transfers between devices: 42.5 us -> 50.6 us
  Pallas kernels: 30.8 us -> 32.9 us
    ppermute x47 -> x36, starting transfers between devices: 55.9 us -> 36.9 us  [shift(): lax.ppermute(array, axis, [(i, (i + turn) % count) for i in range(count)])]
    ppermute x47 -> x36, waiting for transfers between devices: 42.5 us -> 50.6 us  [shift(): lax.ppermute(array, axis, [(i, (i + turn) % count) for i in range(count)])]
    pallas_call x4 -> x12, Pallas kernels: 20.2 us -> 22.5 us  [the longest x6 22 us: images(): pl.pallas_call(kernel, out_shape=out_shape, in_specs=[SMEM] + [VMEM] * le...]
  transfers between devices with their start and end apart: 47 -> 36, of which waited for: 27 -> 27; matrix products, arithmetic and copies ran while one was open for 1% -> 1% of each run, Pallas kernels for 6% -> 20%
where the time goes in v5:
time: 124 us; the launch traced here: 123 us
  waiting for transfers between devices  50.6 us (41%)
  starting transfers between devices  36.9 us (30%)
  Pallas kernels  32.9 us (27%)
  local copies, waits for them, and re-layouts  1.8 us (1%)
    ppermute x36, waiting for transfers between devices, shift(): lax.ppermute(array, axis, [(i, (i + turn) % count) for i in range(count)])  50.6 us
    ppermute x36, starting transfers between devices, shift(): lax.ppermute(array, axis, [(i, (i + turn) % count) for i in range(count)])  36.9 us
    pallas_call x6, Pallas kernels, images(): pl.pallas_call(kernel, out_shape=out_shape, in_specs=[SMEM] + [VMEM] * le...  22 us
    pallas_call x1, Pallas kernels, load(): pl.pallas_call(functools.partial(load_kernel, secs, places), out_shape=(j...  7.84 us
  transfers between devices with their start and end apart: 36, of which 27 were waited for; matrix products, arithmetic and copies ran while one was open for 1% of the time, Pallas kernels for 20%

profile of v5, /device:TPU:0, one launch (start us, length us, event | category | flops | bytes accessed | tf_op | source)
XLA Modules:
  0.0 123.1 jit_solution(11913592019884367483)
XLA Ops:
  3.3 2.8 %collective-permute-start.1 = (f32[8,128]{1,0:T(8,128)S(1)}, f32[8,128]{1,0:T(8,128)S(1)}, u32[]{:S(2)}, u32[]{:S(2)}) collective-permute-start(f32[8,128]{1,0:T(8,128)S(1)} %add.5.refs_0_), channel_id=1, source_target_pairs={{0,2},{2,0},{1,3},{3,1},{4,6},{6,4},{5,7},{7,5},{8,10},{10,8},{9,1... | collective-permute-start | bytes 12296 | tf_op jit(solution)/shard_map/ppermute | solution.py:409
  6.9 7.8 %load.1 = (s32[542]{0:T(1024)S(1)}, bf16[96,256,256]{2,1,0:T(8,128)(2,1)S(1)}, bf16[96,128,256]{2,1,0:T(8,128)(2,1)S(1)}) custom-call(s32[24,4]{1,0:T(8,128)S(1)} %copy.7.targets, bf16[96,256,256]{2,1,0:T(8,128)(2,1)} %bitcast.53, bf16[96,128,256]{2,1,0:T(8,128)(2,1)} %bitcast.54), custom_call_target="tpu_custom_call" | custom-call | bytes 41943040 | tf_op jit(solution)/shard_map/load/pallas_call | solution.py:101
  14.7 2.8 %remote_images.2 = (f32[4,256,128]{2,1,0:T(8,128)S(1)}, bf16[5,256,128]{2,1,0:T(8,128)(2,1)S(1)}, f32[4,256,128]{2,1,0:T(8,128)S(1)}, f32[4,256,128]{2,1,0:T(8,128)S(1)}) custom-call(s32[542]{0:T(1024)S(1)} %get-tuple-element.55.lists, f32[4,256,128]{2,1,0:T(8,128)S(1)} %copy-done.2, f32[8,128]{1,0:T(8,128)S(1)} %add.5.refs_0_, ...), custom_call_target="tpu_custom_call" | custom-call | flops 2147483648 | bytes 4194304 | tf_op jit(solution)/shard_map/remote_images/pallas_call | solution.py:238
  17.6 2.7 %own_first.2 = (f32[4,256,128]{2,1,0:T(8,128)S(1)}, f32[4,256,128]{2,1,0:T(8,128)S(1)}) custom-call(s32[542]{0:T(1024)S(1)} %get-tuple-element.55.lists, bf16[5,256,128]{2,1,0:T(8,128)(2,1)S(1)} %get-tuple-element.59.vector_bf, bf16[96,256,256]{2,1,0:T(8,128)(2,1)S(1)} %get-tuple-element.56.refs_2_.left, ...), custom_call_target="tpu_custom_call" | custom-call | flops 2147483648 | bytes 4194304 | tf_op jit(solution)/shard_map/own_first/pallas_call | solution.py:238
  21.3 5.4 %own_rest.2 = (f32[4,256,128]{2,1,0:T(8,128)S(1)}, f32[4,256,128]{2,1,0:T(8,128)S(1)}) custom-call(s32[542]{0:T(1024)S(1)} %get-tuple-element.55.lists, bf16[5,256,128]{2,1,0:T(8,128)(2,1)S(1)} %get-tuple-element.59.vector_bf, f32[4,256,128]{2,1,0:T(8,128)S(1)} %get-tuple-element.60.keep_in, f32[4,256,128]{2,1,0:T(8,128)S(1)} %get-tuple-element.61.send_in, ...), custom_call_target="tpu_custom_call" | custom-call | flops 4294967296 | bytes 8388608 | tf_op jit(solution)/shard_map/own_rest/pallas_call | solution.py:238
  26.7 2.5 %collective-permute-done.3.refs_2_ = f32[2,256,128]{2,1,0:T(8,128)S(1)} collective-permute-done((f32[2,256,128]{2,1,0:T(8,128)S(1)}, f32[2,256,128]{2,1,0:T(8,128)S(1)}, u32[]{:S(2)}, u32[]{:S(2)}) %collective-permute-start.3) | collective-permute-done | bytes 262176 | tf_op jit(solution)/shard_map/ppermute | solution.py:409
  31.4 2.3 %collective-permute-start.5 = (f32[136,128]{1,0:T(8,128)S(1)}, f32[136,128]{1,0:T(8,128)S(1)}, u32[]{:S(2)}, u32[]{:S(2)}) collective-permute-start(f32[136,128]{1,0:T(8,128)S(1)} %get-tuple-element.70), channel_id=1, source_target_pairs={{0,4},{4,8},{8,12},{12,0},{1,5},{5,9},{9,13},{13,1},{2,6},{6,10},{... | collective-permute-start | bytes 208904 | tf_op jit(solution)/shard_map/ppermute | solution.py:409
  33.6 2.6 %collective-permute-start.6 = (f32[136,128]{1,0:T(8,128)S(1)}, f32[136,128]{1,0:T(8,128)S(1)}, u32[]{:S(2)}, u32[]{:S(2)}) collective-permute-start(f32[136,128]{1,0:T(8,128)S(1)} %get-tuple-element.71), channel_id=1, source_target_pairs={{0,8},{4,12},{8,0},{12,4},{1,9},{5,13},{9,1},{13,5},{2,10},{6,14},... | collective-permute-start | bytes 208904 | tf_op jit(solution)/shard_map/ppermute | solution.py:409
  38.7 2.5 %collective-permute-done.6.refs_2_ = f32[136,128]{1,0:T(8,128)S(1)} collective-permute-done((f32[136,128]{1,0:T(8,128)S(1)}, f32[136,128]{1,0:T(8,128)S(1)}, u32[]{:S(2)}, u32[]{:S(2)}) %collective-permute-start.6) | collective-permute-done | bytes 69664 | tf_op jit(solution)/shard_map/ppermute | solution.py:409
  42.3 3.4 %collective-permute-start.11 = (f32[136,128]{1,0:T(8,128)S(1)}, f32[136,128]{1,0:T(8,128)S(1)}, u32[]{:S(2)}, u32[]{:S(2)}) collective-permute-start(f32[136,128]{1,0:T(8,128)S(1)} %get-tuple-element.77), channel_id=1, source_target_pairs={{0,12},{4,0},{8,4},{12,8},{1,13},{5,1},{9,5},{13,9},{2,14},{6,2},{... | collective-permute-start | bytes 208904 | tf_op jit(solution)/shard_map/ppermute | solution.py:409
  45.7 2.6 %collective-permute-done.10.refs_6_ = f32[136,128]{1,0:T(8,128)S(1)} collective-permute-done((f32[136,128]{1,0:T(8,128)S(1)}, f32[136,128]{1,0:T(8,128)S(1)}, u32[]{:S(2)}, u32[]{:S(2)}) %collective-permute-start.10) | collective-permute-done | bytes 69664 | tf_op jit(solution)/shard_map/ppermute | solution.py:409
  48.3 3.5 %collective-permute-done.9.refs_5_ = f32[136,128]{1,0:T(8,128)S(1)} collective-permute-done((f32[136,128]{1,0:T(8,128)S(1)}, f32[136,128]{1,0:T(8,128)S(1)}, u32[]{:S(2)}, u32[]{:S(2)}) %collective-permute-start.9) | collective-permute-done | bytes 69664 | tf_op jit(solution)/shard_map/ppermute | solution.py:409
  52.9 2.9 %collective-permute-start.14 = (f32[2,128,128]{2,1,0:T(8,128)S(1)}, f32[2,128,128]{2,1,0:T(8,128)S(1)}, u32[]{:S(2)}, u32[]{:S(2)}) collective-permute-start(f32[2,128,128]{2,1,0:T(8,128)S(1)} %get-tuple-element.78.refs_0_), channel_id=1, source_target_pairs={{0,12},{4,0},{8,4},{12,8},{1,13},{5,1},{9,5},{13,9},{2,14},{6,2},{... | collective-permute-start | bytes 393224 | tf_op jit(solution)/shard_map/ppermute | solution.py:409
  57.3 3.3 %collective-permute-done.16.refs_5_ = f32[8,128]{1,0:T(8,128)S(1)} collective-permute-done((f32[8,128]{1,0:T(8,128)S(1)}, f32[8,128]{1,0:T(8,128)S(1)}, u32[]{:S(2)}, u32[]{:S(2)}) %collective-permute-start.16) | collective-permute-done | bytes 4128 | tf_op jit(solution)/shard_map/ppermute | solution.py:409
  60.6 2.7 %collective-permute-done.13.refs_2_ = f32[2,128,128]{2,1,0:T(8,128)S(1)} collective-permute-done((f32[2,128,128]{2,1,0:T(8,128)S(1)}, f32[2,128,128]{2,1,0:T(8,128)S(1)}, u32[]{:S(2)}, u32[]{:S(2)}) %collective-permute-start.13) | collective-permute-done | bytes 131104 | tf_op jit(solution)/shard_map/ppermute | solution.py:409
  65.3 3.3 %collective-permute-done.18.refs_1_ = f32[8,128]{1,0:T(8,128)S(1)} collective-permute-done((f32[8,128]{1,0:T(8,128)S(1)}, f32[8,128]{1,0:T(8,128)S(1)}, u32[]{:S(2)}, u32[]{:S(2)}) %collective-permute-start.18) | collective-permute-done | bytes 4128 | tf_op jit(solution)/shard_map/ppermute | solution.py:409
  68.6 3.0 %remote_images.3 = (f32[4,256,128]{2,1,0:T(8,128)S(1)}, bf16[5,256,128]{2,1,0:T(8,128)(2,1)S(1)}, f32[4,256,128]{2,1,0:T(8,128)S(1)}, f32[4,256,128]{2,1,0:T(8,128)S(1)}) custom-call(s32[542]{0:T(1024)S(1)} %get-tuple-element.55.lists, f32[4,256,128]{2,1,0:T(8,128)S(1)} %get-tuple-element.58.held, f32[4,256,128]{2,1,0:T(8,128)S(1)} %bitcast.45, ...), custom_call_target="tpu_custom_call" | custom-call | flops 2147483648 | bytes 4194304 | tf_op jit(solution)/shard_map/remote_images/pallas_call | solution.py:238
  71.7 2.7 %own_first.3 = (f32[4,256,128]{2,1,0:T(8,128)S(1)}, f32[4,256,128]{2,1,0:T(8,128)S(1)}) custom-call(s32[542]{0:T(1024)S(1)} %get-tuple-element.55.lists, bf16[5,256,128]{2,1,0:T(8,128)(2,1)S(1)} %get-tuple-element.83.vector_bf, bf16[96,256,256]{2,1,0:T(8,128)(2,1)S(1)} %get-tuple-element.56.refs_2_.left, ...), custom_call_target="tpu_custom_call" | custom-call | flops 2147483648 | bytes 4194304 | tf_op jit(solution)/shard_map/own_first/pallas_call | solution.py:238
  75.5 5.4 %own_rest.3 = (f32[4,256,128]{2,1,0:T(8,128)S(1)}, f32[4,256,128]{2,1,0:T(8,128)S(1)}) custom-call(s32[542]{0:T(1024)S(1)} %get-tuple-element.55.lists, bf16[5,256,128]{2,1,0:T(8,128)(2,1)S(1)} %get-tuple-element.83.vector_bf, f32[4,256,128]{2,1,0:T(8,128)S(1)} %get-tuple-element.84.keep_in, f32[4,256,128]{2,1,0:T(8,128)S(1)} %get-tuple-element.85.send_in, ...), custom_call_target="tpu_custom_call" | custom-call | flops 4294967296 | bytes 8388608 | tf_op jit(solution)/shard_map/own_rest/pallas_call | solution.py:238
  80.9 2.4 %collective-permute-done.20.refs_2_ = f32[2,256,128]{2,1,0:T(8,128)S(1)} collective-permute-done((f32[2,256,128]{2,1,0:T(8,128)S(1)}, f32[2,256,128]{2,1,0:T(8,128)S(1)}, u32[]{:S(2)}, u32[]{:S(2)}) %collective-permute-start.20) | collective-permute-done | bytes 262176 | tf_op jit(solution)/shard_map/ppermute | solution.py:409
  85.4 3.1 %collective-permute-start.22 = (f32[136,128]{1,0:T(8,128)S(1)}, f32[136,128]{1,0:T(8,128)S(1)}, u32[]{:S(2)}, u32[]{:S(2)}) collective-permute-start(f32[136,128]{1,0:T(8,128)S(1)} %get-tuple-element.94), channel_id=1, source_target_pairs={{0,4},{4,8},{8,12},{12,0},{1,5},{5,9},{9,13},{13,1},{2,6},{6,10},{... | collective-permute-start | bytes 208904 | tf_op jit(solution)/shard_map/ppermute | solution.py:409
  89.5 1.4 %collective-permute-start.24 = (f32[136,128]{1,0:T(8,128)S(1)}, f32[136,128]{1,0:T(8,128)S(1)}, u32[]{:S(2)}, u32[]{:S(2)}) collective-permute-start(f32[136,128]{1,0:T(8,128)S(1)} %get-tuple-element.96), channel_id=1, source_target_pairs={{0,12},{4,0},{8,4},{12,8},{1,13},{5,1},{9,5},{13,9},{2,14},{6,2},{... | collective-permute-start | bytes 208904 | tf_op jit(solution)/shard_map/ppermute | solution.py:409
  92.1 2.6 %collective-permute-done.23.refs_2_ = f32[136,128]{1,0:T(8,128)S(1)} collective-permute-done((f32[136,128]{1,0:T(8,128)S(1)}, f32[136,128]{1,0:T(8,128)S(1)}, u32[]{:S(2)}, u32[]{:S(2)}) %collective-permute-start.23) | collective-permute-done | bytes 69664 | tf_op jit(solution)/shard_map/ppermute | solution.py:409
  95.3 1.5 %collective-permute-start.26 = (f32[136,128]{1,0:T(8,128)S(1)}, f32[136,128]{1,0:T(8,128)S(1)}, u32[]{:S(2)}, u32[]{:S(2)}) collective-permute-start(f32[136,128]{1,0:T(8,128)S(1)} %get-tuple-element.99), channel_id=1, source_target_pairs={{0,4},{4,8},{8,12},{12,0},{1,5},{5,9},{9,13},{13,1},{2,6},{6,10},{... | collective-permute-start | bytes 208904 | tf_op jit(solution)/shard_map/ppermute | solution.py:409
  96.8 1.7 %collective-permute-start.27 = (f32[136,128]{1,0:T(8,128)S(1)}, f32[136,128]{1,0:T(8,128)S(1)}, u32[]{:S(2)}, u32[]{:S(2)}) collective-permute-start(f32[136,128]{1,0:T(8,128)S(1)} %get-tuple-element.100), channel_id=1, source_target_pairs={{0,8},{4,12},{8,0},{12,4},{1,9},{5,13},{9,1},{13,5},{2,10},{6,14},... | collective-permute-start | bytes 208904 | tf_op jit(solution)/shard_map/ppermute | solution.py:409
  99.2 2.4 %collective-permute-done.26.refs_5_ = f32[136,128]{1,0:T(8,128)S(1)} collective-permute-done((f32[136,128]{1,0:T(8,128)S(1)}, f32[136,128]{1,0:T(8,128)S(1)}, u32[]{:S(2)}, u32[]{:S(2)}) %collective-permute-start.26) | collective-permute-done | bytes 69664 | tf_op jit(solution)/shard_map/ppermute | solution.py:409
  101.7 2.0 %collective-permute-done.27.refs_6_ = f32[136,128]{1,0:T(8,128)S(1)} collective-permute-done((f32[136,128]{1,0:T(8,128)S(1)}, f32[136,128]{1,0:T(8,128)S(1)}, u32[]{:S(2)}, u32[]{:S(2)}) %collective-permute-start.27) | collective-permute-done | bytes 69664 | tf_op jit(solution)/shard_map/ppermute | solution.py:409
  104.0 1.9 %collective-permute-start.29 = (f32[2,128,128]{2,1,0:T(8,128)S(1)}, f32[2,128,128]{2,1,0:T(8,128)S(1)}, u32[]{:S(2)}, u32[]{:S(2)}) collective-permute-start(f32[2,128,128]{2,1,0:T(8,128)S(1)} %get-tuple-element.102.refs_0_), channel_id=1, source_target_pairs={{0,4},{4,8},{8,12},{12,0},{1,5},{5,9},{9,13},{13,1},{2,6},{6,10},{... | collective-permute-start | bytes 393224 | tf_op jit(solution)/shard_map/ppermute | solution.py:409
  105.9 1.3 %collective-permute-start.30 = (f32[2,128,128]{2,1,0:T(8,128)S(1)}, f32[2,128,128]{2,1,0:T(8,128)S(1)}, u32[]{:S(2)}, u32[]{:S(2)}) collective-permute-start(f32[2,128,128]{2,1,0:T(8,128)S(1)} %get-tuple-element.102.refs_0_), channel_id=1, source_target_pairs={{0,8},{4,12},{8,0},{12,4},{1,9},{5,13},{9,1},{13,5},{2,10},{6,14},... | collective-permute-start | bytes 393224 | tf_op jit(solution)/shard_map/ppermute | solution.py:409
  110.4 2.7 %collective-permute-done.33.refs_5_ = f32[8,128]{1,0:T(8,128)S(1)} collective-permute-done((f32[8,128]{1,0:T(8,128)S(1)}, f32[8,128]{1,0:T(8,128)S(1)}, u32[]{:S(2)}, u32[]{:S(2)}) %collective-permute-start.33) | collective-permute-done | bytes 4128 | tf_op jit(solution)/shard_map/ppermute | solution.py:409
  113.1 3.7 %collective-permute-done.30.refs_2_ = f32[2,128,128]{2,1,0:T(8,128)S(1)} collective-permute-done((f32[2,128,128]{2,1,0:T(8,128)S(1)}, f32[2,128,128]{2,1,0:T(8,128)S(1)}, u32[]{:S(2)}, u32[]{:S(2)}) %collective-permute-start.30) | collective-permute-done | bytes 131104 | tf_op jit(solution)/shard_map/ppermute | solution.py:409
  119.4 2.7 %collective-permute-done.35.refs_1_ = f32[8,128]{1,0:T(8,128)S(1)} collective-permute-done((f32[8,128]{1,0:T(8,128)S(1)}, f32[8,128]{1,0:T(8,128)S(1)}, u32[]{:S(2)}, u32[]{:S(2)}) %collective-permute-start.35) | collective-permute-done | bytes 4128 | tf_op jit(solution)/shard_map/ppermute | solution.py:409
  (73 shorter events, 28.4 us)
Async XLA Ops:
  1.9 1.3 %collective-permute-start = (f32[8,128]{1,0:T(8,128)S(1)}, f32[8,128]{1,0:T(8,128)S(1)}, u32[]{:S(2)}, u32[]{:S(2)}) collective-permute-start(f32[8,128]{1,0:T(8,128)S(1)} %square_sum.1.refs_0_), channel_id=1, source_target_pairs={{0,1},{1,0},{2,3},{3,2},{4,5},{5,4},{6,7},{7,6},{8,9},{9,8},{10,11... | collective-permute-start | bytes 12296 | tf_op jit(solution)/shard_map/ppermute | solution.py:409
  3.3 11.4 %collective-permute-start.1 = (f32[8,128]{1,0:T(8,128)S(1)}, f32[8,128]{1,0:T(8,128)S(1)}, u32[]{:S(2)}, u32[]{:S(2)}) collective-permute-start(f32[8,128]{1,0:T(8,128)S(1)} %add.5.refs_0_), channel_id=1, source_target_pairs={{0,2},{2,0},{1,3},{3,1},{4,6},{6,4},{5,7},{7,5},{8,10},{10,8},{9,1... | collective-permute-start | bytes 12296 | tf_op jit(solution)/shard_map/ppermute | solution.py:409
  17.6 2.8 %collective-permute-start.2 = (f32[4,256,128]{2,1,0:T(8,128)S(1)}, f32[4,256,128]{2,1,0:T(8,128)S(1)}, u32[]{:S(2)}, u32[]{:S(2)}) collective-permute-start(f32[4,256,128]{2,1,0:T(8,128)S(1)} %get-tuple-element.63), channel_id=1, source_target_pairs={{0,1},{1,0},{2,3},{3,2},{4,5},{5,4},{6,7},{7,6},{8,9},{9,8},{10,11... | collective-permute-start | bytes 1572872 | tf_op jit(solution)/shard_map/ppermute | solution.py:409
  20.5 8.8 %collective-permute-start.3 = (f32[2,256,128]{2,1,0:T(8,128)S(1)}, f32[2,256,128]{2,1,0:T(8,128)S(1)}, u32[]{:S(2)}, u32[]{:S(2)}) collective-permute-start(f32[2,256,128]{2,1,0:T(8,128)S(1)} %get-tuple-element.64.after), channel_id=1, source_target_pairs={{0,2},{2,0},{1,3},{3,1},{4,6},{6,4},{5,7},{7,5},{8,10},{10,8},{9,1... | collective-permute-start | bytes 786440 | tf_op jit(solution)/shard_map/ppermute | solution.py:409
  29.3 2.0 %collective-permute-start.4 = (f32[4,256,128]{2,1,0:T(8,128)S(1)}, f32[4,256,128]{2,1,0:T(8,128)S(1)}, u32[]{:S(2)}, u32[]{:S(2)}) collective-permute-start(f32[4,256,128]{2,1,0:T(8,128)S(1)} %get-tuple-element.68), channel_id=1, source_target_pairs={{0,1},{1,0},{2,3},{3,2},{4,5},{5,4},{6,7},{7,6},{8,9},{9,8},{10,11... | collective-permute-start | bytes 1572872 | tf_op jit(solution)/shard_map/ppermute | solution.py:409
  29.4 8.7 %collective-permute-start.8 = (f32[2,256,128]{2,1,0:T(8,128)S(1)}, f32[2,256,128]{2,1,0:T(8,128)S(1)}, u32[]{:S(2)}, u32[]{:S(2)}) collective-permute-start(f32[2,256,128]{2,1,0:T(8,128)S(1)} %get-tuple-element.73), channel_id=1, source_target_pairs={{0,2},{2,0},{1,3},{3,1},{4,6},{6,4},{5,7},{7,5},{8,10},{10,8},{9,1... | collective-permute-start | bytes 786440 | tf_op jit(solution)/shard_map/ppermute | solution.py:409
  31.4 7.3 %collective-permute-start.5 = (f32[136,128]{1,0:T(8,128)S(1)}, f32[136,128]{1,0:T(8,128)S(1)}, u32[]{:S(2)}, u32[]{:S(2)}) collective-permute-start(f32[136,128]{1,0:T(8,128)S(1)} %get-tuple-element.70), channel_id=1, source_target_pairs={{0,4},{4,8},{8,12},{12,0},{1,5},{5,9},{9,13},{13,1},{2,6},{6,10},{... | collective-permute-start | bytes 208904 | tf_op jit(solution)/shard_map/ppermute | solution.py:409
  33.6 7.6 %collective-permute-start.6 = (f32[136,128]{1,0:T(8,128)S(1)}, f32[136,128]{1,0:T(8,128)S(1)}, u32[]{:S(2)}, u32[]{:S(2)}) collective-permute-start(f32[136,128]{1,0:T(8,128)S(1)} %get-tuple-element.71), channel_id=1, source_target_pairs={{0,8},{4,12},{8,0},{12,4},{1,9},{5,13},{9,1},{13,5},{2,10},{6,14},... | collective-permute-start | bytes 208904 | tf_op jit(solution)/shard_map/ppermute | solution.py:409
  36.2 5.5 %collective-permute-start.7 = (f32[136,128]{1,0:T(8,128)S(1)}, f32[136,128]{1,0:T(8,128)S(1)}, u32[]{:S(2)}, u32[]{:S(2)}) collective-permute-start(f32[136,128]{1,0:T(8,128)S(1)} %get-tuple-element.72), channel_id=1, source_target_pairs={{0,12},{4,0},{8,4},{12,8},{1,13},{5,1},{9,5},{13,9},{2,14},{6,2},{... | collective-permute-start | bytes 208904 | tf_op jit(solution)/shard_map/ppermute | solution.py:409
  41.7 6.6 %collective-permute-start.10 = (f32[136,128]{1,0:T(8,128)S(1)}, f32[136,128]{1,0:T(8,128)S(1)}, u32[]{:S(2)}, u32[]{:S(2)}) collective-permute-start(f32[136,128]{1,0:T(8,128)S(1)} %get-tuple-element.76), channel_id=1, source_target_pairs={{0,8},{4,12},{8,0},{12,4},{1,9},{5,13},{9,1},{13,5},{2,10},{6,14},... | collective-permute-start | bytes 208904 | tf_op jit(solution)/shard_map/ppermute | solution.py:409
  42.3 6.0 %collective-permute-start.11 = (f32[136,128]{1,0:T(8,128)S(1)}, f32[136,128]{1,0:T(8,128)S(1)}, u32[]{:S(2)}, u32[]{:S(2)}) collective-permute-start(f32[136,128]{1,0:T(8,128)S(1)} %get-tuple-element.77), channel_id=1, source_target_pairs={{0,12},{4,0},{8,4},{12,8},{1,13},{5,1},{9,5},{13,9},{2,14},{6,2},{... | collective-permute-start | bytes 208904 | tf_op jit(solution)/shard_map/ppermute | solution.py:409
  45.7 6.1 %collective-permute-start.9 = (f32[136,128]{1,0:T(8,128)S(1)}, f32[136,128]{1,0:T(8,128)S(1)}, u32[]{:S(2)}, u32[]{:S(2)}) collective-permute-start(f32[136,128]{1,0:T(8,128)S(1)} %get-tuple-element.75), channel_id=1, source_target_pairs={{0,4},{4,8},{8,12},{12,0},{1,5},{5,9},{9,13},{13,1},{2,6},{6,10},{... | collective-permute-start | bytes 208904 | tf_op jit(solution)/shard_map/ppermute | solution.py:409
  51.9 8.7 %collective-permute-start.12 = (f32[2,128,128]{2,1,0:T(8,128)S(1)}, f32[2,128,128]{2,1,0:T(8,128)S(1)}, u32[]{:S(2)}, u32[]{:S(2)}) collective-permute-start(f32[2,128,128]{2,1,0:T(8,128)S(1)} %get-tuple-element.78.refs_0_), channel_id=1, source_target_pairs={{0,4},{4,8},{8,12},{12,0},{1,5},{5,9},{9,13},{13,1},{2,6},{6,10},{... | collective-permute-start | bytes 393224 | tf_op jit(solution)/shard_map/ppermute | solution.py:409
  52.0 11.3 %collective-permute-start.13 = (f32[2,128,128]{2,1,0:T(8,128)S(1)}, f32[2,128,128]{2,1,0:T(8,128)S(1)}, u32[]{:S(2)}, u32[]{:S(2)}) collective-permute-start(f32[2,128,128]{2,1,0:T(8,128)S(1)} %get-tuple-element.78.refs_0_), channel_id=1, source_target_pairs={{0,8},{4,12},{8,0},{12,4},{1,9},{5,13},{9,1},{13,5},{2,10},{6,14},... | collective-permute-start | bytes 393224 | tf_op jit(solution)/shard_map/ppermute | solution.py:409
  52.9 10.4 %collective-permute-start.14 = (f32[2,128,128]{2,1,0:T(8,128)S(1)}, f32[2,128,128]{2,1,0:T(8,128)S(1)}, u32[]{:S(2)}, u32[]{:S(2)}) collective-permute-start(f32[2,128,128]{2,1,0:T(8,128)S(1)} %get-tuple-element.78.refs_0_), channel_id=1, source_target_pairs={{0,12},{4,0},{8,4},{12,8},{1,13},{5,1},{9,5},{13,9},{2,14},{6,2},{... | collective-permute-start | bytes 393224 | tf_op jit(solution)/shard_map/ppermute | solution.py:409
  57.0 3.6 %collective-permute-start.16 = (f32[8,128]{1,0:T(8,128)S(1)}, f32[8,128]{1,0:T(8,128)S(1)}, u32[]{:S(2)}, u32[]{:S(2)}) collective-permute-start(f32[8,128]{1,0:T(8,128)S(1)} %add.6.refs_4_), channel_id=1, source_target_pairs={{0,2},{2,0},{1,3},{3,1},{4,6},{6,4},{5,7},{7,5},{8,10},{10,8},{9,1... | collective-permute-start | bytes 12296 | tf_op jit(solution)/shard_map/ppermute | solution.py:409
  65.0 3.6 %collective-permute-start.18 = (f32[8,128]{1,0:T(8,128)S(1)}, f32[8,128]{1,0:T(8,128)S(1)}, u32[]{:S(2)}, u32[]{:S(2)}) collective-permute-start(f32[8,128]{1,0:T(8,128)S(1)} %add.7.refs_0_), channel_id=1, source_target_pairs={{0,2},{2,0},{1,3},{3,1},{4,6},{6,4},{5,7},{7,5},{8,10},{10,8},{9,1... | collective-permute-start | bytes 12296 | tf_op jit(solution)/shard_map/ppermute | solution.py:409
  71.6 2.8 %collective-permute-start.19 = (f32[4,256,128]{2,1,0:T(8,128)S(1)}, f32[4,256,128]{2,1,0:T(8,128)S(1)}, u32[]{:S(2)}, u32[]{:S(2)}) collective-permute-start(f32[4,256,128]{2,1,0:T(8,128)S(1)} %get-tuple-element.87), channel_id=1, source_target_pairs={{0,1},{1,0},{2,3},{3,2},{4,5},{5,4},{6,7},{7,6},{8,9},{9,8},{10,11... | collective-permute-start | bytes 1572872 | tf_op jit(solution)/shard_map/ppermute | solution.py:409
  74.5 8.8 %collective-permute-start.20 = (f32[2,256,128]{2,1,0:T(8,128)S(1)}, f32[2,256,128]{2,1,0:T(8,128)S(1)}, u32[]{:S(2)}, u32[]{:S(2)}) collective-permute-start(f32[2,256,128]{2,1,0:T(8,128)S(1)} %get-tuple-element.88.after), channel_id=1, source_target_pairs={{0,2},{2,0},{1,3},{3,1},{4,6},{6,4},{5,7},{7,5},{8,10},{10,8},{9,1... | collective-permute-start | bytes 786440 | tf_op jit(solution)/shard_map/ppermute | solution.py:409
  83.3 2.0 %collective-permute-start.21 = (f32[4,256,128]{2,1,0:T(8,128)S(1)}, f32[4,256,128]{2,1,0:T(8,128)S(1)}, u32[]{:S(2)}, u32[]{:S(2)}) collective-permute-start(f32[4,256,128]{2,1,0:T(8,128)S(1)} %get-tuple-element.92), channel_id=1, source_target_pairs={{0,1},{1,0},{2,3},{3,2},{4,5},{5,4},{6,7},{7,6},{8,9},{9,8},{10,11... | collective-permute-start | bytes 1572872 | tf_op jit(solution)/shard_map/ppermute | solution.py:409
  83.4 8.7 %collective-permute-start.25 = (f32[2,256,128]{2,1,0:T(8,128)S(1)}, f32[2,256,128]{2,1,0:T(8,128)S(1)}, u32[]{:S(2)}, u32[]{:S(2)}) collective-permute-start(f32[2,256,128]{2,1,0:T(8,128)S(1)} %get-tuple-element.97), channel_id=1, source_target_pairs={{0,2},{2,0},{1,3},{3,1},{4,6},{6,4},{5,7},{7,5},{8,10},{10,8},{9,1... | collective-permute-start | bytes 786440 | tf_op jit(solution)/shard_map/ppermute | solution.py:409
  85.4 6.7 %collective-permute-start.22 = (f32[136,128]{1,0:T(8,128)S(1)}, f32[136,128]{1,0:T(8,128)S(1)}, u32[]{:S(2)}, u32[]{:S(2)}) collective-permute-start(f32[136,128]{1,0:T(8,128)S(1)} %get-tuple-element.94), channel_id=1, source_target_pairs={{0,4},{4,8},{8,12},{12,0},{1,5},{5,9},{9,13},{13,1},{2,6},{6,10},{... | collective-permute-start | bytes 208904 | tf_op jit(solution)/shard_map/ppermute | solution.py:409
  88.5 6.2 %collective-permute-start.23 = (f32[136,128]{1,0:T(8,128)S(1)}, f32[136,128]{1,0:T(8,128)S(1)}, u32[]{:S(2)}, u32[]{:S(2)}) collective-permute-start(f32[136,128]{1,0:T(8,128)S(1)} %get-tuple-element.95), channel_id=1, source_target_pairs={{0,8},{4,12},{8,0},{12,4},{1,9},{5,13},{9,1},{13,5},{2,10},{6,14},... | collective-permute-start | bytes 208904 | tf_op jit(solution)/shard_map/ppermute | solution.py:409
  89.5 5.7 %collective-permute-start.24 = (f32[136,128]{1,0:T(8,128)S(1)}, f32[136,128]{1,0:T(8,128)S(1)}, u32[]{:S(2)}, u32[]{:S(2)}) collective-permute-start(f32[136,128]{1,0:T(8,128)S(1)} %get-tuple-element.96), channel_id=1, source_target_pairs={{0,12},{4,0},{8,4},{12,8},{1,13},{5,1},{9,5},{13,9},{2,14},{6,2},{... | collective-permute-start | bytes 208904 | tf_op jit(solution)/shard_map/ppermute | solution.py:409
  95.3 6.4 %collective-permute-start.26 = (f32[136,128]{1,0:T(8,128)S(1)}, f32[136,128]{1,0:T(8,128)S(1)}, u32[]{:S(2)}, u32[]{:S(2)}) collective-permute-start(f32[136,128]{1,0:T(8,128)S(1)} %get-tuple-element.99), channel_id=1, source_target_pairs={{0,4},{4,8},{8,12},{12,0},{1,5},{5,9},{9,13},{13,1},{2,6},{6,10},{... | collective-permute-start | bytes 208904 | tf_op jit(solution)/shard_map/ppermute | solution.py:409
  96.8 6.9 %collective-permute-start.27 = (f32[136,128]{1,0:T(8,128)S(1)}, f32[136,128]{1,0:T(8,128)S(1)}, u32[]{:S(2)}, u32[]{:S(2)}) collective-permute-start(f32[136,128]{1,0:T(8,128)S(1)} %get-tuple-element.100), channel_id=1, source_target_pairs={{0,8},{4,12},{8,0},{12,4},{1,9},{5,13},{9,1},{13,5},{2,10},{6,14},... | collective-permute-start | bytes 208904 | tf_op jit(solution)/shard_map/ppermute | solution.py:409
  98.5 5.3 %collective-permute-start.28 = (f32[136,128]{1,0:T(8,128)S(1)}, f32[136,128]{1,0:T(8,128)S(1)}, u32[]{:S(2)}, u32[]{:S(2)}) collective-permute-start(f32[136,128]{1,0:T(8,128)S(1)} %get-tuple-element.101), channel_id=1, source_target_pairs={{0,12},{4,0},{8,4},{12,8},{1,13},{5,1},{9,5},{13,9},{2,14},{6,2},{... | collective-permute-start | bytes 208904 | tf_op jit(solution)/shard_map/ppermute | solution.py:409
  104.0 9.1 %collective-permute-start.29 = (f32[2,128,128]{2,1,0:T(8,128)S(1)}, f32[2,128,128]{2,1,0:T(8,128)S(1)}, u32[]{:S(2)}, u32[]{:S(2)}) collective-permute-start(f32[2,128,128]{2,1,0:T(8,128)S(1)} %get-tuple-element.102.refs_0_), channel_id=1, source_target_pairs={{0,4},{4,8},{8,12},{12,0},{1,5},{5,9},{9,13},{13,1},{2,6},{6,10},{... | collective-permute-start | bytes 393224 | tf_op jit(solution)/shard_map/ppermute | solution.py:409
  105.9 10.9 %collective-permute-start.30 = (f32[2,128,128]{2,1,0:T(8,128)S(1)}, f32[2,128,128]{2,1,0:T(8,128)S(1)}, u32[]{:S(2)}, u32[]{:S(2)}) collective-permute-start(f32[2,128,128]{2,1,0:T(8,128)S(1)} %get-tuple-element.102.refs_0_), channel_id=1, source_target_pairs={{0,8},{4,12},{8,0},{12,4},{1,9},{5,13},{9,1},{13,5},{2,10},{6,14},... | collective-permute-start | bytes 393224 | tf_op jit(solution)/shard_map/ppermute | solution.py:409
  107.2 9.6 %collective-permute-start.31 = (f32[2,128,128]{2,1,0:T(8,128)S(1)}, f32[2,128,128]{2,1,0:T(8,128)S(1)}, u32[]{:S(2)}, u32[]{:S(2)}) collective-permute-start(f32[2,128,128]{2,1,0:T(8,128)S(1)} %get-tuple-element.102.refs_0_), channel_id=1, source_target_pairs={{0,12},{4,0},{8,4},{12,8},{1,13},{5,1},{9,5},{13,9},{2,14},{6,2},{... | collective-permute-start | bytes 393224 | tf_op jit(solution)/shard_map/ppermute | solution.py:409
  109.5 3.6 %collective-permute-start.33 = (f32[8,128]{1,0:T(8,128)S(1)}, f32[8,128]{1,0:T(8,128)S(1)}, u32[]{:S(2)}, u32[]{:S(2)}) collective-permute-start(f32[8,128]{1,0:T(8,128)S(1)} %add.8.refs_4_), channel_id=1, source_target_pairs={{0,2},{2,0},{1,3},{3,1},{4,6},{6,4},{5,7},{7,5},{8,10},{10,8},{9,1... | collective-permute-start | bytes 12296 | tf_op jit(solution)/shard_map/ppermute | solution.py:409
  118.5 3.6 %collective-permute-start.35 = (f32[8,128]{1,0:T(8,128)S(1)}, f32[8,128]{1,0:T(8,128)S(1)}, u32[]{:S(2)}, u32[]{:S(2)}) collective-permute-start(f32[8,128]{1,0:T(8,128)S(1)} %add.9.refs_0_), channel_id=1, source_target_pairs={{0,2},{2,0},{1,3},{3,1},{4,6},{6,4},{5,7},{7,5},{8,10},{10,8},{9,1... | collective-permute-start | bytes 12296 | tf_op jit(solution)/shard_map/ppermute | solution.py:409
  (7 other events, 29.8 us)
